TPU v7x, 128 devices: a whole 4x4x4 slice. The times are simulated.
128 devices in a mesh: blk: 32 (over y, x_lo, z), vir: 4 (over x_hi, core).
Axes of the slice: x: 4 (x_hi: 2, x_lo: 2; x = x_hi * 2 + x_lo), y: 4, z: 4, core: 2. Of those that a mesh axis runs over, the one named last changes fastest.
Arguments:
- cholesky: float32 [8, 1536, 1536], P(None, 'blk', 'vir'), may hold values from -0.09375 to 0.09375
- amplitudes: float32 [8, 1536, 1536], P(None, 'blk', 'vir'), may hold values from -6 to 6
Outputs:
- ladder: float32 [8, 1536, 1536], P(None, 'vir', 'blk')
All inputs are finite; a program needn't handle non-finite values.
Results may differ from a plain program's by a relative error of at most 0.0001.
Values sent between devices are 32-bit elements; how exact they have to be, the bound alone decides.
No kernel may reach another device: no remote copies, remote signals or barrier semaphores. Data moves between devices by JAX's collectives and lax.ppermute only.
A program may use at most 128 MiB of HBM per device.

v0:
```python
import jax
import jax.numpy as jnp
from jax import lax
from jax.sharding import PartitionSpec as P


def body(cholesky, amplitudes):
    partial_pairs = jnp.einsum(
        "pbd,icd->pibc",
        cholesky,
        lax.all_gather(amplitudes, "blk", axis=1, tiled=True),
        precision=lax.Precision.HIGHEST,
    )
    halfway = lax.psum_scatter(partial_pairs, "vir", scatter_dimension=3, tiled=True)
    ladder_part = jnp.einsum(
        "pac,pibc->iab",
        lax.all_gather(cholesky, "blk", axis=1, tiled=True),
        halfway,
        precision=lax.Precision.HIGHEST,
    )
    return lax.psum_scatter(ladder_part, "vir", scatter_dimension=1, tiled=True)


def solution(mesh):
    in_specs = (P(None, "blk", "vir"), P(None, "blk", "vir"))
    out_specs = P(None, "vir", "blk")
    return jax.shard_map(body, mesh=mesh, in_specs=in_specs, out_specs=out_specs, check_vma=False)
```

profile of v0, /device:TPU:1, one launch (start us, length us, event | category | flops | bytes accessed | tf_op | source)
XLA Modules:
  0.0 657.0 jit_solution(155433187949293745)
XLA Ops:
  6.5 0.0 all-gather.3.cloned.1.call-start
  6.5 0.7 all-gather.3.cloned.1.call-update
  7.3 0.0 all-gather.5.cloned.1.call-start
  7.3 0.7 all-gather.5.cloned.1.call-update
  8.0 0.0 reduce-scatter.3.cloned.1.call-start
  8.1 216.8 %all-gather.3.cloned.1.call-done = f32[8,1536,384]{2,1,0:T(8,128)} async-done(((f32[8,48,384]{2,1,0:T(8,128)}), f32[8,1536,384]{2,1,0:T(8,128)}) %all-gather.3.cloned.1.call-update) | async-done | bytes 18874384 | tf_op jit(solution)/shard_map/all_gather | solution.py:11
  224.8 35.1 %fusion.4 = f32[8,8,48,1536]{3,2,0,1:T(8,128)} fusion(f32[8,1536,384]{2,1,0:T(8,128)} %all-gather.3.cloned.1.call-done, f32[8,48,384]{2,1,0:T(8,128)} %param.2), kind=kOutput, calls=%fused_computation.4 | convolution fusion | flops 21743271936 | bytes 38338560 | tf_op jit(solution)/shard_map/pbd,icd->pibc/dot_general | solution.py:8
  259.9 0.0 reduce-scatter.3.cloned.1.call-update
  259.9 0.2 reduce-scatter.5.cloned.1.call-start
  260.2 176.2 %all-gather.5.cloned.1.call-done = f32[8,1536,384]{2,1,0:T(8,128)} async-done(((f32[8,48,384]{2,1,0:T(8,128)}), f32[8,1536,384]{2,1,0:T(8,128)}) %all-gather.5.cloned.1.call-update) | async-done | bytes 18874384 | tf_op jit(solution)/shard_map/all_gather | solution.py:17
  436.3 146.4 %reduce-scatter.3.cloned.1.call-done = f32[8,8,48,384]{3,2,0,1:T(8,128)} async-done(((f32[8,8,48,1536]{3,2,0,1:T(8,128)}), f32[8,8,48,384]{3,2,0,1:T(8,128)}) %reduce-scatter.3.cloned.1.call-update) | async-done | bytes 4718608 | tf_op jit(solution)/shard_map/reduce_scatter | solution.py:14
  582.7 28.2 %fusion.7 = f32[8,1536,48]{1,2,0:T(8,128)} fusion(f32[8,8,48,384]{3,2,0,1:T(8,128)} %reduce-scatter.3.cloned.1.call-done, f32[8,1536,384]{2,1,0:T(8,128)} %all-gather.5.cloned.1.call-done), kind=kOutput, calls=%fused_computation.5 | convolution fusion | flops 21743271936 | bytes 25952256 | tf_op jit(solution)/shard_map/pac,pibc->iab/dot_general | solution.py:15
  610.9 0.0 reduce-scatter.5.cloned.1.call-update
  610.9 39.6 %reduce-scatter.5.cloned.1.call-done = f32[8,384,48]{1,2,0:T(8,128)} async-done(((f32[8,1536,48]{1,2,0:T(8,128)}), f32[8,384,48]{1,2,0:T(8,128)}) %reduce-scatter.5.cloned.1.call-update) | async-done | bytes 589840 | tf_op jit(solution)/shard_map/reduce_scatter | solution.py:21
Async XLA Ops:
  6.5 218.3 %all-gather.3.cloned.1.call-start = ((), (), s32[]{:S(2)}) async-start(), calls=%async_computation.2 | async-start | bytes 19464192 | tf_op jit(solution)/shard_map/all_gather | solution.py:11
  7.3 429.1 %all-gather.5.cloned.1.call-start = ((), (), s32[]{:S(2)}) async-start(), calls=%async_computation.4 | async-start | bytes 19464192 | tf_op jit(solution)/shard_map/all_gather | solution.py:17
  8.0 574.7 %reduce-scatter.3.cloned.1.call-start = ((), (), s32[]{:S(2)}) async-start(), calls=%async_computation.3 | async-start | bytes 23592960 | tf_op jit(solution)/shard_map/reduce_scatter | solution.py:14
  259.9 390.5 %reduce-scatter.5.cloned.1.call-start = ((), (), s32[]{:S(2)}) async-start(), calls=%async_computation.5 | async-start | bytes 2949120 | tf_op jit(solution)/shard_map/reduce_scatter | solution.py:21
Sparse Core Ops, SparseCore 0:
  9.0 215.7 all-gather.2
  226.5 209.8 all-gather.4
  439.0 143.6 reduce-scatter.2
  611.0 39.3 reduce-scatter.4
where the time goes:
time: 657 us
  waiting for transfers between devices  580 us (88%)
  matrix products  63.3 us (10%)
  between operations  13.1 us (2%)
    all_gather x1, waiting for transfers between devices, body(): lax.all_gather(amplitudes, 'blk', axis=1, tiled=True)  217 us
    all_gather x1, waiting for transfers between devices, body(): lax.all_gather(cholesky, 'blk', axis=1, tiled=True)  176 us
    reduce_scatter x1, waiting for transfers between devices, body(): lax.psum_scatter(partial_pairs, 'vir', scatter_dimension=3, tiled=True)  146 us
    reduce_scatter x1, waiting for transfers between devices, body(): return lax.psum_scatter(ladder_part, 'vir', scatter_dimension=1, tiled=True)  39.6 us
    dot_general x1, matrix products, body(): jnp.einsum('pbd,icd->pibc', cholesky, lax.all_gather(amplitudes, 'blk', a...  35.1 us
    dot_general x1, matrix products, body(): jnp.einsum('pac,pibc->iab', lax.all_gather(cholesky, 'blk', axis=1, tiled...  28.2 us
  transfers between devices with their start and end apart: 4, of which 4 were waited for; matrix products, arithmetic and copies ran while one was open for 5% of the time, Pallas kernels for 0%

commit v1 on v0

v1 whole, which is shorter than its diff:
```python
import jax
import jax.numpy as jnp
from jax import lax
from jax.experimental import pallas as pl
from jax.experimental.pallas import tpu as pltpu
from jax.sharding import Mesh
from jax.sharding import PartitionSpec as P

AXES = ("y", "xl", "z", "xh", "c")
SIZES = (4, 2, 4, 2, 2)
F32, BF16 = jnp.float32, jnp.bfloat16


def coords(index):
    out = []
    for size in reversed(SIZES):
        out.append(index % size)
        index //= size
    return tuple(reversed(out))


def index_of(at):
    index = 0
    for size, value in zip(SIZES, at):
        index = index * size + value
    return index


def permute(value, target):
    pairs = [(s, index_of(target(*coords(s)))) for s in range(128)]
    return lax.ppermute(value, AXES, pairs)


def shift_x(at, by):
    y, xl, z, xh, c = at
    x = (2 * xh + xl + by) % 4
    return (y, x % 2, z, x // 2, c)


def shift_z(at, by):
    y, xl, z, xh, c = at
    return (y, xl, (z + by) % 4, xh, c)


def shift_y(at, by):
    y, xl, z, xh, c = at
    return ((y + by) % 4, xl, z, xh, c)


def near(at, by):
    return shift_z(at, by) if at[4] == 0 else shift_x(at, by)


def far(at, by):
    return shift_x(at, by) if at[4] == 0 else shift_z(at, by)


def swapped(at):
    y, xl, z, xh, c = at
    return (y, c, z, xh, xl)


def other_core(*at):
    return at[:4] + (1 - at[4],)


def split(value):
    high = value.astype(BF16)
    return high, (value - high.astype(F32)).astype(BF16)


def dot3(a, b):
    def one(p, q):
        return lax.dot_general(p, q, (((1,), (1,)), ((), ())), preferred_element_type=F32)

    return one(a[0], b[0]) + (one(a[0], b[1]) + one(a[1], b[0]))


def kernel(place, *refs):
    rows, (g, ga, fw, gb, fb) = refs[:8], refs[8:13]
    outs = refs[13:21]
    (l_rows, t_raw, l_cols, t_hi, t_lo, c_hi, c_lo, half, a_hi, a_lo, total, row_sem, t_sem, c_sem, out_sem) = refs[21:]
    y, z, x, c = place[0], place[1], place[2], place[3]

    def spot(u, v):
        on_first = c == 0
        at_z = lax.rem(z + jnp.where(on_first, u, v), 4)
        at_x = lax.rem(x + jnp.where(on_first, v, u), 4)
        return at_z, at_x

    t_copies, c_copies, row_copies = [], [], []
    down = jnp.where(c == 0, lax.rem(y + 3, 4), lax.rem(y + 1, 4))
    up = jnp.where(c == 0, lax.rem(y + 1, 4), lax.rem(y + 3, 4))
    across = lax.rem(y + 2, 4)
    for ref, at_y, core in ((g, y, c), (ga, down, c), (fw, across, c), (gb, up, 1 - c), (fb, across, 1 - c)):
        for k in range(ref.shape[0] // 2):
            core_k = core if k == 0 else 1 - core
            t_copies.append(
                pltpu.make_async_copy(
                    ref.at[2 * k],
                    t_raw.at[:, pl.ds(pl.multiple_of(lax.rem(at_y, 2) * 48, 48), 48), pl.ds(pl.multiple_of((2 * (at_y // 2) + core_k) * 384, 384), 384)],
                    t_sem,
                )
            )
            c_copies.append(
                pltpu.make_async_copy(
                    ref.at[2 * k + 1],
                    l_cols.at[pl.ds(at_y * 8, 8), :, pl.ds(pl.multiple_of(core_k * 384, 384), 384)],
                    c_sem,
                )
            )
    for ref, (v, u0) in zip(rows, ((0, 0), (0, 2), (1, 0), (1, 2), (3, 0), (3, 2), (2, 0), (2, 2))):
        for k in range(2):
            at_z, at_x = spot(u0 + k, v)
            row_copies.append(
                pltpu.make_async_copy(
                    ref.at[k],
                    l_rows.at[:, pl.ds(pl.multiple_of(at_z * 48, 48), 48), pl.ds(pl.multiple_of(at_x * 384, 384), 384)],
                    row_sem,
                )
            )
    for copy in t_copies + row_copies + c_copies:
        copy.start()
    for copy in t_copies:
        copy.wait()

    @pl.loop(0, 8)
    def _(i):
        high, low = split(t_raw[i])
        t_hi[pl.ds(pl.multiple_of(i * 96, 96), 96), :] = high
        t_lo[pl.ds(pl.multiple_of(i * 96, 96), 96), :] = low

    for copy in row_copies:
        copy.wait()

    @pl.loop(0, 8)
    def _(p):
        b = split(l_rows[p])
        for m in range(2):
            chunk = pl.ds(m * 384, 384)
            h = dot3((t_hi[chunk, :], t_lo[chunk, :]), b)
            for j in range(8):
                i, lo = m * 4 + j // 2, j % 2
                half[i, pl.ds(pl.multiple_of((lo * 8 + p) * 48, 48), 48), :] = h[j * 48 : (j + 1) * 48, :]

    @pl.loop(0, 8)
    def _(i):
        high, low = split(half[i].T)
        a_hi[pl.ds(pl.multiple_of(i * 192, 192), 192), :] = high
        a_lo[pl.ds(pl.multiple_of(i * 192, 192), 192), :] = low

    for copy in c_copies:
        copy.wait()

    @pl.loop(0, 8)
    def _(e):
        high, low = split(l_cols[pl.ds(e * 4, 4)].reshape(192, 768))
        c_hi[pl.ds(pl.multiple_of(e * 192, 192), 192), :] = high
        c_lo[pl.ds(pl.multiple_of(e * 192, 192), 192), :] = low

    for n in range(2):
        wide = pl.ds(n * 768, 768)

        @pl.loop(0, 4)
        def _(m):
            chunk = pl.ds(pl.multiple_of(m * 384, 384), 384)
            r = dot3((a_hi[chunk, :], a_lo[chunk, :]), (c_hi[wide, :], c_lo[wide, :]))
            for j in range(2):
                for at_z in range(4):
                    for k in range(2):
                        to_z = lax.rem(at_z - z + 4, 4)
                        to_x = lax.rem(n * 2 + k - x + 4, 4)
                        v = jnp.where(c == 0, to_x, to_z)
                        u = jnp.where(c == 0, to_z, to_x)
                        rows_at = j * 192 + at_z * 48
                        total[v * 4 + u, m * 2 + j] = r[rows_at : rows_at + 48, k * 384 : (k + 1) * 384]

    copies = []
    for k, out in enumerate(outs):
        copies.append(pltpu.make_async_copy(total.at[pl.ds(2 * k, 2)], out, out_sem))
    for copy in copies:
        copy.start()
    for copy in copies:
        copy.wait()


def multiply(place, rows, cols):
    piece = jax.ShapeDtypeStruct((2, 8, 48, 384), F32)
    anywhere = pl.BlockSpec(memory_space=pl.ANY)
    return pl.pallas_call(
        kernel,
        out_shape=[piece] * 8,
        in_specs=[pl.BlockSpec(memory_space=pltpu.SMEM)] + [anywhere] * 13,
        out_specs=[anywhere] * 8,
        scratch_shapes=[
            pltpu.VMEM((8, 192, 1536), F32),
            pltpu.VMEM((8, 96, 1536), F32),
            pltpu.VMEM((32, 48, 768), F32),
            pltpu.VMEM((768, 1536), BF16),
            pltpu.VMEM((768, 1536), BF16),
            pltpu.VMEM((1536, 768), BF16),
            pltpu.VMEM((1536, 768), BF16),
            pltpu.VMEM((8, 768, 192), F32),
            pltpu.VMEM((1536, 768), BF16),
            pltpu.VMEM((1536, 768), BF16),
            pltpu.VMEM((16, 8, 48, 384), F32),
            pltpu.SemaphoreType.DMA,
            pltpu.SemaphoreType.DMA,
            pltpu.SemaphoreType.DMA,
            pltpu.SemaphoreType.DMA,
        ],
        compiler_params=pltpu.CompilerParams(vmem_limit_bytes=56 << 20),
        cost_estimate=pl.CostEstimate(flops=3 * 7247757312, bytes_accessed=28 << 20, transcendentals=0),
    )(place, *rows, *cols)


def body(cholesky, amplitudes):
    y, xl, z, xh, c = (lax.axis_index(axis) for axis in AXES)
    place = jnp.stack([y, z, 2 * xh + xl, c]).astype(jnp.int32)

    near_rows = [permute(cholesky, lambda *at, u=u: near(swapped(at), -u)) for u in range(4)]
    s01, s23 = jnp.stack(near_rows[:2]), jnp.stack(near_rows[2:])

    def from_plus(value):
        return permute(value, lambda *at: far(at, -1))

    def from_minus(value):
        return permute(value, lambda *at: far(at, 1))

    p01, m23 = from_plus(s01), from_minus(s23)
    p23, m01 = from_plus(s23), from_minus(s01)
    rows = (s01, s23, p01, p23, m01, m23, from_plus(p01), from_minus(m23))

    own_t = permute(amplitudes, lambda y, xl, z, xh, c: (2 * xh + y % 2, xl, z, y // 2, c))
    columns = cholesky.reshape(8, 48, 8, 48).transpose(2, 1, 0, 3).reshape(8, 48, 384)
    own_c = lax.all_to_all(columns, ("xl", "z"), 0, 0, tiled=True)
    own = jnp.stack([own_t, own_c])
    g = jnp.concatenate([own, permute(own, other_core)])

    def along_y(value):
        return permute(value, lambda *at: shift_y(at, 1 if at[4] == 0 else -1))

    ga = along_y(g)
    fw = along_y(ga[:2])
    cols = (g, ga, fw, permute(ga, other_core), permute(fw, other_core))

    r0a, r0b, r1a, r1b, r2a, r2b, r3a, r3b = multiply(place, rows, cols)

    def to_plus(value):
        return permute(value, lambda *at: far(at, 1))

    def to_minus(value):
        return permute(value, lambda *at: far(at, -1))

    a0, a1 = to_plus(r2a), to_minus(r2b)
    b1, d0 = to_plus(r1b), to_minus(r3a)
    b0, d1 = to_plus(r1a + a0), to_minus(r3b + a1)
    q = (r0a + b0 + d0, r0b + b1 + d1)
    pieces = [q[u // 2][u % 2] for u in range(4)]
    got = [permute(piece, lambda *at, u=u: swapped(near(at, u))) for u, piece in enumerate(pieces)]
    return ((got[0] + got[1]) + (got[2] + got[3])).transpose(0, 2, 1)


def solution(mesh):
    fine = Mesh(mesh.devices.reshape(SIZES), AXES)
    split_in = P(None, ("y", "xl", "z"), ("xh", "c"))
    return jax.shard_map(
        body, mesh=fine, in_specs=(split_in, split_in), out_specs=P(None, ("xh", "c"), ("y", "xl", "z")), check_vma=False
    )
```

time: 657 us -> 242 us (0.37)
  waiting for transfers between devices: 580 us -> 118 us
  matrix products: 63.3 us -> 0 us
  starting transfers between devices: 0.3 us -> 47 us
  Pallas kernels: 0 us -> 41.5 us
  blocking collectives: 0 us -> 16.2 us
  between operations: 13.1 us -> 0.21 us
  other arithmetic: 0 us -> 7.35 us
  local copies, waits for them, and re-layouts: 0 us -> 7.31 us
    all_gather x2 -> x0, waiting for transfers between devices: 393 us -> none  [the longest x1 217 us: body(): lax.all_gather(amplitudes, 'blk', axis=1, tiled=True)]
    reduce_scatter x2 -> x0, waiting for transfers between devices: 186 us -> none  [the longest x1 146 us: body(): lax.psum_scatter(partial_pairs, 'vir', scatter_dimension=3, tiled=True)]
    ppermute x0 -> x26, waiting for transfers between devices: none -> 118 us  [permute(): return lax.ppermute(value, AXES, pairs)]
    dot_general x2 -> x0, matrix products: 63.3 us -> none  [the longest x1 35.1 us: body(): jnp.einsum('pbd,icd->pibc', cholesky, lax.all_gather(amplitudes, 'blk', a...]
    ppermute x0 -> x26, starting transfers between devices: none -> 47 us  [permute(): return lax.ppermute(value, AXES, pairs)]
    pallas_call x0 -> x1, Pallas kernels: none -> 41.5 us  [multiply(): pl.pallas_call(kernel, out_shape=[piece] * 8, in_specs=[pl.BlockSpec(memo...]
    all_to_all x0 -> x1, blocking collectives: none -> 16.2 us  [body(): own_c = lax.all_to_all(columns, ('xl', 'z'), 0, 0, tiled=True)]
  transfers between devices with their start and end apart: 4 -> 26, of which waited for: 4 -> 15; matrix products, arithmetic and copies ran while one was open for 5% -> 4% of each run, Pallas kernels for 0% -> 0%
where the time goes in v1:
time: 242 us; the launch traced here: 237 us
  waiting for transfers between devices  118 us (49%)
  starting transfers between devices  47 us (19%)
  Pallas kernels  41.5 us (17%)
  blocking collectives  16.2 us (7%)
  other arithmetic  7.35 us (3%)
  local copies, waits for them, and re-layouts  7.31 us (3%)
    ppermute x26, waiting for transfers between devices, permute(): return lax.ppermute(value, AXES, pairs)  118 us
    ppermute x26, starting transfers between devices, permute(): return lax.ppermute(value, AXES, pairs)  47 us
    pallas_call x1, Pallas kernels, multiply(): pl.pallas_call(kernel, out_shape=[piece] * 8, in_specs=[pl.BlockSpec(memo...  41.5 us
    all_to_all x1, blocking collectives, body(): own_c = lax.all_to_all(columns, ('xl', 'z'), 0, 0, tiled=True)  16.2 us
  transfers between devices with their start and end apart: 26, of which 15 were waited for; matrix products, arithmetic and copies ran while one was open for 4% of the time, Pallas kernels for 0%

profile of v1, /device:TPU:1, one launch (start us, length us, event | category | flops | bytes accessed | tf_op | source)
XLA Modules:
  0.0 237.2 jit_solution(9748774137929260536)
XLA Ops:
  0.0 6.0 %collective-permute-start.10 = (f32[8,48,384]{2,1,0:T(8,128)}, f32[8,48,384]{2,1,0:T(8,128)}, u32[]{:S(2)}, u32[]{:S(2)}) collective-permute-start(f32[8,48,384]{2,1,0:T(8,128)} %param.3), channel_id=1, source_target_pairs={{0,0},{1,1},{2,64},{3,65},{4,4},{5,5},{6,68},{7,69},{8,8},{9,9},{1... | collective-permute-start | bytes 1769480 | tf_op jit(solution)/shard_map/ppermute | solution.py:31
  6.0 1.7 reshape.6
  9.1 16.2 %all_to_all.5 = f32[8,48,384]{2,1,0:T(8,128)S(1)} all-to-all(f32[8,48,384]{2,1,0:T(8,128)S(1)} %reshape.7), channel_id=1, replica_groups=mesh['y'=4,'xl'=2,'z'=4,'xh'=2,'c'=2] {'xl','z'}, dimensions={0} | all-to-all | bytes 1179648 | tf_op jit(solution)/shard_map/all_to_all | solution.py:236
  26.5 2.4 %collective-permute-start.11 = (f32[2,8,48,384]{3,2,1,0:T(8,128)S(1)}, f32[2,8,48,384]{3,2,1,0:T(8,128)S(1)}, u32[]{:S(2)}, u32[]{:S(2)}) collective-permute-start(f32[2,8,48,384]{3,2,1,0:T(8,128)S(1)} %pad_maximum_fusion.3), channel_id=1, source_target_pairs={{0,1},{1,0},{2,3},{3,2},{4,5},{5,4},{6,7},{7,6},{8,9},{9,8},{10,11... | collective-permute-start | bytes 3538952 | tf_op jit(solution)/shard_map/ppermute | solution.py:31
  28.9 2.5 %collective-permute-done.11 = f32[2,8,48,384]{3,2,1,0:T(8,128)S(1)} collective-permute-done((f32[2,8,48,384]{3,2,1,0:T(8,128)S(1)}, f32[2,8,48,384]{3,2,1,0:T(8,128)S(1)}, u32[]{:S(2)}, u32[]{:S(2)}) %collective-permute-start.11) | collective-permute-done | bytes 1179680 | tf_op jit(solution)/shard_map/ppermute | solution.py:31
  32.6 5.9 %collective-permute-start.12 = (f32[4,8,48,384]{3,2,1,0:T(8,128)S(1)}, f32[4,8,48,384]{3,2,1,0:T(8,128)}, u32[]{:S(2)}, u32[]{:S(2)}) collective-permute-start(f32[4,8,48,384]{3,2,1,0:T(8,128)S(1)} %pad_maximum_fusion.refs_8_), channel_id=1, source_target_pairs={{0,32},{1,97},{2,34},{3,99},{4,36},{5,101},{6,38},{7,103},{8,40},{... | collective-permute-start | bytes 7077896 | tf_op jit(solution)/shard_map/ppermute | solution.py:31
  40.1 4.7 %collective-permute-start = (f32[8,48,384]{2,1,0:T(8,128)S(1)}, f32[8,48,384]{2,1,0:T(8,128)S(1)}, u32[]{:S(2)}, u32[]{:S(2)}) collective-permute-start(f32[8,48,384]{2,1,0:T(8,128)S(1)} %copy-done.5), channel_id=1, source_target_pairs={{0,0},{1,16},{2,2},{3,18},{4,4},{5,20},{6,6},{7,22},{8,8},{9,24},{... | collective-permute-start | bytes 1769480 | tf_op jit(solution)/shard_map/ppermute | solution.py:31
  44.8 10.6 %collective-permute-done.2 = f32[8,48,384]{2,1,0:T(8,128)S(1)} collective-permute-done((f32[8,48,384]{2,1,0:T(8,128)S(1)}, f32[8,48,384]{2,1,0:T(8,128)S(1)}, u32[]{:S(2)}, u32[]{:S(2)}) %collective-permute-start.2) | collective-permute-done | bytes 589856 | tf_op jit(solution)/shard_map/ppermute | solution.py:31
  56.4 2.2 collective-permute-start.5
  58.6 4.1 %collective-permute-done.1 = f32[8,48,384]{2,1,0:T(8,128)S(1)} collective-permute-done((f32[8,48,384]{2,1,0:T(8,128)S(1)}, f32[8,48,384]{2,1,0:T(8,128)S(1)}, u32[]{:S(2)}, u32[]{:S(2)}) %collective-permute-start.1) | collective-permute-done | bytes 589856 | tf_op jit(solution)/shard_map/ppermute | solution.py:31
  62.7 9.7 %collective-permute-done = f32[8,48,384]{2,1,0:T(8,128)S(1)} collective-permute-done((f32[8,48,384]{2,1,0:T(8,128)S(1)}, f32[8,48,384]{2,1,0:T(8,128)S(1)}, u32[]{:S(2)}, u32[]{:S(2)}) %collective-permute-start) | collective-permute-done | bytes 589856 | tf_op jit(solution)/shard_map/ppermute | solution.py:31
  73.6 1.6 collective-permute-start.4
  75.2 1.3 slice.20
  76.6 3.2 %collective-permute-start.13 = (f32[2,8,48,384]{3,2,1,0:T(8,128)S(1)}, f32[2,8,48,384]{3,2,1,0:T(8,128)}, u32[]{:S(2)}, u32[]{:S(2)}) collective-permute-start(f32[2,8,48,384]{3,2,1,0:T(8,128)S(1)} %slice.20), channel_id=1, source_target_pairs={{0,32},{1,97},{2,34},{3,99},{4,36},{5,101},{6,38},{7,103},{8,40},{... | collective-permute-start | bytes 3538952 | tf_op jit(solution)/shard_map/ppermute | solution.py:31
  79.8 1.5 collective-permute-start.6
  81.5 8.1 %collective-permute-done.4.refs_2_ = f32[2,8,48,384]{3,2,1,0:T(8,128)} collective-permute-done((f32[2,8,48,384]{3,2,1,0:T(8,128)}, f32[2,8,48,384]{3,2,1,0:T(8,128)}, u32[]{:S(2)}, u32[]{:S(2)}) %collective-permute-start.4) | collective-permute-done | bytes 1179680 | tf_op jit(solution)/shard_map/ppermute | solution.py:31
  89.6 2.5 %collective-permute-start.8 = (f32[2,8,48,384]{3,2,1,0:T(8,128)}, f32[2,8,48,384]{3,2,1,0:T(8,128)}, u32[]{:S(2)}, u32[]{:S(2)}) collective-permute-start(f32[2,8,48,384]{3,2,1,0:T(8,128)} %collective-permute-done.4.refs_2_), channel_id=1, source_target_pairs={{0,18},{1,13},{2,16},{3,15},{4,22},{5,1},{6,20},{7,3},{8,26},{9,5}... | collective-permute-start | bytes 3538952 | tf_op jit(solution)/shard_map/ppermute | solution.py:31
  93.1 2.8 %collective-permute-start.15 = (f32[2,8,48,384]{3,2,1,0:T(8,128)}, f32[2,8,48,384]{3,2,1,0:T(8,128)}, u32[]{:S(2)}, u32[]{:S(2)}) collective-permute-start(f32[2,8,48,384]{3,2,1,0:T(8,128)} %collective-permute-done.13.refs_10_), channel_id=1, source_target_pairs={{0,1},{1,0},{2,3},{3,2},{4,5},{5,4},{6,7},{7,6},{8,9},{9,8},{10,11... | collective-permute-start | bytes 3538952 | tf_op jit(solution)/shard_map/ppermute | solution.py:31
  96.7 12.5 %collective-permute-done.9.refs_7_ = f32[2,8,48,384]{3,2,1,0:T(8,128)S(1)} collective-permute-done((f32[2,8,48,384]{3,2,1,0:T(8,128)}, f32[2,8,48,384]{3,2,1,0:T(8,128)S(1)}, u32[]{:S(2)}, u32[]{:S(2)}) %collective-permute-start.9) | collective-permute-done | bytes 1179680 | tf_op jit(solution)/shard_map/ppermute | solution.py:31
  110.3 1.5 copy-done.6
  111.7 41.5 %shard_map.28 = (f32[2,8,48,384]{3,2,1,0:T(8,128)}, f32[2,8,48,384]{3,2,1,0:T(8,128)}, f32[2,8,48,384]{3,2,1,0:T(8,128)}, f32[2,8,48,384]{3,2,1,0:T(8,128)}, f32...) custom-call(s32[4]{0:T(128)} %pad_add_fusion.place, ...), custom_call_target="tpu_custom_call" | custom-call | flops 21743271936 | bytes 29360128 | tf_op jit(solution)/shard_map/pallas_call | solution.py:190
  153.6 2.4 collective-permute-start.22
  156.0 14.1 %collective-permute-done.16 = f32[2,8,48,384]{3,2,1,0:T(8,128)S(1)} collective-permute-done((f32[2,8,48,384]{3,2,1,0:T(8,128)}, f32[2,8,48,384]{3,2,1,0:T(8,128)S(1)}, u32[]{:S(2)}, u32[]{:S(2)}) %collective-permute-start.16) | collective-permute-done | bytes 1179680 | tf_op jit(solution)/shard_map/ppermute | solution.py:31
  170.1 1.6 add.31
  172.2 2.5 %collective-permute-start.23 = (f32[2,8,48,384]{3,2,1,0:T(8,128)S(1)}, f32[2,8,48,384]{3,2,1,0:T(8,128)S(1)}, u32[]{:S(2)}, u32[]{:S(2)}) collective-permute-start(f32[2,8,48,384]{3,2,1,0:T(8,128)S(1)} %add.36), channel_id=1, source_target_pairs={{0,18},{1,13},{2,16},{3,15},{4,22},{5,1},{6,20},{7,3},{8,26},{9,5}... | collective-permute-start | bytes 3538952 | tf_op jit(solution)/shard_map/ppermute | solution.py:31
  174.7 7.4 %collective-permute-done.18 = f32[2,8,48,384]{3,2,1,0:T(8,128)S(1)} collective-permute-done((f32[2,8,48,384]{3,2,1,0:T(8,128)}, f32[2,8,48,384]{3,2,1,0:T(8,128)S(1)}, u32[]{:S(2)}, u32[]{:S(2)}) %collective-permute-start.18) | collective-permute-done | bytes 1179680 | tf_op jit(solution)/shard_map/ppermute | solution.py:31
  182.1 6.2 %collective-permute-done.17 = f32[2,8,48,384]{3,2,1,0:T(8,128)S(1)} collective-permute-done((f32[2,8,48,384]{3,2,1,0:T(8,128)S(1)}, f32[2,8,48,384]{3,2,1,0:T(8,128)S(1)}, u32[]{:S(2)}, u32[]{:S(2)}) %collective-permute-start.17) | collective-permute-done | bytes 1179680 | tf_op jit(solution)/shard_map/ppermute | solution.py:31
  188.7 3.5 %collective-permute-start.19 = (f32[8,48,384]{2,1,0:T(8,128)S(1)}, f32[8,48,384]{2,1,0:T(8,128)S(1)}, u32[]{:S(2)}, u32[]{:S(2)}) collective-permute-start(f32[8,48,384]{2,1,0:T(8,128)S(1)} %get-tuple-element.22), channel_id=1, source_target_pairs={{0,0},{1,16},{2,2},{3,18},{4,4},{5,20},{6,6},{7,22},{8,8},{9,24},{... | collective-permute-start | bytes 1769480 | tf_op jit(solution)/shard_map/ppermute | solution.py:31
  192.2 19.8 %collective-permute-done.21 = f32[2,8,48,384]{3,2,1,0:T(8,128)S(1)} collective-permute-done((f32[2,8,48,384]{3,2,1,0:T(8,128)S(1)}, f32[2,8,48,384]{3,2,1,0:T(8,128)S(1)}, u32[]{:S(2)}, u32[]{:S(2)}) %collective-permute-start.21) | collective-permute-done | bytes 1179680 | tf_op jit(solution)/shard_map/ppermute | solution.py:31
  212.4 2.8 %collective-permute-start.24 = (f32[8,48,384]{2,1,0:T(8,128)S(1)}, f32[8,48,384]{2,1,0:T(8,128)S(1)}, u32[]{:S(2)}, u32[]{:S(2)}) collective-permute-start(f32[8,48,384]{2,1,0:T(8,128)S(1)} %get-tuple-element.24), channel_id=1, source_target_pairs={{0,8},{1,18},{2,10},{3,16},{4,12},{5,22},{6,14},{7,20},{8,0},{9,26... | collective-permute-start | bytes 1769480 | tf_op jit(solution)/shard_map/ppermute | solution.py:31
  215.2 13.8 %collective-permute-done.25 = f32[8,48,384]{2,1,0:T(8,128)S(1)} collective-permute-done((f32[8,48,384]{2,1,0:T(8,128)S(1)}, f32[8,48,384]{2,1,0:T(8,128)S(1)}, u32[]{:S(2)}, u32[]{:S(2)}) %collective-permute-start.25) | collective-permute-done | bytes 589856 | tf_op jit(solution)/shard_map/ppermute | solution.py:31
  229.0 7.3 %collective-permute-done.24 = f32[8,48,384]{2,1,0:T(8,128)S(1)} collective-permute-done((f32[8,48,384]{2,1,0:T(8,128)S(1)}, f32[8,48,384]{2,1,0:T(8,128)S(1)}, u32[]{:S(2)}, u32[]{:S(2)}) %collective-permute-start.24) | collective-permute-done | bytes 589856 | tf_op jit(solution)/shard_map/ppermute | solution.py:31
  (58 shorter events, 13.0 us)
Async XLA Ops:
  0.0 25.3 %collective-permute-start.10 = (f32[8,48,384]{2,1,0:T(8,128)}, f32[8,48,384]{2,1,0:T(8,128)}, u32[]{:S(2)}, u32[]{:S(2)}) collective-permute-start(f32[8,48,384]{2,1,0:T(8,128)} %param.3), channel_id=1, source_target_pairs={{0,0},{1,1},{2,64},{3,65},{4,4},{5,5},{6,68},{7,69},{8,8},{9,9},{1... | collective-permute-start | bytes 1769480 | tf_op jit(solution)/shard_map/ppermute | solution.py:31
  26.5 12.0 %copy-start.5 = (f32[8,48,384]{2,1,0:T(8,128)S(1)}, f32[8,48,384]{2,1,0:T(8,128)}, u32[]{:S(2)}) copy-start(f32[8,48,384]{2,1,0:T(8,128)} %param.2) | copy-start | bytes 1769476
  26.5 4.9 %collective-permute-start.11 = (f32[2,8,48,384]{3,2,1,0:T(8,128)S(1)}, f32[2,8,48,384]{3,2,1,0:T(8,128)S(1)}, u32[]{:S(2)}, u32[]{:S(2)}) collective-permute-start(f32[2,8,48,384]{3,2,1,0:T(8,128)S(1)} %pad_maximum_fusion.3), channel_id=1, source_target_pairs={{0,1},{1,0},{2,3},{3,2},{4,5},{5,4},{6,7},{7,6},{8,9},{9,8},{10,11... | collective-permute-start | bytes 3538952 | tf_op jit(solution)/shard_map/ppermute | solution.py:31
  32.6 23.2 %copy-start = (f32[4,8,48,384]{3,2,1,0:T(8,128)}, f32[4,8,48,384]{3,2,1,0:T(8,128)S(1)}, u32[]{:S(2)}) copy-start(f32[4,8,48,384]{3,2,1,0:T(8,128)S(1)} %pad_maximum_fusion.refs_8_) | copy-start | bytes 7077892
  32.6 42.6 %collective-permute-start.12 = (f32[4,8,48,384]{3,2,1,0:T(8,128)S(1)}, f32[4,8,48,384]{3,2,1,0:T(8,128)}, u32[]{:S(2)}, u32[]{:S(2)}) collective-permute-start(f32[4,8,48,384]{3,2,1,0:T(8,128)S(1)} %pad_maximum_fusion.refs_8_), channel_id=1, source_target_pairs={{0,32},{1,97},{2,34},{3,99},{4,36},{5,101},{6,38},{7,103},{8,40},{... | collective-permute-start | bytes 7077896 | tf_op jit(solution)/shard_map/ppermute | solution.py:31
  38.5 16.9 %collective-permute-start.2 = (f32[8,48,384]{2,1,0:T(8,128)S(1)}, f32[8,48,384]{2,1,0:T(8,128)S(1)}, u32[]{:S(2)}, u32[]{:S(2)}) collective-permute-start(f32[8,48,384]{2,1,0:T(8,128)S(1)} %copy-done.5), channel_id=1, source_target_pairs={{0,8},{1,24},{2,10},{3,26},{4,12},{5,28},{6,14},{7,30},{8,0},{9,16... | collective-permute-start | bytes 1769480 | tf_op jit(solution)/shard_map/ppermute | solution.py:31
  38.5 17.2 %collective-permute-start.3 = (f32[8,48,384]{2,1,0:T(8,128)S(1)}, f32[8,48,384]{2,1,0:T(8,128)S(1)}, u32[]{:S(2)}, u32[]{:S(2)}) collective-permute-start(f32[8,48,384]{2,1,0:T(8,128)S(1)} %copy-done.5), channel_id=1, source_target_pairs={{0,4},{1,20},{2,6},{3,22},{4,8},{5,24},{6,10},{7,26},{8,12},{9,28}... | collective-permute-start | bytes 1769480 | tf_op jit(solution)/shard_map/ppermute | solution.py:31
  39.7 23.0 %collective-permute-start.1 = (f32[8,48,384]{2,1,0:T(8,128)S(1)}, f32[8,48,384]{2,1,0:T(8,128)S(1)}, u32[]{:S(2)}, u32[]{:S(2)}) collective-permute-start(f32[8,48,384]{2,1,0:T(8,128)S(1)} %copy-done.5), channel_id=1, source_target_pairs={{0,12},{1,28},{2,14},{3,30},{4,0},{5,16},{6,2},{7,18},{8,4},{9,20}... | collective-permute-start | bytes 1769480 | tf_op jit(solution)/shard_map/ppermute | solution.py:31
  40.1 32.3 %collective-permute-start = (f32[8,48,384]{2,1,0:T(8,128)S(1)}, f32[8,48,384]{2,1,0:T(8,128)S(1)}, u32[]{:S(2)}, u32[]{:S(2)}) collective-permute-start(f32[8,48,384]{2,1,0:T(8,128)S(1)} %copy-done.5), channel_id=1, source_target_pairs={{0,0},{1,16},{2,2},{3,18},{4,4},{5,20},{6,6},{7,22},{8,8},{9,24},{... | collective-permute-start | bytes 1769480 | tf_op jit(solution)/shard_map/ppermute | solution.py:31
  55.8 17.8 %copy-start.2 = (f32[2,8,48,384]{3,2,1,0:T(8,128)}, f32[2,8,48,384]{3,2,1,0:T(8,128)S(1)}, u32[]{:S(2)}) copy-start(f32[2,8,48,384]{3,2,1,0:T(8,128)S(1)} %pad_maximum_fusion.2.refs_1_) | copy-start | bytes 3538948
  55.8 24.0 %collective-permute-start.7 = (f32[2,8,48,384]{3,2,1,0:T(8,128)S(1)}, f32[2,8,48,384]{3,2,1,0:T(8,128)}, u32[]{:S(2)}, u32[]{:S(2)}) collective-permute-start(f32[2,8,48,384]{3,2,1,0:T(8,128)S(1)} %pad_maximum_fusion.2.refs_1_), channel_id=1, source_target_pairs={{0,16},{1,5},{2,18},{3,7},{4,20},{5,9},{6,22},{7,11},{8,24},{9,13}... | collective-permute-start | bytes 3538952 | tf_op jit(solution)/shard_map/ppermute | solution.py:31
  56.4 25.0 %collective-permute-start.5 = (f32[2,8,48,384]{3,2,1,0:T(8,128)S(1)}, f32[2,8,48,384]{3,2,1,0:T(8,128)S(1)}, u32[]{:S(2)}, u32[]{:S(2)}) collective-permute-start(f32[2,8,48,384]{3,2,1,0:T(8,128)S(1)} %pad_maximum_fusion.2.refs_1_), channel_id=1, source_target_pairs={{0,18},{1,13},{2,16},{3,15},{4,22},{5,1},{6,20},{7,3},{8,26},{9,5}... | collective-permute-start | bytes 3538952 | tf_op jit(solution)/shard_map/ppermute | solution.py:31
  73.6 16.0 %collective-permute-start.4 = (f32[2,8,48,384]{3,2,1,0:T(8,128)}, f32[2,8,48,384]{3,2,1,0:T(8,128)}, u32[]{:S(2)}, u32[]{:S(2)}) collective-permute-start(f32[2,8,48,384]{3,2,1,0:T(8,128)} %pad_maximum_fusion.1.refs_0_), channel_id=1, source_target_pairs={{0,18},{1,13},{2,16},{3,15},{4,22},{5,1},{6,20},{7,3},{8,26},{9,5}... | collective-permute-start | bytes 3538952 | tf_op jit(solution)/shard_map/ppermute | solution.py:31
  76.6 16.5 %collective-permute-start.13 = (f32[2,8,48,384]{3,2,1,0:T(8,128)S(1)}, f32[2,8,48,384]{3,2,1,0:T(8,128)}, u32[]{:S(2)}, u32[]{:S(2)}) collective-permute-start(f32[2,8,48,384]{3,2,1,0:T(8,128)S(1)} %slice.20), channel_id=1, source_target_pairs={{0,32},{1,97},{2,34},{3,99},{4,36},{5,101},{6,38},{7,103},{8,40},{... | collective-permute-start | bytes 3538952 | tf_op jit(solution)/shard_map/ppermute | solution.py:31
  79.8 29.4 %collective-permute-start.14 = (f32[4,8,48,384]{3,2,1,0:T(8,128)}, f32[4,8,48,384]{3,2,1,0:T(8,128)S(1)}, u32[]{:S(2)}, u32[]{:S(2)}) collective-permute-start(f32[4,8,48,384]{3,2,1,0:T(8,128)} %collective-permute-done.12.refs_9_), channel_id=1, source_target_pairs={{0,1},{1,0},{2,3},{3,2},{4,5},{5,4},{6,7},{7,6},{8,9},{9,8},{10,11... | collective-permute-start | bytes 7077896 | tf_op jit(solution)/shard_map/ppermute | solution.py:31
  79.8 16.9 %collective-permute-start.6 = (f32[2,8,48,384]{3,2,1,0:T(8,128)}, f32[2,8,48,384]{3,2,1,0:T(8,128)}, u32[]{:S(2)}, u32[]{:S(2)}) collective-permute-start(f32[2,8,48,384]{3,2,1,0:T(8,128)} %pad_maximum_fusion.1.refs_0_), channel_id=1, source_target_pairs={{0,16},{1,5},{2,18},{3,7},{4,20},{5,9},{6,22},{7,11},{8,24},{9,13}... | collective-permute-start | bytes 3538952 | tf_op jit(solution)/shard_map/ppermute | solution.py:31
  81.4 11.7 %copy-start.7 = (f32[2,8,48,384]{3,2,1,0:T(8,128)}, f32[2,8,48,384]{3,2,1,0:T(8,128)S(1)}, u32[]{:S(2)}) copy-start(f32[2,8,48,384]{3,2,1,0:T(8,128)S(1)} %collective-permute-done.5.refs_3_) | copy-start | bytes 3538948
  81.4 27.9 %collective-permute-start.9 = (f32[2,8,48,384]{3,2,1,0:T(8,128)}, f32[2,8,48,384]{3,2,1,0:T(8,128)S(1)}, u32[]{:S(2)}, u32[]{:S(2)}) collective-permute-start(f32[2,8,48,384]{3,2,1,0:T(8,128)} %collective-permute-done.7.refs_5_), channel_id=1, source_target_pairs={{0,16},{1,5},{2,18},{3,7},{4,20},{5,9},{6,22},{7,11},{8,24},{9,13}... | collective-permute-start | bytes 3538952 | tf_op jit(solution)/shard_map/ppermute | solution.py:31
  89.6 19.6 %collective-permute-start.8 = (f32[2,8,48,384]{3,2,1,0:T(8,128)}, f32[2,8,48,384]{3,2,1,0:T(8,128)}, u32[]{:S(2)}, u32[]{:S(2)}) collective-permute-start(f32[2,8,48,384]{3,2,1,0:T(8,128)} %collective-permute-done.4.refs_2_), channel_id=1, source_target_pairs={{0,18},{1,13},{2,16},{3,15},{4,22},{5,1},{6,20},{7,3},{8,26},{9,5}... | collective-permute-start | bytes 3538952 | tf_op jit(solution)/shard_map/ppermute | solution.py:31
  93.1 16.2 %collective-permute-start.15 = (f32[2,8,48,384]{3,2,1,0:T(8,128)}, f32[2,8,48,384]{3,2,1,0:T(8,128)}, u32[]{:S(2)}, u32[]{:S(2)}) collective-permute-start(f32[2,8,48,384]{3,2,1,0:T(8,128)} %collective-permute-done.13.refs_10_), channel_id=1, source_target_pairs={{0,1},{1,0},{2,3},{3,2},{4,5},{5,4},{6,7},{7,6},{8,9},{9,8},{10,11... | collective-permute-start | bytes 3538952 | tf_op jit(solution)/shard_map/ppermute | solution.py:31
  153.3 16.8 %collective-permute-start.16 = (f32[2,8,48,384]{3,2,1,0:T(8,128)}, f32[2,8,48,384]{3,2,1,0:T(8,128)S(1)}, u32[]{:S(2)}, u32[]{:S(2)}) collective-permute-start(f32[2,8,48,384]{3,2,1,0:T(8,128)} %get-tuple-element.15), channel_id=1, source_target_pairs={{0,16},{1,5},{2,18},{3,7},{4,20},{5,9},{6,22},{7,11},{8,24},{9,13}... | collective-permute-start | bytes 3538952 | tf_op jit(solution)/shard_map/ppermute | solution.py:31
  153.6 18.2 %collective-permute-start.22 = (f32[2,8,48,384]{3,2,1,0:T(8,128)}, f32[2,8,48,384]{3,2,1,0:T(8,128)S(1)}, u32[]{:S(2)}, u32[]{:S(2)}) collective-permute-start(f32[2,8,48,384]{3,2,1,0:T(8,128)} %get-tuple-element.20), channel_id=1, source_target_pairs={{0,18},{1,13},{2,16},{3,15},{4,22},{5,1},{6,20},{7,3},{8,26},{9,5}... | collective-permute-start | bytes 3538952 | tf_op jit(solution)/shard_map/ppermute | solution.py:31
  156.0 26.1 %collective-permute-start.18 = (f32[2,8,48,384]{3,2,1,0:T(8,128)}, f32[2,8,48,384]{3,2,1,0:T(8,128)S(1)}, u32[]{:S(2)}, u32[]{:S(2)}) collective-permute-start(f32[2,8,48,384]{3,2,1,0:T(8,128)} %get-tuple-element.16), channel_id=1, source_target_pairs={{0,18},{1,13},{2,16},{3,15},{4,22},{5,1},{6,20},{7,3},{8,26},{9,5}... | collective-permute-start | bytes 3538952 | tf_op jit(solution)/shard_map/ppermute | solution.py:31
  171.7 16.6 %collective-permute-start.17 = (f32[2,8,48,384]{3,2,1,0:T(8,128)S(1)}, f32[2,8,48,384]{3,2,1,0:T(8,128)S(1)}, u32[]{:S(2)}, u32[]{:S(2)}) collective-permute-start(f32[2,8,48,384]{3,2,1,0:T(8,128)S(1)} %add.31), channel_id=1, source_target_pairs={{0,16},{1,5},{2,18},{3,7},{4,20},{5,9},{6,22},{7,11},{8,24},{9,13}... | collective-permute-start | bytes 3538952 | tf_op jit(solution)/shard_map/ppermute | solution.py:31
  171.8 40.3 %collective-permute-start.21 = (f32[2,8,48,384]{3,2,1,0:T(8,128)S(1)}, f32[2,8,48,384]{3,2,1,0:T(8,128)S(1)}, u32[]{:S(2)}, u32[]{:S(2)}) collective-permute-start(f32[2,8,48,384]{3,2,1,0:T(8,128)S(1)} %copy-done.9), channel_id=1, source_target_pairs={{0,16},{1,5},{2,18},{3,7},{4,20},{5,9},{6,22},{7,11},{8,24},{9,13}... | collective-permute-start | bytes 3538952 | tf_op jit(solution)/shard_map/ppermute | solution.py:31
  172.1 16.2 %copy-start.4 = (f32[2,8,48,384]{3,2,1,0:T(8,128)S(1)}, f32[2,8,48,384]{3,2,1,0:T(8,128)}, u32[]{:S(2)}) copy-start(f32[2,8,48,384]{3,2,1,0:T(8,128)} %get-tuple-element.13) | copy-start | bytes 3538948
  172.2 39.8 %collective-permute-start.23 = (f32[2,8,48,384]{3,2,1,0:T(8,128)S(1)}, f32[2,8,48,384]{3,2,1,0:T(8,128)S(1)}, u32[]{:S(2)}, u32[]{:S(2)}) collective-permute-start(f32[2,8,48,384]{3,2,1,0:T(8,128)S(1)} %add.36), channel_id=1, source_target_pairs={{0,18},{1,13},{2,16},{3,15},{4,22},{5,1},{6,20},{7,3},{8,26},{9,5}... | collective-permute-start | bytes 3538952 | tf_op jit(solution)/shard_map/ppermute | solution.py:31
  188.5 23.6 %copy-start.3 = (f32[2,8,48,384]{3,2,1,0:T(8,128)S(1)}, f32[2,8,48,384]{3,2,1,0:T(8,128)}, u32[]{:S(2)}) copy-start(f32[2,8,48,384]{3,2,1,0:T(8,128)} %get-tuple-element.17) | copy-start | bytes 3538948
  188.6 26.6 %collective-permute-start.20 = (f32[8,48,384]{2,1,0:T(8,128)S(1)}, f32[8,48,384]{2,1,0:T(8,128)S(1)}, u32[]{:S(2)}, u32[]{:S(2)}) collective-permute-start(f32[8,48,384]{2,1,0:T(8,128)S(1)} %get-tuple-element.21), channel_id=1, source_target_pairs={{0,4},{1,17},{2,6},{3,19},{4,8},{5,21},{6,10},{7,23},{8,12},{9,25}... | collective-permute-start | bytes 1769480 | tf_op jit(solution)/shard_map/ppermute | solution.py:31
  188.7 26.5 %collective-permute-start.19 = (f32[8,48,384]{2,1,0:T(8,128)S(1)}, f32[8,48,384]{2,1,0:T(8,128)S(1)}, u32[]{:S(2)}, u32[]{:S(2)}) collective-permute-start(f32[8,48,384]{2,1,0:T(8,128)S(1)} %get-tuple-element.22), channel_id=1, source_target_pairs={{0,0},{1,16},{2,2},{3,18},{4,4},{5,20},{6,6},{7,22},{8,8},{9,24},{... | collective-permute-start | bytes 1769480 | tf_op jit(solution)/shard_map/ppermute | solution.py:31
  212.3 16.7 %collective-permute-start.25 = (f32[8,48,384]{2,1,0:T(8,128)S(1)}, f32[8,48,384]{2,1,0:T(8,128)S(1)}, u32[]{:S(2)}, u32[]{:S(2)}) collective-permute-start(f32[8,48,384]{2,1,0:T(8,128)S(1)} %get-tuple-element.23), channel_id=1, source_target_pairs={{0,12},{1,19},{2,14},{3,17},{4,0},{5,23},{6,2},{7,21},{8,4},{9,27}... | collective-permute-start | bytes 1769480 | tf_op jit(solution)/shard_map/ppermute | solution.py:31
  212.4 23.9 %collective-permute-start.24 = (f32[8,48,384]{2,1,0:T(8,128)S(1)}, f32[8,48,384]{2,1,0:T(8,128)S(1)}, u32[]{:S(2)}, u32[]{:S(2)}) collective-permute-start(f32[8,48,384]{2,1,0:T(8,128)S(1)} %get-tuple-element.24), channel_id=1, source_target_pairs={{0,8},{1,18},{2,10},{3,16},{4,12},{5,22},{6,14},{7,20},{8,0},{9,26... | collective-permute-start | bytes 1769480 | tf_op jit(solution)/shard_map/ppermute | solution.py:31
  (4 other events, 6.1 us)

commit v2 on v0

v2 whole, which is shorter than its diff:
```python
import functools

import jax
import jax.numpy as jnp
from jax import lax
from jax.experimental import pallas as pl
from jax.experimental.pallas import tpu as pltpu
from jax.sharding import Mesh
from jax.sharding import PartitionSpec as P

AXES = ("y", "xl", "z", "xh", "c")
SIZES = (4, 2, 4, 2, 2)
F32, BF16 = jnp.float32, jnp.bfloat16


def coords(index):
    out = []
    for size in reversed(SIZES):
        out.append(index % size)
        index //= size
    return tuple(reversed(out))


def index_of(at):
    index = 0
    for size, value in zip(SIZES, at):
        index = index * size + value
    return index


def permute(value, target):
    pairs = [(s, index_of(target(*coords(s)))) for s in range(128)]
    return lax.ppermute(value, AXES, pairs)


def shift_x(at, by):
    y, xl, z, xh, c = at
    x = (2 * xh + xl + by) % 4
    return (y, x % 2, z, x // 2, c)


def shift_z(at, by):
    y, xl, z, xh, c = at
    return (y, xl, (z + by) % 4, xh, c)


def shift_y(at, by):
    y, xl, z, xh, c = at
    return ((y + by) % 4, xl, z, xh, c)


def near(at, by):
    return shift_z(at, by) if at[4] == 0 else shift_x(at, by)


def far(at, by):
    return shift_x(at, by) if at[4] == 0 else shift_z(at, by)


def swapped(at):
    y, xl, z, xh, c = at
    return (y, c, z, xh, xl)


def other_core(*at):
    return at[:4] + (1 - at[4],)


def split(value):
    high = value.astype(BF16)
    return high, (value - high.astype(F32)).astype(BF16)


def dot3(a, b):
    def one(p, q):
        return lax.dot_general(p, q, (((1,), (1,)), ((), ())), preferred_element_type=F32)

    return one(a[0], b[0]) + (one(a[0], b[1]) + one(a[1], b[0]))


def offset(value, size):
    return pl.ds(pl.multiple_of(value * size, size), size)


def row_copies(place, refs, target, vectors, sem):
    z, x, c = place[1], place[2], place[3]
    copies = []
    for ref, v, us in zip(refs, (0, 1, 3, 2, 2), (range(4), range(4), range(4), range(2), range(2, 4))):
        for k, u in enumerate(us):
            at_z = lax.rem(z + jnp.where(c == 0, u, v), 4)
            at_x = lax.rem(x + jnp.where(c == 0, v, u), 4)
            place_of = target.at[vectors, offset(at_z, 48), offset(at_x, 384)]
            copies.append(pltpu.make_async_copy(ref.at[k, vectors], place_of, sem))
    return copies


def shuffle_kernel(l_ref, out):
    for m in range(8):
        out[m] = jnp.concatenate([l_ref[p][:, m * 48 : m * 48 + 48] for p in range(8)], axis=1)


def start(copies):
    for copy in copies:
        copy.start()


def wait(copies):
    for copy in copies:
        copy.wait()


def ladder_of(place, offsets, a_hi, a_lo, c_hi, c_lo, outs):
    z, x, c = place[1], place[2], place[3]
    for n, v in enumerate(offsets):
        for k, out in enumerate(outs[2 * n : 2 * n + 2]):

            @pl.loop(0, 2)
            def _(w):
                u = 2 * k + w
                at_z = lax.rem(z + jnp.where(c == 0, u, v), 4)
                at_x = lax.rem(x + jnp.where(c == 0, v, u), 4)
                r = dot3((a_hi[at_z], a_lo[at_z]), (c_hi[at_x], c_lo[at_x]))
                out[w] = r.reshape(8, 48, 384)


def second_kernel(place, *refs):
    rows, amps, columns = refs[:5], refs[5:7], refs[7:9]
    out_a, out_b, a_hi, a_lo, c_hi, c_lo = refs[9:15]
    l_rows, t_raw, t_hi, t_lo, half, l_cols, t_sem, row_sem, c_sem = refs[15:]
    y, c = place[0], place[3]
    t_copies, c_copies = [], []
    for k in range(4):
        at_y = lax.rem(y + k, 4)
        for ref, core in zip(amps, (c, 1 - c)):
            target = t_raw.at[:, offset(lax.rem(at_y, 2), 48), offset(at_y // 2 * 2 + core, 384)]
            t_copies.append(pltpu.make_async_copy(ref.at[k], target, t_sem))
        for ref, core in zip(columns, (c, 1 - c)):
            c_copies.append(pltpu.make_async_copy(ref.at[k], l_cols.at[at_y, :, :, offset(core, 384)], c_sem))
    quads = [pl.ds(4 * q, 4) for q in range(2)]
    r_copies = [row_copies(place, rows, l_rows, quads[q], row_sem.at[q]) for q in range(2)]
    start(t_copies + r_copies[0] + r_copies[1] + c_copies)
    wait(t_copies)

    @pl.loop(0, 8)
    def _(i):
        high, low = split(t_raw[i])
        t_hi[offset(i, 96), :] = high
        t_lo[offset(i, 96), :] = low

    for q in range(2):
        wait(r_copies[q])
        b = split(l_rows[quads[q]].reshape(768, 1536))
        for m in range(2):
            chunk = pl.ds(m * 384, 384)
            h = dot3((t_hi[chunk, :], t_lo[chunk, :]), b)
            for j in range(8):
                for p in range(4):
                    at = ((j % 2) * 8 + q * 4 + p) * 48
                    half[m * 4 + j // 2, at : at + 48, :] = h[j * 48 : j * 48 + 48, p * 192 : p * 192 + 192]

    @pl.loop(0, 8)
    def _(i):
        high, low = split(half[i].T)
        for at_z in range(4):
            a_hi[at_z, offset(i, 48), :] = high[at_z * 48 : at_z * 48 + 48, :]
            a_lo[at_z, offset(i, 48), :] = low[at_z * 48 : at_z * 48 + 48, :]

    wait(c_copies)

    @pl.loop(0, 4)
    def _(e):
        c_hi[e], c_lo[e] = split(l_cols[e].reshape(384, 768))

    ladder_of(place, (2,), a_hi, a_lo, c_hi, c_lo, (out_a, out_b))


def third_kernel(offsets, place, a_hi, a_lo, c_hi, c_lo, *outs):
    ladder_of(place, offsets, a_hi, a_lo, c_hi, c_lo, outs)


ANYWHERE = pl.BlockSpec(memory_space=pl.ANY)
ON_SMEM = pl.BlockSpec(memory_space=pltpu.SMEM)
ON_VMEM = pl.BlockSpec(memory_space=pltpu.VMEM)
DMA = pltpu.SemaphoreType.DMA
BLOCKS = (4, 384, 768)
PAIR = jax.ShapeDtypeStruct((2, 8, 48, 384), F32)
HALF = jax.ShapeDtypeStruct(BLOCKS, BF16)


def call(body, out_shape, spec, scratch, megabytes, units, place, *args):
    return pl.pallas_call(
        body,
        out_shape=out_shape,
        in_specs=[ON_SMEM] + [spec] * len(args),
        out_specs=[ON_VMEM] * len(out_shape),
        scratch_shapes=scratch,
        compiler_params=pltpu.CompilerParams(vmem_limit_bytes=megabytes << 20),
        cost_estimate=pl.CostEstimate(flops=units * 3 * 905969664, bytes_accessed=12 << 20, transcendentals=0),
    )(place, *args)


def second(place, rows, amps, columns):
    scratch = [
        pltpu.VMEM((8, 192, 1536), F32),
        pltpu.VMEM((8, 96, 1536), F32),
        pltpu.VMEM((768, 1536), BF16),
        pltpu.VMEM((768, 1536), BF16),
        pltpu.VMEM((8, 768, 192), F32),
        pltpu.VMEM((4, 8, 48, 768), F32),
        DMA,
        DMA((2,)),
        DMA,
    ]
    return call(second_kernel, [PAIR, PAIR] + [HALF] * 4, ANYWHERE, scratch, 56, 5, place, *rows, *amps, *columns)


def third(offsets, place, halves):
    body = functools.partial(third_kernel, offsets)
    return call(body, [PAIR] * (2 * len(offsets)), ON_VMEM, [], 24, len(offsets), place, *halves)


def shuffle(cholesky):
    return pl.pallas_call(
        shuffle_kernel,
        out_shape=jax.ShapeDtypeStruct((8, 48, 384), F32),
        in_specs=[ON_VMEM],
        out_specs=ON_VMEM,
        compiler_params=pltpu.CompilerParams(vmem_limit_bytes=8 << 20),
    )(cholesky)


def body(cholesky, amplitudes):
    y, xl, z, xh, c = (lax.axis_index(axis) for axis in AXES)
    place = jnp.stack([y, z, 2 * xh + xl, c]).astype(jnp.int32)

    def from_plus(value):
        return permute(value, lambda *at: far(at, -1))

    def from_minus(value):
        return permute(value, lambda *at: far(at, 1))

    mine = permute(cholesky, lambda *at: swapped(at))
    near_rows = [mine] + [permute(mine, lambda *at, u=u: near(at, -u)) for u in (1, 2, 3)]

    own_t = permute(amplitudes, lambda y, xl, z, xh, c: (2 * xh + y % 2, xl, z, y // 2, c))
    columns, mine = lax.optimization_barrier((shuffle(cholesky), mine))
    own_c = lax.all_to_all(columns, ("xl", "z"), 0, 0, tiled=True)

    def round_y(own):
        ring = jnp.stack([own] + [permute(own, lambda *at, k=k: shift_y(at, -k)) for k in (1, 2, 3)])
        return ring, permute(ring, other_core)

    amps, cols = round_y(own_t), round_y(own_c)

    s = jnp.stack(near_rows)
    p, m = from_plus(s), from_minus(s)
    rows = (s, p, m, from_plus(p[:2]), from_minus(m[2:]))

    r2a, r2b, *halves = second(place, rows, amps, cols)
    r1a, r1b, r3a, r3b = third((1, 3), place, halves)
    r0a, r0b = third((0,), place, halves)

    def to_plus(value):
        return permute(value, lambda *at: far(at, 1))

    def to_minus(value):
        return permute(value, lambda *at: far(at, -1))

    a0, a1 = to_plus(r2a), to_minus(r2b)
    b1, d0 = to_plus(r1b), to_minus(r3a)
    b0, d1 = to_plus(r1a + a0), to_minus(r3b + a1)
    q = (r0a + b0 + d0, r0b + b1 + d1)
    got = [permute(q[u // 2][u % 2], lambda *at, u=u: near(at, u)) for u in (1, 2, 3)]
    total = (q[0][0] + got[0]) + (got[1] + got[2])
    return permute(total, lambda *at: swapped(at)).transpose(0, 2, 1)


def solution(mesh):
    fine = Mesh(mesh.devices.reshape(SIZES), AXES)
    split_in = P(None, ("y", "xl", "z"), ("xh", "c"))
    return jax.shard_map(
        body, mesh=fine, in_specs=(split_in, split_in), out_specs=P(None, ("xh", "c"), ("y", "xl", "z")), check_vma=False
    )
```

time: 657 us -> 227 us (0.35)
  the two profiles are of different devices: /device:TPU:1 before, /device:TPU:14 now
where the time goes in v2:
time: 227 us; the launch traced here: 226 us
  waiting for transfers between devices  107 us (47%)
  starting transfers between devices  54.6 us (24%)
  Pallas kernels  42.2 us (19%)
  local copies, waits for them, and re-layouts  14.4 us (6%)
  other arithmetic  7.85 us (3%)
    ppermute x27, waiting for transfers between devices, permute(): return lax.ppermute(value, AXES, pairs)  107 us
    ppermute x27, starting transfers between devices, permute(): return lax.ppermute(value, AXES, pairs)  50.9 us
    pallas_call x3, Pallas kernels, call(): pl.pallas_call(body, out_shape=out_shape, in_specs=[ON_SMEM] + [spec] * l...  40.9 us
    unnamed x25, local copies, waits for them, and re-layouts  10.6 us
    another operation x2, other arithmetic, round_y(): jnp.stack([own] + [permute(own, lambda *at, k=k: shift_y(at, -k)) for k i...  4.67 us
  transfers between devices with their start and end apart: 28, of which 14 were waited for; matrix products, arithmetic and copies ran while one was open for 5% of the time, Pallas kernels for 7%

profile of v2, /device:TPU:14, one launch (start us, length us, event | category | flops | bytes accessed | tf_op | source)
XLA Modules:
  0.0 226.0 jit_solution(2760897345619720875)
XLA Ops:
  0.0 2.2 collective-permute-start
  2.2 4.8 %collective-permute-start.8 = (f32[8,48,384]{2,1,0:T(8,128)}, f32[8,48,384]{2,1,0:T(8,128)S(1)}, u32[]{:S(2)}, u32[]{:S(2)}) collective-permute-start(f32[8,48,384]{2,1,0:T(8,128)} %param.3), channel_id=1, source_target_pairs={{0,0},{1,1},{2,64},{3,65},{4,4},{5,5},{6,68},{7,69},{8,8},{9,9},{1... | collective-permute-start | bytes 1769480 | tf_op jit(solution)/shard_map/ppermute | solution.py:33
  7.0 7.4 %collective-permute-done = f32[8,48,384]{2,1,0:T(8,128)S(1)} collective-permute-done((f32[8,48,384]{2,1,0:T(8,128)}, f32[8,48,384]{2,1,0:T(8,128)S(1)}, u32[]{:S(2)}, u32[]{:S(2)}) %collective-permute-start) | collective-permute-done | bytes 589856 | tf_op jit(solution)/shard_map/ppermute | solution.py:33
  14.3 1.9 collective-permute-start.3
  16.2 3.6 %collective-permute-start.2 = (f32[8,48,384]{2,1,0:T(8,128)S(1)}, f32[8,48,384]{2,1,0:T(8,128)S(1)}, u32[]{:S(2)}, u32[]{:S(2)}) collective-permute-start(f32[8,48,384]{2,1,0:T(8,128)S(1)} %collective-permute-done), channel_id=1, source_target_pairs={{0,8},{1,3},{2,10},{3,1},{4,12},{5,7},{6,14},{7,5},{8,0},{9,11},{1... | collective-permute-start | bytes 1769480 | tf_op jit(solution)/shard_map/ppermute | solution.py:33
  23.3 3.8 %all-to-all-start = ((f32[8,48,384]{2,1,0:T(8,128)}), f32[8,48,384]{2,1,0:T(8,128)S(1)}, u32[]{:S(2)}, u32[]{:S(2)}) async-start(f32[8,48,384]{2,1,0:T(8,128)} %shard_map.28), calls=%async_computation | async-start | bytes 1179648 | tf_op jit(solution)/shard_map/all_to_all | solution.py:247
  27.0 1.7 collective-permute-done.8
  28.7 4.3 %collective-permute-start.10 = (f32[8,48,384]{2,1,0:T(8,128)S(1)}, f32[8,48,384]{2,1,0:T(8,128)}, u32[]{:S(2)}, u32[]{:S(2)}) collective-permute-start(f32[8,48,384]{2,1,0:T(8,128)S(1)} %collective-permute-done.8), channel_id=1, source_target_pairs={{0,64},{1,65},{2,66},{3,67},{4,68},{5,69},{6,70},{7,71},{8,72},{9,... | collective-permute-start | bytes 1769480 | tf_op jit(solution)/shard_map/ppermute | solution.py:33
  33.1 4.2 %collective-permute-done.2 = f32[8,48,384]{2,1,0:T(8,128)S(1)} collective-permute-done((f32[8,48,384]{2,1,0:T(8,128)S(1)}, f32[8,48,384]{2,1,0:T(8,128)S(1)}, u32[]{:S(2)}, u32[]{:S(2)}) %collective-permute-start.2) | collective-permute-done | bytes 589856 | tf_op jit(solution)/shard_map/ppermute | solution.py:33
  38.3 1.8 pad_maximum_fusion.refs_0_
  40.2 2.0 collective-permute-start.4
  42.2 6.6 %collective-permute-done.11 = f32[8,48,384]{2,1,0:T(8,128)} collective-permute-done((f32[8,48,384]{2,1,0:T(8,128)S(1)}, f32[8,48,384]{2,1,0:T(8,128)}, u32[]{:S(2)}, u32[]{:S(2)}) %collective-permute-start.11) | collective-permute-done | bytes 589856 | tf_op jit(solution)/shard_map/ppermute | solution.py:33
  48.8 3.1 %collective-permute-start.15 = (f32[8,48,384]{2,1,0:T(8,128)S(1)}, f32[8,48,384]{2,1,0:T(8,128)S(1)}, u32[]{:S(2)}, u32[]{:S(2)}) collective-permute-start(f32[8,48,384]{2,1,0:T(8,128)S(1)} %all-to-all-done), channel_id=1, source_target_pairs={{0,32},{1,33},{2,34},{3,35},{4,36},{5,37},{6,38},{7,39},{8,40},{9,... | collective-permute-start | bytes 1769480 | tf_op jit(solution)/shard_map/ppermute | solution.py:33
  51.9 8.1 %collective-permute-done.9 = f32[8,48,384]{2,1,0:T(8,128)} collective-permute-done((f32[8,48,384]{2,1,0:T(8,128)S(1)}, f32[8,48,384]{2,1,0:T(8,128)}, u32[]{:S(2)}, u32[]{:S(2)}) %collective-permute-start.9) | collective-permute-done | bytes 589856 | tf_op jit(solution)/shard_map/ppermute | solution.py:33
  61.2 3.1 %pad_maximum_fusion.1.refs_5_ = f32[4,8,48,384]{3,2,1,0:T(8,128)} fusion(f32[1,8,48,384]{3,2,1,0:T(8,128)} %bitcast.11, f32[1,8,48,384]{3,2,1,0:T(8,128)} %bitcast.10, f32[1,8,48,384]{3,2,1,0:T(8,128)} %bitcast.9, f32[1,8,48,384]{3,2,1,0:T(8,128)S(1)} %bitcast.30), kind=kLoop, calls=%fused_computation.1 | loop fusion | flops 1769472 | bytes 4718592 | tf_op jit(solution)/shard_map/stack | solution.py:250
  64.3 13.7 %collective-permute-done.15 = f32[8,48,384]{2,1,0:T(8,128)S(1)} collective-permute-done((f32[8,48,384]{2,1,0:T(8,128)S(1)}, f32[8,48,384]{2,1,0:T(8,128)S(1)}, u32[]{:S(2)}, u32[]{:S(2)}) %collective-permute-start.15) | collective-permute-done | bytes 589856 | tf_op jit(solution)/shard_map/ppermute | solution.py:33
  78.0 3.7 %collective-permute-done.13 = f32[8,48,384]{2,1,0:T(8,128)S(1)} collective-permute-done((f32[8,48,384]{2,1,0:T(8,128)S(1)}, f32[8,48,384]{2,1,0:T(8,128)S(1)}, u32[]{:S(2)}, u32[]{:S(2)}) %collective-permute-start.13) | collective-permute-done | bytes 589856 | tf_op jit(solution)/shard_map/ppermute | solution.py:33
  83.3 2.4 %slice.25 = f32[2,8,48,384]{3,2,1,0:T(8,128)} slice(f32[4,8,48,384]{3,2,1,0:T(8,128)} %collective-permute-done.5.refs_2_), slice={[2:4], [0:8], [0:48], [0:384]} | slice | bytes 2359296 | tf_op jit(solution)/shard_map/slice | solution.py:257
  87.8 2.4 %collective-permute-start.6 = (f32[2,8,48,384]{3,2,1,0:T(8,128)S(1)}, f32[2,8,48,384]{3,2,1,0:T(8,128)S(1)}, u32[]{:S(2)}, u32[]{:S(2)}) collective-permute-start(f32[2,8,48,384]{3,2,1,0:T(8,128)S(1)} %slice.24), channel_id=1, source_target_pairs={{0,18},{1,13},{2,16},{3,15},{4,22},{5,1},{6,20},{7,3},{8,26},{9,5}... | collective-permute-start | bytes 3538952 | tf_op jit(solution)/shard_map/ppermute | solution.py:33
  90.9 12.2 %collective-permute-done.7.refs_4_ = f32[2,8,48,384]{3,2,1,0:T(8,128)} collective-permute-done((f32[2,8,48,384]{3,2,1,0:T(8,128)}, f32[2,8,48,384]{3,2,1,0:T(8,128)}, u32[]{:S(2)}, u32[]{:S(2)}) %collective-permute-start.7) | collective-permute-done | bytes 1179680 | tf_op jit(solution)/shard_map/ppermute | solution.py:33
  103.1 2.4 %collective-permute-done.6.refs_3_ = f32[2,8,48,384]{3,2,1,0:T(8,128)S(1)} collective-permute-done((f32[2,8,48,384]{3,2,1,0:T(8,128)S(1)}, f32[2,8,48,384]{3,2,1,0:T(8,128)S(1)}, u32[]{:S(2)}, u32[]{:S(2)}) %collective-permute-start.6) | collective-permute-done | bytes 1179680 | tf_op jit(solution)/shard_map/ppermute | solution.py:33
  106.5 26.6 %shard_map.29 = (f32[2,8,48,384]{3,2,1,0:T(8,128)}, f32[2,8,48,384]{3,2,1,0:T(8,128)}, bf16[4,384,768]{2,1,0:T(8,128)(2,1)}, bf16[4,384,768]{2,1,0:T(8,128)(2,1)...) custom-call(s32[4]{0:T(128)} %pad_add_fusion.place, f32[4,8,48,384]{3,2,1,0:T(8,128)} %copy-done.6, ...), custom_call_target="tpu_custom_call" | custom-call | flops 13589544960 | bytes 12582912 | tf_op jit(solution)/shard_map/pallas_call | solution.py:191
  141.9 9.3 %shard_map.31 = (f32[2,8,48,384]{3,2,1,0:T(8,128)S(1)}, f32[2,8,48,384]{3,2,1,0:T(8,128)S(1)}, f32[2,8,48,384]{3,2,1,0:T(8,128)S(1)}, f32[2,8,48,384]{3,2,1,0:T(8,128)S(1)}) custom-call(s32[4]{0:T(128)S(1)} %copy-done.1, bf16[4,384,768]{2,1,0:T(8,128)(2,1)S(1)} %copy-done.2, bf16[4,384,768]{2,1,0:T(8,128)(2,1)S(1)} %copy-done.3, ...), custom_call_target="tpu_custom_call" | custom-call | flops 5435817984 | bytes 12582912 | tf_op jit(solution)/shard_map/pallas_call | solution.py:191
  152.6 2.1 collective-permute-start.18
  156.9 4.9 %shard_map.30 = (f32[2,8,48,384]{3,2,1,0:T(8,128)S(1)}, f32[2,8,48,384]{3,2,1,0:T(8,128)S(1)}) custom-call(s32[4]{0:T(128)S(1)} %copy-done.1, bf16[4,384,768]{2,1,0:T(8,128)(2,1)S(1)} %copy-done.2, bf16[4,384,768]{2,1,0:T(8,128)(2,1)S(1)} %copy-done.3, bf16[4,384,768]{2,1,0:T(8,128)(2,1)S(1)} %copy-done.4, bf16[4,384,768]{2,1,0:T(8,128)(2,1)S(1)} %copy-done.5), custom_call_target="tpu_custom_call" | custom-call | flops 2717908992 | bytes 12582912 | tf_op jit(solution)/shard_map/pallas_call | solution.py:191
  161.9 6.8 %collective-permute-done.19 = f32[2,8,48,384]{3,2,1,0:T(8,128)S(1)} collective-permute-done((f32[2,8,48,384]{3,2,1,0:T(8,128)S(1)}, f32[2,8,48,384]{3,2,1,0:T(8,128)S(1)}, u32[]{:S(2)}, u32[]{:S(2)}) %collective-permute-start.19) | collective-permute-done | bytes 1179680 | tf_op jit(solution)/shard_map/ppermute | solution.py:33
  169.1 2.1 collective-permute-start.20
  171.2 16.7 %collective-permute-done.21 = f32[2,8,48,384]{3,2,1,0:T(8,128)S(1)} collective-permute-done((f32[2,8,48,384]{3,2,1,0:T(8,128)S(1)}, f32[2,8,48,384]{3,2,1,0:T(8,128)S(1)}, u32[]{:S(2)}, u32[]{:S(2)}) %collective-permute-start.21) | collective-permute-done | bytes 1179680 | tf_op jit(solution)/shard_map/ppermute | solution.py:33
  188.1 12.0 %collective-permute-start.25 = (f32[8,48,384]{2,1,0:T(8,128)S(1)}, f32[8,48,384]{2,1,0:T(8,128)S(1)}, u32[]{:S(2)}, u32[]{:S(2)}) collective-permute-start(f32[8,48,384]{2,1,0:T(8,128)S(1)} %get-tuple-element.31), channel_id=1, source_target_pairs={{0,12},{1,19},{2,14},{3,17},{4,0},{5,23},{6,2},{7,21},{8,4},{9,27}... | collective-permute-start | bytes 1769480 | tf_op jit(solution)/shard_map/ppermute | solution.py:33
  200.1 13.7 %collective-permute-done.25 = f32[8,48,384]{2,1,0:T(8,128)S(1)} collective-permute-done((f32[8,48,384]{2,1,0:T(8,128)S(1)}, f32[8,48,384]{2,1,0:T(8,128)S(1)}, u32[]{:S(2)}, u32[]{:S(2)}) %collective-permute-start.25) | collective-permute-done | bytes 589856 | tf_op jit(solution)/shard_map/ppermute | solution.py:33
  214.0 1.9 collective-permute-start.26
  215.9 9.3 %collective-permute-done.26 = f32[8,48,384]{2,1,0:T(8,128)S(1)} collective-permute-done((f32[8,48,384]{2,1,0:T(8,128)S(1)}, f32[8,48,384]{2,1,0:T(8,128)S(1)}, u32[]{:S(2)}, u32[]{:S(2)}) %collective-permute-start.26) | collective-permute-done | bytes 589856 | tf_op jit(solution)/shard_map/ppermute | solution.py:33
  (66 shorter events, 25.2 us)
Async XLA Ops:
  0.0 14.3 %collective-permute-start = (f32[8,48,384]{2,1,0:T(8,128)}, f32[8,48,384]{2,1,0:T(8,128)S(1)}, u32[]{:S(2)}, u32[]{:S(2)}) collective-permute-start(f32[8,48,384]{2,1,0:T(8,128)} %l_ref.1), channel_id=1, source_target_pairs={{0,0},{1,16},{2,2},{3,18},{4,4},{5,20},{6,6},{7,22},{8,8},{9,24},{... | collective-permute-start | bytes 1769480 | tf_op jit(solution)/shard_map/ppermute | solution.py:33
  2.2 26.6 %collective-permute-start.8 = (f32[8,48,384]{2,1,0:T(8,128)}, f32[8,48,384]{2,1,0:T(8,128)S(1)}, u32[]{:S(2)}, u32[]{:S(2)}) collective-permute-start(f32[8,48,384]{2,1,0:T(8,128)} %param.3), channel_id=1, source_target_pairs={{0,0},{1,1},{2,64},{3,65},{4,4},{5,5},{6,68},{7,69},{8,8},{9,9},{1... | collective-permute-start | bytes 1769480 | tf_op jit(solution)/shard_map/ppermute | solution.py:33
  14.3 8.9 %copy-start.7 = (f32[8,48,384]{2,1,0:T(8,128)}, f32[8,48,384]{2,1,0:T(8,128)S(1)}, u32[]{:S(2)}) copy-start(f32[8,48,384]{2,1,0:T(8,128)S(1)} %collective-permute-done) | copy-start | bytes 1769476
  14.3 18.7 %collective-permute-start.3 = (f32[8,48,384]{2,1,0:T(8,128)S(1)}, f32[8,48,384]{2,1,0:T(8,128)S(1)}, u32[]{:S(2)}, u32[]{:S(2)}) collective-permute-start(f32[8,48,384]{2,1,0:T(8,128)S(1)} %collective-permute-done), channel_id=1, source_target_pairs={{0,4},{1,17},{2,6},{3,19},{4,8},{5,21},{6,10},{7,23},{8,12},{9,25}... | collective-permute-start | bytes 1769480 | tf_op jit(solution)/shard_map/ppermute | solution.py:33
  16.2 21.0 %collective-permute-start.2 = (f32[8,48,384]{2,1,0:T(8,128)S(1)}, f32[8,48,384]{2,1,0:T(8,128)S(1)}, u32[]{:S(2)}, u32[]{:S(2)}) collective-permute-start(f32[8,48,384]{2,1,0:T(8,128)S(1)} %collective-permute-done), channel_id=1, source_target_pairs={{0,8},{1,3},{2,10},{3,1},{4,12},{5,7},{6,14},{7,5},{8,0},{9,11},{1... | collective-permute-start | bytes 1769480 | tf_op jit(solution)/shard_map/ppermute | solution.py:33
  19.8 17.4 %collective-permute-start.1 = (f32[8,48,384]{2,1,0:T(8,128)S(1)}, f32[8,48,384]{2,1,0:T(8,128)S(1)}, u32[]{:S(2)}, u32[]{:S(2)}) collective-permute-start(f32[8,48,384]{2,1,0:T(8,128)S(1)} %collective-permute-done), channel_id=1, source_target_pairs={{0,12},{1,19},{2,14},{3,17},{4,0},{5,23},{6,2},{7,21},{8,4},{9,27}... | collective-permute-start | bytes 1769480 | tf_op jit(solution)/shard_map/ppermute | solution.py:33
  23.3 18.9 %all-to-all-start = ((f32[8,48,384]{2,1,0:T(8,128)}), f32[8,48,384]{2,1,0:T(8,128)S(1)}, u32[]{:S(2)}, u32[]{:S(2)}) async-start(f32[8,48,384]{2,1,0:T(8,128)} %shard_map.28), calls=%async_computation | async-start | bytes 1179648 | tf_op jit(solution)/shard_map/all_to_all | solution.py:247
  28.7 20.1 %collective-permute-start.11 = (f32[8,48,384]{2,1,0:T(8,128)S(1)}, f32[8,48,384]{2,1,0:T(8,128)}, u32[]{:S(2)}, u32[]{:S(2)}) collective-permute-start(f32[8,48,384]{2,1,0:T(8,128)S(1)} %collective-permute-done.8), channel_id=1, source_target_pairs={{0,32},{1,33},{2,34},{3,35},{4,36},{5,37},{6,38},{7,39},{8,40},{9,... | collective-permute-start | bytes 1769480 | tf_op jit(solution)/shard_map/ppermute | solution.py:33
  28.7 23.2 %collective-permute-start.10 = (f32[8,48,384]{2,1,0:T(8,128)S(1)}, f32[8,48,384]{2,1,0:T(8,128)}, u32[]{:S(2)}, u32[]{:S(2)}) collective-permute-start(f32[8,48,384]{2,1,0:T(8,128)S(1)} %collective-permute-done.8), channel_id=1, source_target_pairs={{0,64},{1,65},{2,66},{3,67},{4,68},{5,69},{6,70},{7,71},{8,72},{9,... | collective-permute-start | bytes 1769480 | tf_op jit(solution)/shard_map/ppermute | solution.py:33
  33.1 4.2 %copy-start.8 = (f32[8,48,384]{2,1,0:T(8,128)}, f32[8,48,384]{2,1,0:T(8,128)S(1)}, u32[]{:S(2)}) copy-start(f32[8,48,384]{2,1,0:T(8,128)S(1)} %collective-permute-done.3) | copy-start | bytes 1769476
  33.1 26.9 %collective-permute-start.9 = (f32[8,48,384]{2,1,0:T(8,128)S(1)}, f32[8,48,384]{2,1,0:T(8,128)}, u32[]{:S(2)}, u32[]{:S(2)}) collective-permute-start(f32[8,48,384]{2,1,0:T(8,128)S(1)} %collective-permute-done.8), channel_id=1, source_target_pairs={{0,96},{1,97},{2,98},{3,99},{4,100},{5,101},{6,102},{7,103},{8,104... | collective-permute-start | bytes 1769480 | tf_op jit(solution)/shard_map/ppermute | solution.py:33
  40.1 24.2 %copy-start.6 = (f32[4,8,48,384]{3,2,1,0:T(8,128)}, f32[4,8,48,384]{3,2,1,0:T(8,128)S(1)}, u32[]{:S(2)}) copy-start(f32[4,8,48,384]{3,2,1,0:T(8,128)S(1)} %pad_maximum_fusion.refs_0_) | copy-start | bytes 7077892
  40.1 43.2 %collective-permute-start.5 = (f32[4,8,48,384]{3,2,1,0:T(8,128)S(1)}, f32[4,8,48,384]{3,2,1,0:T(8,128)}, u32[]{:S(2)}, u32[]{:S(2)}) collective-permute-start(f32[4,8,48,384]{3,2,1,0:T(8,128)S(1)} %pad_maximum_fusion.refs_0_), channel_id=1, source_target_pairs={{0,16},{1,5},{2,18},{3,7},{4,20},{5,9},{6,22},{7,11},{8,24},{9,13}... | collective-permute-start | bytes 7077896 | tf_op jit(solution)/shard_map/ppermute | solution.py:33
  40.2 46.3 %collective-permute-start.4 = (f32[4,8,48,384]{3,2,1,0:T(8,128)S(1)}, f32[4,8,48,384]{3,2,1,0:T(8,128)}, u32[]{:S(2)}, u32[]{:S(2)}) collective-permute-start(f32[4,8,48,384]{3,2,1,0:T(8,128)S(1)} %pad_maximum_fusion.refs_0_), channel_id=1, source_target_pairs={{0,18},{1,13},{2,16},{3,15},{4,22},{5,1},{6,20},{7,3},{8,26},{9,5}... | collective-permute-start | bytes 7077896 | tf_op jit(solution)/shard_map/ppermute | solution.py:33
  48.8 29.1 %collective-permute-start.15 = (f32[8,48,384]{2,1,0:T(8,128)S(1)}, f32[8,48,384]{2,1,0:T(8,128)S(1)}, u32[]{:S(2)}, u32[]{:S(2)}) collective-permute-start(f32[8,48,384]{2,1,0:T(8,128)S(1)} %all-to-all-done), channel_id=1, source_target_pairs={{0,32},{1,33},{2,34},{3,35},{4,36},{5,37},{6,38},{7,39},{8,40},{9,... | collective-permute-start | bytes 1769480 | tf_op jit(solution)/shard_map/ppermute | solution.py:33
  51.9 26.0 %collective-permute-start.14 = (f32[8,48,384]{2,1,0:T(8,128)S(1)}, f32[8,48,384]{2,1,0:T(8,128)S(1)}, u32[]{:S(2)}, u32[]{:S(2)}) collective-permute-start(f32[8,48,384]{2,1,0:T(8,128)S(1)} %all-to-all-done), channel_id=1, source_target_pairs={{0,64},{1,65},{2,66},{3,67},{4,68},{5,69},{6,70},{7,71},{8,72},{9,... | collective-permute-start | bytes 1769480 | tf_op jit(solution)/shard_map/ppermute | solution.py:33
  60.0 21.7 %collective-permute-start.13 = (f32[8,48,384]{2,1,0:T(8,128)S(1)}, f32[8,48,384]{2,1,0:T(8,128)S(1)}, u32[]{:S(2)}, u32[]{:S(2)}) collective-permute-start(f32[8,48,384]{2,1,0:T(8,128)S(1)} %all-to-all-done), channel_id=1, source_target_pairs={{0,96},{1,97},{2,98},{3,99},{4,100},{5,101},{6,102},{7,103},{8,104... | collective-permute-start | bytes 1769480 | tf_op jit(solution)/shard_map/ppermute | solution.py:33
  77.9 12.9 %collective-permute-start.12 = (f32[4,8,48,384]{3,2,1,0:T(8,128)}, f32[4,8,48,384]{3,2,1,0:T(8,128)}, u32[]{:S(2)}, u32[]{:S(2)}) collective-permute-start(f32[4,8,48,384]{3,2,1,0:T(8,128)} %pad_maximum_fusion.1.refs_5_), channel_id=1, source_target_pairs={{0,1},{1,0},{2,3},{3,2},{4,5},{5,4},{6,7},{7,6},{8,9},{9,8},{10,11... | collective-permute-start | bytes 7077896 | tf_op jit(solution)/shard_map/ppermute | solution.py:33
  83.2 7.6 %collective-permute-start.16 = (f32[4,8,48,384]{3,2,1,0:T(8,128)}, f32[4,8,48,384]{3,2,1,0:T(8,128)}, u32[]{:S(2)}, u32[]{:S(2)}) collective-permute-start(f32[4,8,48,384]{3,2,1,0:T(8,128)} %pad_maximum_fusion.2.refs_7_), channel_id=1, source_target_pairs={{0,1},{1,0},{2,3},{3,2},{4,5},{5,4},{6,7},{7,6},{8,9},{9,8},{10,11... | collective-permute-start | bytes 7077896 | tf_op jit(solution)/shard_map/ppermute | solution.py:33
  85.7 17.4 %collective-permute-start.7 = (f32[2,8,48,384]{3,2,1,0:T(8,128)}, f32[2,8,48,384]{3,2,1,0:T(8,128)}, u32[]{:S(2)}, u32[]{:S(2)}) collective-permute-start(f32[2,8,48,384]{3,2,1,0:T(8,128)} %slice.25), channel_id=1, source_target_pairs={{0,16},{1,5},{2,18},{3,7},{4,20},{5,9},{6,22},{7,11},{8,24},{9,13}... | collective-permute-start | bytes 3538952 | tf_op jit(solution)/shard_map/ppermute | solution.py:33
  87.8 17.7 %collective-permute-start.6 = (f32[2,8,48,384]{3,2,1,0:T(8,128)S(1)}, f32[2,8,48,384]{3,2,1,0:T(8,128)S(1)}, u32[]{:S(2)}, u32[]{:S(2)}) collective-permute-start(f32[2,8,48,384]{3,2,1,0:T(8,128)S(1)} %slice.24), channel_id=1, source_target_pairs={{0,18},{1,13},{2,16},{3,15},{4,22},{5,1},{6,20},{7,3},{8,26},{9,5}... | collective-permute-start | bytes 3538952 | tf_op jit(solution)/shard_map/ppermute | solution.py:33
  90.8 44.4 %copy-start.1 = (s32[4]{0:T(128)S(1)}, s32[4]{0:T(128)}, u32[]{:S(2)}) copy-start(s32[4]{0:T(128)} %pad_add_fusion.place) | copy-start | bytes 52
  133.1 19.4 %collective-permute-start.17 = (f32[2,8,48,384]{3,2,1,0:T(8,128)}, f32[2,8,48,384]{3,2,1,0:T(8,128)S(1)}, u32[]{:S(2)}, u32[]{:S(2)}) collective-permute-start(f32[2,8,48,384]{3,2,1,0:T(8,128)} %get-tuple-element.25), channel_id=1, source_target_pairs={{0,16},{1,5},{2,18},{3,7},{4,20},{5,9},{6,22},{7,11},{8,24},{9,13}... | collective-permute-start | bytes 3538952 | tf_op jit(solution)/shard_map/ppermute | solution.py:33
  134.7 21.5 %collective-permute-start.22 = (f32[2,8,48,384]{3,2,1,0:T(8,128)}, f32[2,8,48,384]{3,2,1,0:T(8,128)S(1)}, u32[]{:S(2)}, u32[]{:S(2)}) collective-permute-start(f32[2,8,48,384]{3,2,1,0:T(8,128)} %get-tuple-element.30), channel_id=1, source_target_pairs={{0,18},{1,13},{2,16},{3,15},{4,22},{5,1},{6,20},{7,3},{8,26},{9,5}... | collective-permute-start | bytes 3538952 | tf_op jit(solution)/shard_map/ppermute | solution.py:33
  151.2 17.5 %collective-permute-start.19 = (f32[2,8,48,384]{3,2,1,0:T(8,128)S(1)}, f32[2,8,48,384]{3,2,1,0:T(8,128)S(1)}, u32[]{:S(2)}, u32[]{:S(2)}) collective-permute-start(f32[2,8,48,384]{3,2,1,0:T(8,128)S(1)} %get-tuple-element.26), channel_id=1, source_target_pairs={{0,18},{1,13},{2,16},{3,15},{4,22},{5,1},{6,20},{7,3},{8,26},{9,5}... | collective-permute-start | bytes 3538952 | tf_op jit(solution)/shard_map/ppermute | solution.py:33
  152.6 16.3 %collective-permute-start.18 = (f32[2,8,48,384]{3,2,1,0:T(8,128)S(1)}, f32[2,8,48,384]{3,2,1,0:T(8,128)S(1)}, u32[]{:S(2)}, u32[]{:S(2)}) collective-permute-start(f32[2,8,48,384]{3,2,1,0:T(8,128)S(1)} %add.31), channel_id=1, source_target_pairs={{0,16},{1,5},{2,18},{3,7},{4,20},{5,9},{6,22},{7,11},{8,24},{9,13}... | collective-permute-start | bytes 3538952 | tf_op jit(solution)/shard_map/ppermute | solution.py:33
  154.7 33.2 %collective-permute-start.21 = (f32[2,8,48,384]{3,2,1,0:T(8,128)S(1)}, f32[2,8,48,384]{3,2,1,0:T(8,128)S(1)}, u32[]{:S(2)}, u32[]{:S(2)}) collective-permute-start(f32[2,8,48,384]{3,2,1,0:T(8,128)S(1)} %get-tuple-element.28), channel_id=1, source_target_pairs={{0,16},{1,5},{2,18},{3,7},{4,20},{5,9},{6,22},{7,11},{8,24},{9,13}... | collective-permute-start | bytes 3538952 | tf_op jit(solution)/shard_map/ppermute | solution.py:33
  156.4 31.5 %collective-permute-start.23 = (f32[2,8,48,384]{3,2,1,0:T(8,128)S(1)}, f32[2,8,48,384]{3,2,1,0:T(8,128)S(1)}, u32[]{:S(2)}, u32[]{:S(2)}) collective-permute-start(f32[2,8,48,384]{3,2,1,0:T(8,128)S(1)} %add.36), channel_id=1, source_target_pairs={{0,18},{1,13},{2,16},{3,15},{4,22},{5,1},{6,20},{7,3},{8,26},{9,5}... | collective-permute-start | bytes 3538952 | tf_op jit(solution)/shard_map/ppermute | solution.py:33
  169.1 31.0 %collective-permute-start.20 = (f32[8,48,384]{2,1,0:T(8,128)S(1)}, f32[8,48,384]{2,1,0:T(8,128)S(1)}, u32[]{:S(2)}, u32[]{:S(2)}) collective-permute-start(f32[8,48,384]{2,1,0:T(8,128)S(1)} %slice_bitcast_fusion.2), channel_id=1, source_target_pairs={{0,4},{1,17},{2,6},{3,19},{4,8},{5,21},{6,10},{7,23},{8,12},{9,25}... | collective-permute-start | bytes 1769480 | tf_op jit(solution)/shard_map/ppermute | solution.py:33
  188.1 25.7 %collective-permute-start.25 = (f32[8,48,384]{2,1,0:T(8,128)S(1)}, f32[8,48,384]{2,1,0:T(8,128)S(1)}, u32[]{:S(2)}, u32[]{:S(2)}) collective-permute-start(f32[8,48,384]{2,1,0:T(8,128)S(1)} %get-tuple-element.31), channel_id=1, source_target_pairs={{0,12},{1,19},{2,14},{3,17},{4,0},{5,23},{6,2},{7,21},{8,4},{9,27}... | collective-permute-start | bytes 1769480 | tf_op jit(solution)/shard_map/ppermute | solution.py:33
  200.1 13.7 %collective-permute-start.24 = (f32[8,48,384]{2,1,0:T(8,128)S(1)}, f32[8,48,384]{2,1,0:T(8,128)S(1)}, u32[]{:S(2)}, u32[]{:S(2)}) collective-permute-start(f32[8,48,384]{2,1,0:T(8,128)S(1)} %get-tuple-element.32), channel_id=1, source_target_pairs={{0,8},{1,3},{2,10},{3,1},{4,12},{5,7},{6,14},{7,5},{8,0},{9,11},{1... | collective-permute-start | bytes 1769480 | tf_op jit(solution)/shard_map/ppermute | solution.py:33
  214.0 11.2 %collective-permute-start.26 = (f32[8,48,384]{2,1,0:T(8,128)S(1)}, f32[8,48,384]{2,1,0:T(8,128)S(1)}, u32[]{:S(2)}, u32[]{:S(2)}) collective-permute-start(f32[8,48,384]{2,1,0:T(8,128)S(1)} %fusion.1), channel_id=1, source_target_pairs={{0,0},{1,16},{2,2},{3,18},{4,4},{5,20},{6,6},{7,22},{8,8},{9,24},{... | collective-permute-start | bytes 1769480 | tf_op jit(solution)/shard_map/ppermute | solution.py:33
  (8 other events, 10.6 us)

commit v3 on v2

--- a/solution.py
+++ b/solution.py
@@ -59,7 +59,7 @@
 
 def swapped(at):
     y, xl, z, xh, c = at
-    return (y, c, z, xh, xl)
+    return (y, xl, z // 2 * 2 + c, xh, z % 2)
 
 
 def other_core(*at):
@@ -89,8 +89,8 @@
         for k, u in enumerate(us):
             at_z = lax.rem(z + jnp.where(c == 0, u, v), 4)
             at_x = lax.rem(x + jnp.where(c == 0, v, u), 4)
-            place_of = target.at[vectors, offset(at_z, 48), offset(at_x, 384)]
-            copies.append(pltpu.make_async_copy(ref.at[k, vectors], place_of, sem))
+            b, d = lax.rem(at_x, 2) * 2 + at_z // 2, at_x // 2 * 2 + lax.rem(at_z, 2)
+            copies.append(pltpu.make_async_copy(ref.at[k, vectors], target.at[vectors, offset(b, 48), offset(d, 384)], sem))
     return copies
 
 
@@ -109,24 +109,29 @@
         copy.wait()
 
 
-def ladder_of(place, offsets, a_hi, a_lo, c_hi, c_lo, outs):
+def ladder_of(place, v, a_hi, a_lo, c_hi, c_lo, near_ones, far_ones):
     z, x, c = place[1], place[2], place[3]
-    for n, v in enumerate(offsets):
-        for k, out in enumerate(outs[2 * n : 2 * n + 2]):
-
-            @pl.loop(0, 2)
-            def _(w):
-                u = 2 * k + w
-                at_z = lax.rem(z + jnp.where(c == 0, u, v), 4)
-                at_x = lax.rem(x + jnp.where(c == 0, v, u), 4)
-                r = dot3((a_hi[at_z], a_lo[at_z]), (c_hi[at_x], c_lo[at_x]))
-                out[w] = r.reshape(8, 48, 384)
-
-
-def second_kernel(place, *refs):
-    rows, amps, columns = refs[:5], refs[5:7], refs[7:9]
-    out_a, out_b, a_hi, a_lo, c_hi, c_lo = refs[9:15]
-    l_rows, t_raw, t_hi, t_lo, half, l_cols, t_sem, row_sem, c_sem = refs[15:]
+    at_z, at_x = lax.rem(z + v, 4), lax.rem(x + v, 4)
+    bs = [jnp.where(c == 0, lax.rem(at_x, 2) * 2 + k, at_z // 2 + 2 * k) for k in range(2)]
+    cs = [jnp.where(c == 0, at_x // 2 * 2 + k, lax.rem(at_z, 2) + 2 * k) for k in range(2)]
+    left = [jnp.concatenate([ref[b] for b in bs]) for ref in (a_hi, a_lo)]
+    right = [jnp.concatenate([ref[b] for b in cs]) for ref in (c_hi, c_lo)]
+    r = dot3(left, right)
+    for i in range(2):
+        for j in range(2):
+            block = r[i * 384 : i * 384 + 384, j * 384 : j * 384 + 384].reshape(8, 48, 384)
+            u = lax.rem(jnp.where(c == 0, 2 * i + j - z, 2 * j + i - x) + 4, 4)
+
+            for n, ref in enumerate((near_ones, far_ones)):
+
+                @pl.when(u // 2 == n)
+                def _():
+                    ref[lax.rem(u, 2)] = block
+
+
+def halves_kernel(place, *refs):
+    amps, columns, outs = refs[:2], refs[2:4], refs[4:8]
+    t_raw, l_cols, t_hi, t_lo, c_hi, c_lo, t_sem, c_sem, out_sem = refs[8:]
     y, c = place[0], place[3]
     t_copies, c_copies = [], []
     for k in range(4):
@@ -136,20 +141,36 @@
             t_copies.append(pltpu.make_async_copy(ref.at[k], target, t_sem))
         for ref, core in zip(columns, (c, 1 - c)):
             c_copies.append(pltpu.make_async_copy(ref.at[k], l_cols.at[at_y, :, :, offset(core, 384)], c_sem))
-    quads = [pl.ds(4 * q, 4) for q in range(2)]
-    r_copies = [row_copies(place, rows, l_rows, quads[q], row_sem.at[q]) for q in range(2)]
+    start(t_copies + c_copies)
+    wait(t_copies)
+
+    @pl.loop(0, 8)
+    def _(i):
+        t_hi[offset(i, 96), :], t_lo[offset(i, 96), :] = split(t_raw[i])
+
+    wait(c_copies)
+
+    @pl.loop(0, 4)
+    def _(e):
+        c_hi[e], c_lo[e] = split(l_cols[e].reshape(384, 768))
+
+    copies = [pltpu.make_async_copy(ref, out, out_sem) for ref, out in zip((t_hi, t_lo, c_hi, c_lo), outs)]
+    start(copies)
+    wait(copies)
+
+
+def second_kernel(place, *refs):
+    rows, halves_in, outs = refs[:5], refs[5:9], refs[9:17]
+    l_rows, t_hi, t_lo, c_hi, c_lo, half, a_hi, a_lo = refs[17:25]
+    blocks, (t_sem, row_sem, c_sem, out_sem) = refs[25:31], refs[31:]
+    t_copies = [pltpu.make_async_copy(halves_in[k], ref, t_sem) for k, ref in enumerate((t_hi, t_lo))]
+    c_copies = [pltpu.make_async_copy(halves_in[2 + k], ref, c_sem) for k, ref in enumerate((c_hi, c_lo))]
+    r_copies = [row_copies(place, rows, l_rows, pl.ds(4 * q, 4), row_sem.at[q]) for q in range(2)]
     start(t_copies + r_copies[0] + r_copies[1] + c_copies)
     wait(t_copies)
-
-    @pl.loop(0, 8)
-    def _(i):
-        high, low = split(t_raw[i])
-        t_hi[offset(i, 96), :] = high
-        t_lo[offset(i, 96), :] = low
-
     for q in range(2):
         wait(r_copies[q])
-        b = split(l_rows[quads[q]].reshape(768, 1536))
+        b = split(l_rows[4 * q : 4 * q + 4].reshape(768, 1536))
         for m in range(2):
             chunk = pl.ds(m * 384, 384)
             h = dot3((t_hi[chunk, :], t_lo[chunk, :]), b)
@@ -161,24 +182,30 @@
     @pl.loop(0, 8)
     def _(i):
         high, low = split(half[i].T)
-        for at_z in range(4):
-            a_hi[at_z, offset(i, 48), :] = high[at_z * 48 : at_z * 48 + 48, :]
-            a_lo[at_z, offset(i, 48), :] = low[at_z * 48 : at_z * 48 + 48, :]
+        for b in range(4):
+            a_hi[b, offset(i, 48), :] = high[b * 48 : b * 48 + 48, :]
+            a_lo[b, offset(i, 48), :] = low[b * 48 : b * 48 + 48, :]
 
     wait(c_copies)
-
-    @pl.loop(0, 4)
-    def _(e):
-        c_hi[e], c_lo[e] = split(l_cols[e].reshape(384, 768))
-
-    ladder_of(place, (2,), a_hi, a_lo, c_hi, c_lo, (out_a, out_b))
-
-
-def third_kernel(offsets, place, a_hi, a_lo, c_hi, c_lo, *outs):
-    ladder_of(place, offsets, a_hi, a_lo, c_hi, c_lo, outs)
+    copies = [pltpu.make_async_copy(ref, out, out_sem) for ref, out in zip((*blocks, a_hi, a_lo), outs)]
+    start(copies[6:])
+    for k, v in enumerate((2, 1, 3)):
+        ladder_of(place, v, a_hi, a_lo, c_hi, c_lo, blocks[2 * k], blocks[2 * k + 1])
+        start(copies[2 * k : 2 * k + 2])
+    wait(copies)
+
+
+def third_kernel(place, a_hi_in, a_lo_in, c_hi_in, c_lo_in, b1, d0, out_a, out_b, a_hi, a_lo, c_hi, c_lo, sem):
+    del b1, d0
+    pairs = ((a_hi_in, a_hi), (a_lo_in, a_lo), (c_hi_in, c_hi), (c_lo_in, c_lo))
+    copies = [pltpu.make_async_copy(ref, held, sem) for ref, held in pairs]
+    start(copies)
+    wait(copies)
+    ladder_of(place, 0, a_hi, a_lo, c_hi, c_lo, out_a, out_b)
 
 
 ANYWHERE = pl.BlockSpec(memory_space=pl.ANY)
+ON_HBM = pl.BlockSpec(memory_space=pltpu.HBM)
 ON_SMEM = pl.BlockSpec(memory_space=pltpu.SMEM)
 ON_VMEM = pl.BlockSpec(memory_space=pltpu.VMEM)
 DMA = pltpu.SemaphoreType.DMA
@@ -187,36 +214,38 @@
 HALF = jax.ShapeDtypeStruct(BLOCKS, BF16)
 
 
-def call(body, out_shape, spec, scratch, megabytes, units, place, *args):
+AMPS = (768, 1536)
+HALF_AMPS = jax.ShapeDtypeStruct(AMPS, BF16)
+
+
+def call(body, out_shape, out_spec, scratch, megabytes, units, place, *args):
     return pl.pallas_call(
         body,
         out_shape=out_shape,
-        in_specs=[ON_SMEM] + [spec] * len(args),
-        out_specs=[ON_VMEM] * len(out_shape),
+        in_specs=[ON_SMEM] + [ANYWHERE] * len(args),
+        out_specs=[out_spec] * len(out_shape),
         scratch_shapes=scratch,
         compiler_params=pltpu.CompilerParams(vmem_limit_bytes=megabytes << 20),
         cost_estimate=pl.CostEstimate(flops=units * 3 * 905969664, bytes_accessed=12 << 20, transcendentals=0),
     )(place, *args)
 
 
-def second(place, rows, amps, columns):
-    scratch = [
-        pltpu.VMEM((8, 192, 1536), F32),
-        pltpu.VMEM((8, 96, 1536), F32),
-        pltpu.VMEM((768, 1536), BF16),
-        pltpu.VMEM((768, 1536), BF16),
-        pltpu.VMEM((8, 768, 192), F32),
-        pltpu.VMEM((4, 8, 48, 768), F32),
-        DMA,
-        DMA((2,)),
-        DMA,
-    ]
-    return call(second_kernel, [PAIR, PAIR] + [HALF] * 4, ANYWHERE, scratch, 56, 5, place, *rows, *amps, *columns)
-
-
-def third(offsets, place, halves):
-    body = functools.partial(third_kernel, offsets)
-    return call(body, [PAIR] * (2 * len(offsets)), ON_VMEM, [], 24, len(offsets), place, *halves)
+def halves(place, amps, columns):
+    scratch = [pltpu.VMEM((8, 96, 1536), F32), pltpu.VMEM((4, 8, 48, 768), F32)]
+    scratch += [pltpu.VMEM(AMPS, BF16)] * 2 + [pltpu.VMEM(BLOCKS, BF16)] * 2 + [DMA] * 3
+    return call(halves_kernel, [HALF_AMPS] * 2 + [HALF] * 2, ON_HBM, scratch, 24, 1, place, *amps, *columns)
+
+
+def second(place, rows, parts):
+    scratch = [pltpu.VMEM((8, 192, 1536), F32)] + [pltpu.VMEM(AMPS, BF16)] * 2 + [pltpu.VMEM(BLOCKS, BF16)] * 2
+    scratch += [pltpu.VMEM((8, 768, 192), F32)] + [pltpu.VMEM(BLOCKS, BF16)] * 2 + [pltpu.VMEM(PAIR.shape, F32)] * 6
+    scratch += [DMA, DMA((2,)), DMA, DMA]
+    return call(second_kernel, [PAIR] * 6 + [HALF] * 2, ON_HBM, scratch, 48, 7, place, *rows, *parts)
+
+
+def third(place, parts, after):
+    scratch = [pltpu.VMEM(BLOCKS, BF16)] * 4 + [DMA]
+    return call(third_kernel, [PAIR] * 2, ON_VMEM, scratch, 24, 1, place, *parts, *after)
 
 
 def shuffle(cholesky):
@@ -246,8 +275,13 @@
     columns, mine = lax.optimization_barrier((shuffle(cholesky), mine))
     own_c = lax.all_to_all(columns, ("xl", "z"), 0, 0, tiled=True)
 
+    def from_y(value, by):
+        return permute(value, lambda *at: shift_y(at, -by))
+
     def round_y(own):
-        ring = jnp.stack([own] + [permute(own, lambda *at, k=k: shift_y(at, -k)) for k in (1, 2, 3)])
+        p, m = from_y(own, 1), from_y(own, -1)
+        far_one = jnp.concatenate([from_y(p[:4], 1), from_y(m[4:], -1)])
+        ring = jnp.stack([own, p, far_one, m])
         return ring, permute(ring, other_core)
 
     amps, cols = round_y(own_t), round_y(own_c)
@@ -256,9 +290,8 @@
     p, m = from_plus(s), from_minus(s)
     rows = (s, p, m, from_plus(p[:2]), from_minus(m[2:]))
 
-    r2a, r2b, *halves = second(place, rows, amps, cols)
-    r1a, r1b, r3a, r3b = third((1, 3), place, halves)
-    r0a, r0b = third((0,), place, halves)
+    t_hi, t_lo, c_hi, c_lo = halves(place, amps, cols)
+    r2a, r2b, r1a, r1b, r3a, r3b, a_hi, a_lo = second(place, rows, (t_hi, t_lo, c_hi, c_lo))
 
     def to_plus(value):
         return permute(value, lambda *at: far(at, 1))
@@ -268,6 +301,7 @@
 
     a0, a1 = to_plus(r2a), to_minus(r2b)
     b1, d0 = to_plus(r1b), to_minus(r3a)
+    r0a, r0b = third(place, (a_hi, a_lo, c_hi, c_lo), (b1, d0))
     b0, d1 = to_plus(r1a + a0), to_minus(r3b + a1)
     q = (r0a + b0 + d0, r0b + b1 + d1)
     got = [permute(q[u // 2][u % 2], lambda *at, u=u: near(at, u)) for u in (1, 2, 3)]

time: 227 us -> 211 us (0.930)
  the two profiles are of different devices: /device:TPU:14 before, /device:TPU:1 now
where the time goes in v3:
time: 211 us; the launch traced here: 210 us
  waiting for transfers between devices  78.9 us (37%)
  starting transfers between devices  60.8 us (29%)
  Pallas kernels  50.1 us (24%)
  local copies, waits for them, and re-layouts  13 us (6%)
  other arithmetic  6.58 us (3%)
    ppermute x29, waiting for transfers between devices, permute(): return lax.ppermute(value, AXES, pairs)  77 us
    ppermute x29, starting transfers between devices, permute(): return lax.ppermute(value, AXES, pairs)  55 us
    pallas_call x3, Pallas kernels, call(): pl.pallas_call(body, out_shape=out_shape, in_specs=[ON_SMEM] + [ANYWHERE]...  48.8 us
    unnamed x31, local copies, waits for them, and re-layouts  10.4 us
    all_to_all x1, starting transfers between devices, body(): own_c = lax.all_to_all(columns, ('xl', 'z'), 0, 0, tiled=True)  5.8 us
  transfers between devices with their start and end apart: 30, of which 17 were waited for; matrix products, arithmetic and copies ran while one was open for 4% of the time, Pallas kernels for 5%

profile of v3, /device:TPU:1, one launch (start us, length us, event | category | flops | bytes accessed | tf_op | source)
XLA Modules:
  0.0 209.7 jit_solution(1170700834476492901)
XLA Ops:
  0.0 4.9 %collective-permute-start = (f32[8,48,384]{2,1,0:T(8,128)}, f32[8,48,384]{2,1,0:T(8,128)S(1)}, u32[]{:S(2)}, u32[]{:S(2)}) collective-permute-start(f32[8,48,384]{2,1,0:T(8,128)} %l_ref.1), channel_id=1, source_target_pairs={{0,0},{1,4},{2,2},{3,6},{4,1},{5,5},{6,3},{7,7},{8,8},{9,12},{10,1... | collective-permute-start | bytes 1769480 | tf_op jit(solution)/shard_map/ppermute | solution.py:33
  4.9 1.7 collective-permute-start.8
  6.7 6.0 %collective-permute-done = f32[8,48,384]{2,1,0:T(8,128)S(1)} collective-permute-done((f32[8,48,384]{2,1,0:T(8,128)}, f32[8,48,384]{2,1,0:T(8,128)S(1)}, u32[]{:S(2)}, u32[]{:S(2)}) %collective-permute-start) | collective-permute-done | bytes 589856 | tf_op jit(solution)/shard_map/ppermute | solution.py:33
  16.3 5.8 %all-to-all-start = ((f32[8,48,384]{2,1,0:T(8,128)}), f32[8,48,384]{2,1,0:T(8,128)S(1)}, u32[]{:S(2)}, u32[]{:S(2)}) async-start(f32[8,48,384]{2,1,0:T(8,128)} %shard_map.28), calls=%async_computation | async-start | bytes 1179648 | tf_op jit(solution)/shard_map/all_to_all | solution.py:276
  23.6 2.3 %collective-permute-start.1 = (f32[8,48,384]{2,1,0:T(8,128)S(1)}, f32[8,48,384]{2,1,0:T(8,128)}, u32[]{:S(2)}, u32[]{:S(2)}) collective-permute-start(f32[8,48,384]{2,1,0:T(8,128)S(1)} %collective-permute-done), channel_id=1, source_target_pairs={{0,12},{1,19},{2,14},{3,17},{4,0},{5,23},{6,2},{7,21},{8,4},{9,27}... | collective-permute-start | bytes 1769480 | tf_op jit(solution)/shard_map/ppermute | solution.py:33
  28.6 1.9 all-to-all-done
  32.0 12.1 %collective-permute-done.2 = f32[8,48,384]{2,1,0:T(8,128)} collective-permute-done((f32[8,48,384]{2,1,0:T(8,128)S(1)}, f32[8,48,384]{2,1,0:T(8,128)}, u32[]{:S(2)}, u32[]{:S(2)}) %collective-permute-start.2) | collective-permute-done | bytes 589856 | tf_op jit(solution)/shard_map/ppermute | solution.py:33
  50.0 2.9 %collective-permute-done.16 = f32[8,48,384]{2,1,0:T(8,128)S(1)} collective-permute-done((f32[8,48,384]{2,1,0:T(8,128)S(1)}, f32[8,48,384]{2,1,0:T(8,128)S(1)}, u32[]{:S(2)}, u32[]{:S(2)}) %collective-permute-start.16) | collective-permute-done | bytes 589856 | tf_op jit(solution)/shard_map/ppermute | solution.py:33
  53.8 1.9 collective-permute-done.14
  56.8 2.4 %collective-permute-done.12 = f32[4,48,384]{2,1,0:T(8,128)S(1)} collective-permute-done((f32[4,48,384]{2,1,0:T(8,128)S(1)}, f32[4,48,384]{2,1,0:T(8,128)S(1)}, u32[]{:S(2)}, u32[]{:S(2)}) %collective-permute-start.12) | collective-permute-done | bytes 294944 | tf_op jit(solution)/shard_map/ppermute | solution.py:33
  61.5 6.7 %collective-permute-start.13 = (f32[4,8,48,384]{3,2,1,0:T(8,128)S(1)}, f32[4,8,48,384]{3,2,1,0:T(8,128)}, u32[]{:S(2)}, u32[]{:S(2)}) collective-permute-start(f32[4,8,48,384]{3,2,1,0:T(8,128)S(1)} %pad_maximum_fusion.1.refs_0_), channel_id=1, source_target_pairs={{0,1},{1,0},{2,3},{3,2},{4,5},{5,4},{6,7},{7,6},{8,9},{9,8},{10,11... | collective-permute-start | bytes 7077896 | tf_op jit(solution)/shard_map/ppermute | solution.py:33
  68.3 1.6 pad_maximum_fusion.2.refs_2_
  69.8 2.6 %collective-permute-start.18 = (f32[4,8,48,384]{3,2,1,0:T(8,128)}, f32[4,8,48,384]{3,2,1,0:T(8,128)}, u32[]{:S(2)}, u32[]{:S(2)}) collective-permute-start(f32[4,8,48,384]{3,2,1,0:T(8,128)} %pad_maximum_fusion.2.refs_2_), channel_id=1, source_target_pairs={{0,1},{1,0},{2,3},{3,2},{4,5},{5,4},{6,7},{7,6},{8,9},{9,8},{10,11... | collective-permute-start | bytes 7077896 | tf_op jit(solution)/shard_map/ppermute | solution.py:33
  72.5 2.4 %collective-permute-done.5.refs_2_ = f32[4,8,48,384]{3,2,1,0:T(8,128)S(1)} collective-permute-done((f32[4,8,48,384]{3,2,1,0:T(8,128)S(1)}, f32[4,8,48,384]{3,2,1,0:T(8,128)S(1)}, u32[]{:S(2)}, u32[]{:S(2)}) %collective-permute-start.5) | collective-permute-done | bytes 2359328 | tf_op jit(solution)/shard_map/ppermute | solution.py:33
  78.4 2.7 %collective-permute-start.6 = (f32[2,8,48,384]{3,2,1,0:T(8,128)}, f32[2,8,48,384]{3,2,1,0:T(8,128)}, u32[]{:S(2)}, u32[]{:S(2)}) collective-permute-start(f32[2,8,48,384]{3,2,1,0:T(8,128)} %slice.40), channel_id=1, source_target_pairs={{0,18},{1,13},{2,16},{3,15},{4,22},{5,1},{6,20},{7,3},{8,26},{9,5}... | collective-permute-start | bytes 3538952 | tf_op jit(solution)/shard_map/ppermute | solution.py:33
  81.2 5.0 %shard_map.29 = (bf16[768,1536]{1,0:T(8,128)(2,1)S(1)}, bf16[768,1536]{1,0:T(8,128)(2,1)S(1)}, bf16[4,384,768]{2,1,0:T(8,128)(2,1)S(1)}, bf16[4,384,768]{2,1,0:T(8,128)(2,1)S(1)}) custom-call(s32[4]{0:T(128)S(1)} %pad_add_fusion.place, f32[4,8,48,384]{3,2,1,0:T(8,128)S(1)} %pad_maximum_fusion.1.refs_0_, f32[4,8,48,384]{3,2,1,0:T(8,128)} %collective-permute-done.13.refs_1_, ...), custom_call_target="tpu_custom_call" | custom-call | flops 2717908992 | bytes 12582912 | tf_op jit(solution)/shard_map/pallas_call | solution.py:222
  91.8 1.7 collective-permute-done.7.refs_4_
  94.7 39.5 %shard_map.30 = (f32[2,8,48,384]{3,2,1,0:T(8,128)S(1)}, f32[2,8,48,384]{3,2,1,0:T(8,128)S(1)}, f32[2,8,48,384]{3,2,1,0:T(8,128)S(1)}, f32[2,8,48,384]{3,2,1,0:T(...) custom-call(s32[4]{0:T(128)S(1)} %pad_add_fusion.place, ...), custom_call_target="tpu_custom_call" | custom-call | flops 19025362944 | bytes 12582912 | tf_op jit(solution)/shard_map/pallas_call | solution.py:222
  135.7 1.6 collective-permute-start.24
  137.3 2.7 %collective-permute-start.20 = (f32[2,8,48,384]{3,2,1,0:T(8,128)S(1)}, f32[2,8,48,384]{3,2,1,0:T(8,128)S(1)}, u32[]{:S(2)}, u32[]{:S(2)}) collective-permute-start(f32[2,8,48,384]{3,2,1,0:T(8,128)S(1)} %get-tuple-element.28), channel_id=1, source_target_pairs={{0,18},{1,13},{2,16},{3,15},{4,22},{5,1},{6,20},{7,3},{8,26},{9,5}... | collective-permute-start | bytes 3538952 | tf_op jit(solution)/shard_map/ppermute | solution.py:33
  140.0 11.1 %collective-permute-done.21 = f32[2,8,48,384]{3,2,1,0:T(8,128)S(1)} collective-permute-done((f32[2,8,48,384]{3,2,1,0:T(8,128)S(1)}, f32[2,8,48,384]{3,2,1,0:T(8,128)S(1)}, u32[]{:S(2)}, u32[]{:S(2)}) %collective-permute-start.21) | collective-permute-done | bytes 1179680 | tf_op jit(solution)/shard_map/ppermute | solution.py:33
  152.9 3.0 %collective-permute-start.25 = (f32[2,8,48,384]{3,2,1,0:T(8,128)S(1)}, f32[2,8,48,384]{3,2,1,0:T(8,128)S(1)}, u32[]{:S(2)}, u32[]{:S(2)}) collective-permute-start(f32[2,8,48,384]{3,2,1,0:T(8,128)S(1)} %add.36), channel_id=1, source_target_pairs={{0,18},{1,13},{2,16},{3,15},{4,22},{5,1},{6,20},{7,3},{8,26},{9,5}... | collective-permute-start | bytes 3538952 | tf_op jit(solution)/shard_map/ppermute | solution.py:33
  155.9 7.9 %collective-permute-done.19.b1 = f32[2,8,48,384]{3,2,1,0:T(8,128)S(1)} collective-permute-done((f32[2,8,48,384]{3,2,1,0:T(8,128)S(1)}, f32[2,8,48,384]{3,2,1,0:T(8,128)S(1)}, u32[]{:S(2)}, u32[]{:S(2)}) %collective-permute-start.19) | collective-permute-done | bytes 1179680 | tf_op jit(solution)/shard_map/ppermute | solution.py:33
  163.8 1.7 copy-done.5
  165.5 4.3 %shard_map.31 = (f32[2,8,48,384]{3,2,1,0:T(8,128)S(1)}, f32[2,8,48,384]{3,2,1,0:T(8,128)S(1)}) custom-call(s32[4]{0:T(128)S(1)} %pad_add_fusion.place, bf16[4,384,768]{2,1,0:T(8,128)(2,1)S(1)} %copy-done.4, bf16[4,384,768]{2,1,0:T(8,128)(2,1)S(1)} %copy-done.5, bf16[4,384,768]{2,1,0:T(8,128)(2,1)S(1)} %copy-done.1, bf16[4,384,768]{2,1,0:T(8,128)(2,1)S(1)} %copy-done.3, ...), custom_call_target="tpu_custom_call" | custom-call | flops 2717908992 | bytes 12582912 | tf_op jit(solution)/shard_map/pallas_call | solution.py:222
  169.8 6.6 %collective-permute-done.22 = f32[2,8,48,384]{3,2,1,0:T(8,128)S(1)} collective-permute-done((f32[2,8,48,384]{3,2,1,0:T(8,128)S(1)}, f32[2,8,48,384]{3,2,1,0:T(8,128)S(1)}, u32[]{:S(2)}, u32[]{:S(2)}) %collective-permute-start.22) | collective-permute-done | bytes 1179680 | tf_op jit(solution)/shard_map/ppermute | solution.py:33
  177.0 2.7 %collective-permute-start.27 = (f32[8,48,384]{2,1,0:T(8,128)S(1)}, f32[8,48,384]{2,1,0:T(8,128)S(1)}, u32[]{:S(2)}, u32[]{:S(2)}) collective-permute-start(f32[8,48,384]{2,1,0:T(8,128)S(1)} %get-tuple-element.35), channel_id=1, source_target_pairs={{0,12},{1,19},{2,14},{3,17},{4,0},{5,23},{6,2},{7,21},{8,4},{9,27}... | collective-permute-start | bytes 1769480 | tf_op jit(solution)/shard_map/ppermute | solution.py:33
  179.7 2.0 collective-permute-start.26
  181.7 5.2 %collective-permute-done.23 = f32[8,48,384]{2,1,0:T(8,128)S(1)} collective-permute-done((f32[8,48,384]{2,1,0:T(8,128)S(1)}, f32[8,48,384]{2,1,0:T(8,128)S(1)}, u32[]{:S(2)}, u32[]{:S(2)}) %collective-permute-start.23) | collective-permute-done | bytes 589856 | tf_op jit(solution)/shard_map/ppermute | solution.py:33
  187.5 6.3 %collective-permute-done.26 = f32[8,48,384]{2,1,0:T(8,128)S(1)} collective-permute-done((f32[8,48,384]{2,1,0:T(8,128)S(1)}, f32[8,48,384]{2,1,0:T(8,128)S(1)}, u32[]{:S(2)}, u32[]{:S(2)}) %collective-permute-start.26) | collective-permute-done | bytes 589856 | tf_op jit(solution)/shard_map/ppermute | solution.py:33
  193.9 7.3 %collective-permute-start.28 = (f32[8,48,384]{2,1,0:T(8,128)S(1)}, f32[8,48,384]{2,1,0:T(8,128)S(1)}, u32[]{:S(2)}, u32[]{:S(2)}) collective-permute-start(f32[8,48,384]{2,1,0:T(8,128)S(1)} %fusion.1), channel_id=1, source_target_pairs={{0,0},{1,4},{2,2},{3,6},{4,1},{5,5},{6,3},{7,7},{8,8},{9,12},{10,1... | collective-permute-start | bytes 1769480 | tf_op jit(solution)/shard_map/ppermute | solution.py:33
  201.3 7.6 %collective-permute-done.28 = f32[8,48,384]{2,1,0:T(8,128)S(1)} collective-permute-done((f32[8,48,384]{2,1,0:T(8,128)S(1)}, f32[8,48,384]{2,1,0:T(8,128)S(1)}, u32[]{:S(2)}, u32[]{:S(2)}) %collective-permute-start.28) | collective-permute-done | bytes 589856 | tf_op jit(solution)/shard_map/ppermute | solution.py:33
  (82 shorter events, 35.2 us)
Async XLA Ops:
  0.0 12.7 %collective-permute-start = (f32[8,48,384]{2,1,0:T(8,128)}, f32[8,48,384]{2,1,0:T(8,128)S(1)}, u32[]{:S(2)}, u32[]{:S(2)}) collective-permute-start(f32[8,48,384]{2,1,0:T(8,128)} %l_ref.1), channel_id=1, source_target_pairs={{0,0},{1,4},{2,2},{3,6},{4,1},{5,5},{6,3},{7,7},{8,8},{9,12},{10,1... | collective-permute-start | bytes 1769480 | tf_op jit(solution)/shard_map/ppermute | solution.py:33
  4.9 21.0 %collective-permute-start.8 = (f32[8,48,384]{2,1,0:T(8,128)}, f32[8,48,384]{2,1,0:T(8,128)S(1)}, u32[]{:S(2)}, u32[]{:S(2)}) collective-permute-start(f32[8,48,384]{2,1,0:T(8,128)} %param.3), channel_id=1, source_target_pairs={{0,0},{1,1},{2,64},{3,65},{4,4},{5,5},{6,68},{7,69},{8,8},{9,9},{1... | collective-permute-start | bytes 1769480 | tf_op jit(solution)/shard_map/ppermute | solution.py:33
  12.7 18.9 %collective-permute-start.3 = (f32[8,48,384]{2,1,0:T(8,128)S(1)}, f32[8,48,384]{2,1,0:T(8,128)S(1)}, u32[]{:S(2)}, u32[]{:S(2)}) collective-permute-start(f32[8,48,384]{2,1,0:T(8,128)S(1)} %collective-permute-done), channel_id=1, source_target_pairs={{0,4},{1,17},{2,6},{3,19},{4,8},{5,21},{6,10},{7,23},{8,12},{9,25}... | collective-permute-start | bytes 1769480 | tf_op jit(solution)/shard_map/ppermute | solution.py:33
  16.3 14.2 %all-to-all-start = ((f32[8,48,384]{2,1,0:T(8,128)}), f32[8,48,384]{2,1,0:T(8,128)S(1)}, u32[]{:S(2)}, u32[]{:S(2)}) async-start(f32[8,48,384]{2,1,0:T(8,128)} %shard_map.28), calls=%async_computation | async-start | bytes 1179648 | tf_op jit(solution)/shard_map/all_to_all | solution.py:276
  22.1 22.0 %collective-permute-start.2 = (f32[8,48,384]{2,1,0:T(8,128)S(1)}, f32[8,48,384]{2,1,0:T(8,128)}, u32[]{:S(2)}, u32[]{:S(2)}) collective-permute-start(f32[8,48,384]{2,1,0:T(8,128)S(1)} %collective-permute-done), channel_id=1, source_target_pairs={{0,8},{1,3},{2,10},{3,1},{4,12},{5,7},{6,14},{7,5},{8,0},{9,11},{1... | collective-permute-start | bytes 1769480 | tf_op jit(solution)/shard_map/ppermute | solution.py:33
  23.6 20.5 %collective-permute-start.1 = (f32[8,48,384]{2,1,0:T(8,128)S(1)}, f32[8,48,384]{2,1,0:T(8,128)}, u32[]{:S(2)}, u32[]{:S(2)}) collective-permute-start(f32[8,48,384]{2,1,0:T(8,128)S(1)} %collective-permute-done), channel_id=1, source_target_pairs={{0,12},{1,19},{2,14},{3,17},{4,0},{5,23},{6,2},{7,21},{8,4},{9,27}... | collective-permute-start | bytes 1769480 | tf_op jit(solution)/shard_map/ppermute | solution.py:33
  26.0 19.6 %copy-start.11 = (f32[8,48,384]{2,1,0:T(8,128)}, f32[8,48,384]{2,1,0:T(8,128)S(1)}, u32[]{:S(2)}) copy-start(f32[8,48,384]{2,1,0:T(8,128)S(1)} %collective-permute-done.8) | copy-start | bytes 1769476
  26.0 20.9 %collective-permute-start.11 = (f32[8,48,384]{2,1,0:T(8,128)S(1)}, f32[8,48,384]{2,1,0:T(8,128)S(1)}, u32[]{:S(2)}, u32[]{:S(2)}) collective-permute-start(f32[8,48,384]{2,1,0:T(8,128)S(1)} %collective-permute-done.8), channel_id=1, source_target_pairs={{0,32},{1,33},{2,34},{3,35},{4,36},{5,37},{6,38},{7,39},{8,40},{9,... | collective-permute-start | bytes 1769480 | tf_op jit(solution)/shard_map/ppermute | solution.py:33
  27.3 21.1 %collective-permute-start.9 = (f32[8,48,384]{2,1,0:T(8,128)S(1)}, f32[8,48,384]{2,1,0:T(8,128)S(1)}, u32[]{:S(2)}, u32[]{:S(2)}) collective-permute-start(f32[8,48,384]{2,1,0:T(8,128)S(1)} %collective-permute-done.8), channel_id=1, source_target_pairs={{0,96},{1,97},{2,98},{3,99},{4,100},{5,101},{6,102},{7,103},{8,104... | collective-permute-start | bytes 1769480 | tf_op jit(solution)/shard_map/ppermute | solution.py:33
  31.6 21.3 %collective-permute-start.16 = (f32[8,48,384]{2,1,0:T(8,128)S(1)}, f32[8,48,384]{2,1,0:T(8,128)S(1)}, u32[]{:S(2)}, u32[]{:S(2)}) collective-permute-start(f32[8,48,384]{2,1,0:T(8,128)S(1)} %all-to-all-done), channel_id=1, source_target_pairs={{0,32},{1,33},{2,34},{3,35},{4,36},{5,37},{6,38},{7,39},{8,40},{9,... | collective-permute-start | bytes 1769480 | tf_op jit(solution)/shard_map/ppermute | solution.py:33
  44.1 11.7 %collective-permute-start.14 = (f32[8,48,384]{2,1,0:T(8,128)S(1)}, f32[8,48,384]{2,1,0:T(8,128)S(1)}, u32[]{:S(2)}, u32[]{:S(2)}) collective-permute-start(f32[8,48,384]{2,1,0:T(8,128)S(1)} %all-to-all-done), channel_id=1, source_target_pairs={{0,96},{1,97},{2,98},{3,99},{4,100},{5,101},{6,102},{7,103},{8,104... | collective-permute-start | bytes 1769480 | tf_op jit(solution)/shard_map/ppermute | solution.py:33
  45.6 15.9 %copy-start.9 = (f32[4,8,48,384]{3,2,1,0:T(8,128)}, f32[4,8,48,384]{3,2,1,0:T(8,128)S(1)}, u32[]{:S(2)}) copy-start(f32[4,8,48,384]{3,2,1,0:T(8,128)S(1)} %pad_maximum_fusion.refs_0_) | copy-start | bytes 7077892
  45.6 29.3 %collective-permute-start.5 = (f32[4,8,48,384]{3,2,1,0:T(8,128)S(1)}, f32[4,8,48,384]{3,2,1,0:T(8,128)S(1)}, u32[]{:S(2)}, u32[]{:S(2)}) collective-permute-start(f32[4,8,48,384]{3,2,1,0:T(8,128)S(1)} %pad_maximum_fusion.refs_0_), channel_id=1, source_target_pairs={{0,16},{1,5},{2,18},{3,7},{4,20},{5,9},{6,22},{7,11},{8,24},{9,13}... | collective-permute-start | bytes 7077896 | tf_op jit(solution)/shard_map/ppermute | solution.py:33
  46.9 29.8 %collective-permute-start.4 = (f32[4,8,48,384]{3,2,1,0:T(8,128)S(1)}, f32[4,8,48,384]{3,2,1,0:T(8,128)S(1)}, u32[]{:S(2)}, u32[]{:S(2)}) collective-permute-start(f32[4,8,48,384]{3,2,1,0:T(8,128)S(1)} %pad_maximum_fusion.refs_0_), channel_id=1, source_target_pairs={{0,18},{1,13},{2,16},{3,15},{4,22},{5,1},{6,20},{7,3},{8,26},{9,5}... | collective-permute-start | bytes 7077896 | tf_op jit(solution)/shard_map/ppermute | solution.py:33
  48.4 10.8 %collective-permute-start.12 = (f32[4,48,384]{2,1,0:T(8,128)S(1)}, f32[4,48,384]{2,1,0:T(8,128)S(1)}, u32[]{:S(2)}, u32[]{:S(2)}) collective-permute-start(f32[4,48,384]{2,1,0:T(8,128)S(1)} %slice.43), channel_id=1, source_target_pairs={{0,32},{1,33},{2,34},{3,35},{4,36},{5,37},{6,38},{7,39},{8,40},{9,... | collective-permute-start | bytes 884744 | tf_op jit(solution)/shard_map/ppermute | solution.py:33
  52.9 7.3 %collective-permute-start.10 = (f32[4,48,384]{2,1,0:T(8,128)S(1)}, f32[4,48,384]{2,1,0:T(8,128)S(1)}, u32[]{:S(2)}, u32[]{:S(2)}) collective-permute-start(f32[4,48,384]{2,1,0:T(8,128)S(1)} %slice.42), channel_id=1, source_target_pairs={{0,96},{1,97},{2,98},{3,99},{4,100},{5,101},{6,102},{7,103},{8,104... | collective-permute-start | bytes 884744 | tf_op jit(solution)/shard_map/ppermute | solution.py:33
  55.8 12.4 %collective-permute-start.17 = (f32[4,48,384]{2,1,0:T(8,128)S(1)}, f32[4,48,384]{2,1,0:T(8,128)S(1)}, u32[]{:S(2)}, u32[]{:S(2)}) collective-permute-start(f32[4,48,384]{2,1,0:T(8,128)S(1)} %slice.45), channel_id=1, source_target_pairs={{0,32},{1,33},{2,34},{3,35},{4,36},{5,37},{6,38},{7,39},{8,40},{9,... | collective-permute-start | bytes 884744 | tf_op jit(solution)/shard_map/ppermute | solution.py:33
  59.2 9.0 %collective-permute-start.15 = (f32[4,48,384]{2,1,0:T(8,128)S(1)}, f32[4,48,384]{2,1,0:T(8,128)S(1)}, u32[]{:S(2)}, u32[]{:S(2)}) collective-permute-start(f32[4,48,384]{2,1,0:T(8,128)S(1)} %slice.44), channel_id=1, source_target_pairs={{0,96},{1,97},{2,98},{3,99},{4,100},{5,101},{6,102},{7,103},{8,104... | collective-permute-start | bytes 884744 | tf_op jit(solution)/shard_map/ppermute | solution.py:33
  61.5 19.7 %collective-permute-start.13 = (f32[4,8,48,384]{3,2,1,0:T(8,128)S(1)}, f32[4,8,48,384]{3,2,1,0:T(8,128)}, u32[]{:S(2)}, u32[]{:S(2)}) collective-permute-start(f32[4,8,48,384]{3,2,1,0:T(8,128)S(1)} %pad_maximum_fusion.1.refs_0_), channel_id=1, source_target_pairs={{0,1},{1,0},{2,3},{3,2},{4,5},{5,4},{6,7},{7,6},{8,9},{9,8},{10,11... | collective-permute-start | bytes 7077896 | tf_op jit(solution)/shard_map/ppermute | solution.py:33
  69.8 11.3 %collective-permute-start.18 = (f32[4,8,48,384]{3,2,1,0:T(8,128)}, f32[4,8,48,384]{3,2,1,0:T(8,128)}, u32[]{:S(2)}, u32[]{:S(2)}) collective-permute-start(f32[4,8,48,384]{3,2,1,0:T(8,128)} %pad_maximum_fusion.2.refs_2_), channel_id=1, source_target_pairs={{0,1},{1,0},{2,3},{3,2},{4,5},{5,4},{6,7},{7,6},{8,9},{9,8},{10,11... | collective-permute-start | bytes 7077896 | tf_op jit(solution)/shard_map/ppermute | solution.py:33
  76.6 16.9 %collective-permute-start.7 = (f32[2,8,48,384]{3,2,1,0:T(8,128)}, f32[2,8,48,384]{3,2,1,0:T(8,128)}, u32[]{:S(2)}, u32[]{:S(2)}) collective-permute-start(f32[2,8,48,384]{3,2,1,0:T(8,128)} %slice.41), channel_id=1, source_target_pairs={{0,16},{1,5},{2,18},{3,7},{4,20},{5,9},{6,22},{7,11},{8,24},{9,13}... | collective-permute-start | bytes 3538952 | tf_op jit(solution)/shard_map/ppermute | solution.py:33
  78.4 16.2 %collective-permute-start.6 = (f32[2,8,48,384]{3,2,1,0:T(8,128)}, f32[2,8,48,384]{3,2,1,0:T(8,128)}, u32[]{:S(2)}, u32[]{:S(2)}) collective-permute-start(f32[2,8,48,384]{3,2,1,0:T(8,128)} %slice.40), channel_id=1, source_target_pairs={{0,18},{1,13},{2,16},{3,15},{4,22},{5,1},{6,20},{7,3},{8,26},{9,5}... | collective-permute-start | bytes 3538952 | tf_op jit(solution)/shard_map/ppermute | solution.py:33
  134.2 17.0 %collective-permute-start.21 = (f32[2,8,48,384]{3,2,1,0:T(8,128)S(1)}, f32[2,8,48,384]{3,2,1,0:T(8,128)S(1)}, u32[]{:S(2)}, u32[]{:S(2)}) collective-permute-start(f32[2,8,48,384]{3,2,1,0:T(8,128)S(1)} %get-tuple-element.31), channel_id=1, source_target_pairs={{0,16},{1,5},{2,18},{3,7},{4,20},{5,9},{6,22},{7,11},{8,24},{9,13}... | collective-permute-start | bytes 3538952 | tf_op jit(solution)/shard_map/ppermute | solution.py:33
  135.7 15.7 %collective-permute-start.24 = (f32[2,8,48,384]{3,2,1,0:T(8,128)S(1)}, f32[2,8,48,384]{3,2,1,0:T(8,128)S(1)}, u32[]{:S(2)}, u32[]{:S(2)}) collective-permute-start(f32[2,8,48,384]{3,2,1,0:T(8,128)S(1)} %get-tuple-element.34), channel_id=1, source_target_pairs={{0,18},{1,13},{2,16},{3,15},{4,22},{5,1},{6,20},{7,3},{8,26},{9,5}... | collective-permute-start | bytes 3538952 | tf_op jit(solution)/shard_map/ppermute | solution.py:33
  137.3 26.4 %collective-permute-start.19 = (f32[2,8,48,384]{3,2,1,0:T(8,128)S(1)}, f32[2,8,48,384]{3,2,1,0:T(8,128)S(1)}, u32[]{:S(2)}, u32[]{:S(2)}) collective-permute-start(f32[2,8,48,384]{3,2,1,0:T(8,128)S(1)} %get-tuple-element.27), channel_id=1, source_target_pairs={{0,16},{1,5},{2,18},{3,7},{4,20},{5,9},{6,22},{7,11},{8,24},{9,13}... | collective-permute-start | bytes 3538952 | tf_op jit(solution)/shard_map/ppermute | solution.py:33
  137.3 26.4 %collective-permute-start.20 = (f32[2,8,48,384]{3,2,1,0:T(8,128)S(1)}, f32[2,8,48,384]{3,2,1,0:T(8,128)S(1)}, u32[]{:S(2)}, u32[]{:S(2)}) collective-permute-start(f32[2,8,48,384]{3,2,1,0:T(8,128)S(1)} %get-tuple-element.28), channel_id=1, source_target_pairs={{0,18},{1,13},{2,16},{3,15},{4,22},{5,1},{6,20},{7,3},{8,26},{9,5}... | collective-permute-start | bytes 3538952 | tf_op jit(solution)/shard_map/ppermute | solution.py:33
  151.3 25.1 %collective-permute-start.22 = (f32[2,8,48,384]{3,2,1,0:T(8,128)S(1)}, f32[2,8,48,384]{3,2,1,0:T(8,128)S(1)}, u32[]{:S(2)}, u32[]{:S(2)}) collective-permute-start(f32[2,8,48,384]{3,2,1,0:T(8,128)S(1)} %add.31), channel_id=1, source_target_pairs={{0,16},{1,5},{2,18},{3,7},{4,20},{5,9},{6,22},{7,11},{8,24},{9,13}... | collective-permute-start | bytes 3538952 | tf_op jit(solution)/shard_map/ppermute | solution.py:33
  152.9 23.8 %collective-permute-start.25 = (f32[2,8,48,384]{3,2,1,0:T(8,128)S(1)}, f32[2,8,48,384]{3,2,1,0:T(8,128)S(1)}, u32[]{:S(2)}, u32[]{:S(2)}) collective-permute-start(f32[2,8,48,384]{3,2,1,0:T(8,128)S(1)} %add.36), channel_id=1, source_target_pairs={{0,18},{1,13},{2,16},{3,15},{4,22},{5,1},{6,20},{7,3},{8,26},{9,5}... | collective-permute-start | bytes 3538952 | tf_op jit(solution)/shard_map/ppermute | solution.py:33
  176.6 10.3 %collective-permute-start.23 = (f32[8,48,384]{2,1,0:T(8,128)S(1)}, f32[8,48,384]{2,1,0:T(8,128)S(1)}, u32[]{:S(2)}, u32[]{:S(2)}) collective-permute-start(f32[8,48,384]{2,1,0:T(8,128)S(1)} %slice_bitcast_fusion.2), channel_id=1, source_target_pairs={{0,4},{1,17},{2,6},{3,19},{4,8},{5,21},{6,10},{7,23},{8,12},{9,25}... | collective-permute-start | bytes 1769480 | tf_op jit(solution)/shard_map/ppermute | solution.py:33
  177.0 10.5 %collective-permute-start.27 = (f32[8,48,384]{2,1,0:T(8,128)S(1)}, f32[8,48,384]{2,1,0:T(8,128)S(1)}, u32[]{:S(2)}, u32[]{:S(2)}) collective-permute-start(f32[8,48,384]{2,1,0:T(8,128)S(1)} %get-tuple-element.35), channel_id=1, source_target_pairs={{0,12},{1,19},{2,14},{3,17},{4,0},{5,23},{6,2},{7,21},{8,4},{9,27}... | collective-permute-start | bytes 1769480 | tf_op jit(solution)/shard_map/ppermute | solution.py:33
  179.7 14.1 %collective-permute-start.26 = (f32[8,48,384]{2,1,0:T(8,128)S(1)}, f32[8,48,384]{2,1,0:T(8,128)S(1)}, u32[]{:S(2)}, u32[]{:S(2)}) collective-permute-start(f32[8,48,384]{2,1,0:T(8,128)S(1)} %get-tuple-element.36), channel_id=1, source_target_pairs={{0,8},{1,3},{2,10},{3,1},{4,12},{5,7},{6,14},{7,5},{8,0},{9,11},{1... | collective-permute-start | bytes 1769480 | tf_op jit(solution)/shard_map/ppermute | solution.py:33
  193.9 14.9 %collective-permute-start.28 = (f32[8,48,384]{2,1,0:T(8,128)S(1)}, f32[8,48,384]{2,1,0:T(8,128)S(1)}, u32[]{:S(2)}, u32[]{:S(2)}) collective-permute-start(f32[8,48,384]{2,1,0:T(8,128)S(1)} %fusion.1), channel_id=1, source_target_pairs={{0,0},{1,4},{2,2},{3,6},{4,1},{5,5},{6,3},{7,7},{8,8},{9,12},{10,1... | collective-permute-start | bytes 1769480 | tf_op jit(solution)/shard_map/ppermute | solution.py:33
  (13 other events, 71.7 us)

commit v4 on v3

--- a/solution.py
+++ b/solution.py
@@ -71,11 +71,12 @@
     return high, (value - high.astype(F32)).astype(BF16)
 
 
+def times(a, b):
+    return lax.dot_general(a, b, (((1,), (1,)), ((), ())), preferred_element_type=F32)
+
+
 def dot3(a, b):
-    def one(p, q):
-        return lax.dot_general(p, q, (((1,), (1,)), ((), ())), preferred_element_type=F32)
-
-    return one(a[0], b[0]) + (one(a[0], b[1]) + one(a[1], b[0]))
+    return times(a[0], b[0]) + (times(a[0], b[1]) + times(a[1], b[0]))
 
 
 def offset(value, size):
@@ -94,7 +95,8 @@
     return copies
 
 
-def shuffle_kernel(l_ref, out):
+def shuffle_kernel(l_ref, after, out):
+    del after
     for m in range(8):
         out[m] = jnp.concatenate([l_ref[p][:, m * 48 : m * 48 + 48] for p in range(8)], axis=1)
 
@@ -109,29 +111,21 @@
         copy.wait()
 
 
-def ladder_of(place, v, a_hi, a_lo, c_hi, c_lo, near_ones, far_ones):
+def ladder_of(place, v, a_wide, c_wide, out):
     z, x, c = place[1], place[2], place[3]
     at_z, at_x = lax.rem(z + v, 4), lax.rem(x + v, 4)
-    bs = [jnp.where(c == 0, lax.rem(at_x, 2) * 2 + k, at_z // 2 + 2 * k) for k in range(2)]
-    cs = [jnp.where(c == 0, at_x // 2 * 2 + k, lax.rem(at_z, 2) + 2 * k) for k in range(2)]
-    left = [jnp.concatenate([ref[b] for b in bs]) for ref in (a_hi, a_lo)]
-    right = [jnp.concatenate([ref[b] for b in cs]) for ref in (c_hi, c_lo)]
-    r = dot3(left, right)
+    columns = [jnp.where(c == 0, at_x // 2 * 2 + j, lax.rem(at_z, 2) + 2 * j) for j in range(2)]
     for i in range(2):
+        b = jnp.where(c == 0, lax.rem(at_x, 2) * 2 + i, at_z // 2 + 2 * i)
+        r = times(a_wide[b], jnp.concatenate([c_wide[at] for at in columns]))
         for j in range(2):
-            block = r[i * 384 : i * 384 + 384, j * 384 : j * 384 + 384].reshape(8, 48, 384)
             u = lax.rem(jnp.where(c == 0, 2 * i + j - z, 2 * j + i - x) + 4, 4)
-
-            for n, ref in enumerate((near_ones, far_ones)):
-
-                @pl.when(u // 2 == n)
-                def _():
-                    ref[lax.rem(u, 2)] = block
+            out[u] = r[:, j * 384 : j * 384 + 384].reshape(8, 48, 384)
 
 
 def halves_kernel(place, *refs):
-    amps, columns, outs = refs[:2], refs[2:4], refs[4:8]
-    t_raw, l_cols, t_hi, t_lo, c_hi, c_lo, t_sem, c_sem, out_sem = refs[8:]
+    amps, columns, outs = refs[:2], refs[2:4], refs[4:7]
+    t_raw, l_cols, t_hi, t_lo, c_wide, t_sem, c_sem, out_sem = refs[7:]
     y, c = place[0], place[3]
     t_copies, c_copies = [], []
     for k in range(4):
@@ -152,24 +146,27 @@
 
     @pl.loop(0, 4)
     def _(e):
-        c_hi[e], c_lo[e] = split(l_cols[e].reshape(384, 768))
-
-    copies = [pltpu.make_async_copy(ref, out, out_sem) for ref, out in zip((t_hi, t_lo, c_hi, c_lo), outs)]
+        high, low = split(l_cols[e].reshape(384, 768))
+        for k, part in enumerate((high, high, low)):
+            c_wide[e, :, k * 768 : k * 768 + 768] = part
+
+    copies = [pltpu.make_async_copy(ref, out, out_sem) for ref, out in zip((t_hi, t_lo, c_wide), outs)]
     start(copies)
     wait(copies)
 
 
 def second_kernel(place, *refs):
-    rows, halves_in, outs = refs[:5], refs[5:9], refs[9:17]
-    l_rows, t_hi, t_lo, c_hi, c_lo, half, a_hi, a_lo = refs[17:25]
-    blocks, (t_sem, row_sem, c_sem, out_sem) = refs[25:31], refs[31:]
-    t_copies = [pltpu.make_async_copy(halves_in[k], ref, t_sem) for k, ref in enumerate((t_hi, t_lo))]
-    c_copies = [pltpu.make_async_copy(halves_in[2 + k], ref, c_sem) for k, ref in enumerate((c_hi, c_lo))]
+    rows, (t_hi_in, t_lo_in, c_in), outs = refs[:5], refs[5:8], refs[8:11]
+    l_rows, t_hi, t_lo, half, a_wide, c_wide, blocks, t_sem, row_sem, c_sem, out_sem = refs[11:]
+    t_copies = [pltpu.make_async_copy(t_hi_in, t_hi, t_sem), pltpu.make_async_copy(t_lo_in, t_lo, t_sem)]
     r_copies = [row_copies(place, rows, l_rows, pl.ds(4 * q, 4), row_sem.at[q]) for q in range(2)]
-    start(t_copies + r_copies[0] + r_copies[1] + c_copies)
-    wait(t_copies)
+    c_copies = [pltpu.make_async_copy(c_in, c_wide, c_sem)]
+    start(t_copies + r_copies[0])
+    wait(t_copies + r_copies[0])
+    start(r_copies[1] + c_copies)
     for q in range(2):
-        wait(r_copies[q])
+        if q == 1:
+            wait(r_copies[1])
         b = split(l_rows[4 * q : 4 * q + 4].reshape(768, 1536))
         for m in range(2):
             chunk = pl.ds(m * 384, 384)
@@ -182,26 +179,37 @@
     @pl.loop(0, 8)
     def _(i):
         high, low = split(half[i].T)
-        for b in range(4):
-            a_hi[b, offset(i, 48), :] = high[b * 48 : b * 48 + 48, :]
-            a_lo[b, offset(i, 48), :] = low[b * 48 : b * 48 + 48, :]
+        for k, part in enumerate((high, low, high)):
+            for b in range(4):
+                a_wide[b, offset(i, 48), k * 768 : k * 768 + 768] = part[b * 48 : b * 48 + 48, :]
 
     wait(c_copies)
-    copies = [pltpu.make_async_copy(ref, out, out_sem) for ref, out in zip((*blocks, a_hi, a_lo), outs)]
-    start(copies[6:])
-    for k, v in enumerate((2, 1, 3)):
-        ladder_of(place, v, a_hi, a_lo, c_hi, c_lo, blocks[2 * k], blocks[2 * k + 1])
+    copies = [pltpu.make_async_copy(blocks.at[pl.ds(2 * k, 2)], outs[k], out_sem) for k in range(2)]
+    copies.append(pltpu.make_async_copy(a_wide, outs[2], out_sem))
+    start(copies[2:])
+    ladder_of(place, 2, a_wide, c_wide, blocks)
+    start(copies[:2])
+    wait(copies)
+
+
+def third_kernel(place, a_in, c_in, *refs):
+    outs, (a_wide, c_wide, blocks, sem, out_sem) = refs[:4], refs[4:]
+    held = [pltpu.make_async_copy(a_in, a_wide, sem), pltpu.make_async_copy(c_in, c_wide, sem)]
+    start(held)
+    wait(held)
+    copies = [pltpu.make_async_copy(blocks.at[k // 2, pl.ds(k % 2 * 2, 2)], out, out_sem) for k, out in enumerate(outs)]
+    for k, v in enumerate((1, 3)):
+        ladder_of(place, v, a_wide, c_wide, blocks.at[k])
         start(copies[2 * k : 2 * k + 2])
     wait(copies)
 
 
-def third_kernel(place, a_hi_in, a_lo_in, c_hi_in, c_lo_in, b1, d0, out_a, out_b, a_hi, a_lo, c_hi, c_lo, sem):
+def fourth_kernel(place, a_in, c_in, b1, d0, out, a_wide, c_wide, sem):
     del b1, d0
-    pairs = ((a_hi_in, a_hi), (a_lo_in, a_lo), (c_hi_in, c_hi), (c_lo_in, c_lo))
-    copies = [pltpu.make_async_copy(ref, held, sem) for ref, held in pairs]
-    start(copies)
-    wait(copies)
-    ladder_of(place, 0, a_hi, a_lo, c_hi, c_lo, out_a, out_b)
+    held = [pltpu.make_async_copy(a_in, a_wide, sem), pltpu.make_async_copy(c_in, c_wide, sem)]
+    start(held)
+    wait(held)
+    ladder_of(place, 0, a_wide, c_wide, out)
 
 
 ANYWHERE = pl.BlockSpec(memory_space=pl.ANY)
@@ -209,9 +217,9 @@
 ON_SMEM = pl.BlockSpec(memory_space=pltpu.SMEM)
 ON_VMEM = pl.BlockSpec(memory_space=pltpu.VMEM)
 DMA = pltpu.SemaphoreType.DMA
-BLOCKS = (4, 384, 768)
+QUAD = jax.ShapeDtypeStruct((4, 8, 48, 384), F32)
 PAIR = jax.ShapeDtypeStruct((2, 8, 48, 384), F32)
-HALF = jax.ShapeDtypeStruct(BLOCKS, BF16)
+WIDE = jax.ShapeDtypeStruct((4, 384, 2304), BF16)
 
 
 AMPS = (768, 1536)
@@ -232,30 +240,35 @@
 
 def halves(place, amps, columns):
     scratch = [pltpu.VMEM((8, 96, 1536), F32), pltpu.VMEM((4, 8, 48, 768), F32)]
-    scratch += [pltpu.VMEM(AMPS, BF16)] * 2 + [pltpu.VMEM(BLOCKS, BF16)] * 2 + [DMA] * 3
-    return call(halves_kernel, [HALF_AMPS] * 2 + [HALF] * 2, ON_HBM, scratch, 24, 1, place, *amps, *columns)
+    scratch += [pltpu.VMEM(AMPS, BF16)] * 2 + [pltpu.VMEM(WIDE.shape, BF16)] + [DMA] * 3
+    return call(halves_kernel, [HALF_AMPS] * 2 + [WIDE], ON_HBM, scratch, 28, 1, place, *amps, *columns)
 
 
 def second(place, rows, parts):
-    scratch = [pltpu.VMEM((8, 192, 1536), F32)] + [pltpu.VMEM(AMPS, BF16)] * 2 + [pltpu.VMEM(BLOCKS, BF16)] * 2
-    scratch += [pltpu.VMEM((8, 768, 192), F32)] + [pltpu.VMEM(BLOCKS, BF16)] * 2 + [pltpu.VMEM(PAIR.shape, F32)] * 6
+    scratch = [pltpu.VMEM((8, 192, 1536), F32)] + [pltpu.VMEM(AMPS, BF16)] * 2 + [pltpu.VMEM((8, 768, 192), F32)]
+    scratch += [pltpu.VMEM(WIDE.shape, BF16)] * 2 + [pltpu.VMEM(QUAD.shape, F32)]
     scratch += [DMA, DMA((2,)), DMA, DMA]
-    return call(second_kernel, [PAIR] * 6 + [HALF] * 2, ON_HBM, scratch, 48, 7, place, *rows, *parts)
-
-
-def third(place, parts, after):
-    scratch = [pltpu.VMEM(BLOCKS, BF16)] * 4 + [DMA]
-    return call(third_kernel, [PAIR] * 2, ON_VMEM, scratch, 24, 1, place, *parts, *after)
-
-
-def shuffle(cholesky):
+    return call(second_kernel, [PAIR] * 2 + [WIDE], ON_HBM, scratch, 48, 5, place, *rows, *parts)
+
+
+def third(place, parts):
+    scratch = [pltpu.VMEM(WIDE.shape, BF16)] * 2 + [pltpu.VMEM((2, *QUAD.shape), F32), DMA, DMA]
+    return call(third_kernel, [PAIR] * 4, ON_HBM, scratch, 32, 2, place, *parts)
+
+
+def fourth(place, parts, after):
+    scratch = [pltpu.VMEM(WIDE.shape, BF16)] * 2 + [DMA]
+    return call(fourth_kernel, [QUAD], ON_VMEM, scratch, 28, 1, place, *parts, *after)[0]
+
+
+def shuffle(cholesky, after):
     return pl.pallas_call(
         shuffle_kernel,
         out_shape=jax.ShapeDtypeStruct((8, 48, 384), F32),
-        in_specs=[ON_VMEM],
+        in_specs=[ON_VMEM, ANYWHERE],
         out_specs=ON_VMEM,
         compiler_params=pltpu.CompilerParams(vmem_limit_bytes=8 << 20),
-    )(cholesky)
+    )(cholesky, after)
 
 
 def body(cholesky, amplitudes):
@@ -272,8 +285,7 @@
     near_rows = [mine] + [permute(mine, lambda *at, u=u: near(at, -u)) for u in (1, 2, 3)]
 
     own_t = permute(amplitudes, lambda y, xl, z, xh, c: (2 * xh + y % 2, xl, z, y // 2, c))
-    columns, mine = lax.optimization_barrier((shuffle(cholesky), mine))
-    own_c = lax.all_to_all(columns, ("xl", "z"), 0, 0, tiled=True)
+    own_c = lax.all_to_all(shuffle(cholesky, mine), ("xl", "z"), 0, 0, tiled=True)
 
     def from_y(value, by):
         return permute(value, lambda *at: shift_y(at, -by))
@@ -290,8 +302,9 @@
     p, m = from_plus(s), from_minus(s)
     rows = (s, p, m, from_plus(p[:2]), from_minus(m[2:]))
 
-    t_hi, t_lo, c_hi, c_lo = halves(place, amps, cols)
-    r2a, r2b, r1a, r1b, r3a, r3b, a_hi, a_lo = second(place, rows, (t_hi, t_lo, c_hi, c_lo))
+    t_hi, t_lo, c_wide = halves(place, amps, cols)
+    r2a, r2b, a_wide = second(place, rows, (t_hi, t_lo, c_wide))
+    r1a, r1b, r3a, r3b = third(place, (a_wide, c_wide))
 
     def to_plus(value):
         return permute(value, lambda *at: far(at, 1))
@@ -301,9 +314,9 @@
 
     a0, a1 = to_plus(r2a), to_minus(r2b)
     b1, d0 = to_plus(r1b), to_minus(r3a)
-    r0a, r0b = third(place, (a_hi, a_lo, c_hi, c_lo), (b1, d0))
+    r0 = fourth(place, (a_wide, c_wide), (b1, d0))
     b0, d1 = to_plus(r1a + a0), to_minus(r3b + a1)
-    q = (r0a + b0 + d0, r0b + b1 + d1)
+    q = (r0[:2] + b0 + d0, r0[2:] + b1 + d1)
     got = [permute(q[u // 2][u % 2], lambda *at, u=u: near(at, u)) for u in (1, 2, 3)]
     total = (q[0][0] + got[0]) + (got[1] + got[2])
     return permute(total, lambda *at: swapped(at)).transpose(0, 2, 1)

time: 211 us -> 199 us (0.943)
  waiting for transfers between devices: 78.9 us -> 72.2 us
  Pallas kernels: 50.1 us -> 46.9 us
    ppermute x29, waiting for transfers between devices: 77 us -> 70.3 us  [permute(): return lax.ppermute(value, AXES, pairs)]
    pallas_call x3 -> x4, Pallas kernels: 48.8 us -> 45.6 us  [call(): pl.pallas_call(body, out_shape=out_shape, in_specs=[ON_SMEM] + [ANYWHERE]...]
    unnamed x31 -> x25, local copies, waits for them, and re-layouts: 10.4 us -> 10.7 us
  transfers between devices with their start and end apart: 30 -> 30, of which waited for: 17 -> 16; matrix products, arithmetic and copies ran while one was open for 4% -> 4% of each run, Pallas kernels for 5% -> 10%
where the time goes in v4:
time: 199 us
  waiting for transfers between devices  72.2 us (36%)
  starting transfers between devices  60.7 us (31%)
  Pallas kernels  46.9 us (24%)
  local copies, waits for them, and re-layouts  13.4 us (7%)
  other arithmetic  5.22 us (3%)
    ppermute x29, waiting for transfers between devices, permute(): return lax.ppermute(value, AXES, pairs)  70.3 us
    ppermute x29, starting transfers between devices, permute(): return lax.ppermute(value, AXES, pairs)  54.9 us
    pallas_call x4, Pallas kernels, call(): pl.pallas_call(body, out_shape=out_shape, in_specs=[ON_SMEM] + [ANYWHERE]...  45.6 us
    unnamed x25, local copies, waits for them, and re-layouts  10.7 us
    all_to_all x1, starting transfers between devices, body(): lax.all_to_all(shuffle(cholesky, mine), ('xl', 'z'), 0, 0, tiled=True)  5.8 us
  transfers between devices with their start and end apart: 30, of which 16 were waited for; matrix products, arithmetic and copies ran while one was open for 4% of the time, Pallas kernels for 10%

profile of v4, /device:TPU:1, one launch (start us, length us, event | category | flops | bytes accessed | tf_op | source)
XLA Modules:
  0.0 198.7 jit_solution(10614001921515399452)
XLA Ops:
  0.0 4.9 %collective-permute-start = (f32[8,48,384]{2,1,0:T(8,128)}, f32[8,48,384]{2,1,0:T(8,128)S(1)}, u32[]{:S(2)}, u32[]{:S(2)}) collective-permute-start(f32[8,48,384]{2,1,0:T(8,128)} %l_ref.1), channel_id=1, source_target_pairs={{0,0},{1,4},{2,2},{3,6},{4,1},{5,5},{6,3},{7,7},{8,8},{9,12},{10,1... | collective-permute-start | bytes 1769480 | tf_op jit(solution)/shard_map/ppermute | solution.py:33
  4.9 1.7 collective-permute-start.8
  6.7 6.0 %collective-permute-done.after = f32[8,48,384]{2,1,0:T(8,128)S(1)} collective-permute-done((f32[8,48,384]{2,1,0:T(8,128)}, f32[8,48,384]{2,1,0:T(8,128)S(1)}, u32[]{:S(2)}, u32[]{:S(2)}) %collective-permute-start) | collective-permute-done | bytes 589856 | tf_op jit(solution)/shard_map/ppermute | solution.py:33
  16.3 5.8 %all-to-all-start = ((f32[8,48,384]{2,1,0:T(8,128)}), f32[8,48,384]{2,1,0:T(8,128)S(1)}, u32[]{:S(2)}, u32[]{:S(2)}) async-start(f32[8,48,384]{2,1,0:T(8,128)} %shard_map.28), calls=%async_computation | async-start | bytes 1179648 | tf_op jit(solution)/shard_map/all_to_all | solution.py:288
  23.6 2.3 %collective-permute-start.1 = (f32[8,48,384]{2,1,0:T(8,128)S(1)}, f32[8,48,384]{2,1,0:T(8,128)}, u32[]{:S(2)}, u32[]{:S(2)}) collective-permute-start(f32[8,48,384]{2,1,0:T(8,128)S(1)} %collective-permute-done.after), channel_id=1, source_target_pairs={{0,12},{1,19},{2,14},{3,17},{4,0},{5,23},{6,2},{7,21},{8,4},{9,27}... | collective-permute-start | bytes 1769480 | tf_op jit(solution)/shard_map/ppermute | solution.py:33
  28.6 1.9 all-to-all-done
  32.0 12.1 %collective-permute-done.2 = f32[8,48,384]{2,1,0:T(8,128)} collective-permute-done((f32[8,48,384]{2,1,0:T(8,128)S(1)}, f32[8,48,384]{2,1,0:T(8,128)}, u32[]{:S(2)}, u32[]{:S(2)}) %collective-permute-start.2) | collective-permute-done | bytes 589856 | tf_op jit(solution)/shard_map/ppermute | solution.py:33
  50.0 2.9 %collective-permute-done.16 = f32[8,48,384]{2,1,0:T(8,128)S(1)} collective-permute-done((f32[8,48,384]{2,1,0:T(8,128)S(1)}, f32[8,48,384]{2,1,0:T(8,128)S(1)}, u32[]{:S(2)}, u32[]{:S(2)}) %collective-permute-start.16) | collective-permute-done | bytes 589856 | tf_op jit(solution)/shard_map/ppermute | solution.py:33
  53.8 1.9 collective-permute-done.14
  56.8 2.4 %collective-permute-done.12 = f32[4,48,384]{2,1,0:T(8,128)S(1)} collective-permute-done((f32[4,48,384]{2,1,0:T(8,128)S(1)}, f32[4,48,384]{2,1,0:T(8,128)S(1)}, u32[]{:S(2)}, u32[]{:S(2)}) %collective-permute-start.12) | collective-permute-done | bytes 294944 | tf_op jit(solution)/shard_map/ppermute | solution.py:33
  61.5 6.7 %collective-permute-start.13 = (f32[4,8,48,384]{3,2,1,0:T(8,128)S(1)}, f32[4,8,48,384]{3,2,1,0:T(8,128)}, u32[]{:S(2)}, u32[]{:S(2)}) collective-permute-start(f32[4,8,48,384]{3,2,1,0:T(8,128)S(1)} %pad_maximum_fusion.1.refs_0_), channel_id=1, source_target_pairs={{0,1},{1,0},{2,3},{3,2},{4,5},{5,4},{6,7},{7,6},{8,9},{9,8},{10,11... | collective-permute-start | bytes 7077896 | tf_op jit(solution)/shard_map/ppermute | solution.py:33
  68.3 1.6 pad_maximum_fusion.2.refs_2_
  69.9 2.6 %collective-permute-start.18 = (f32[4,8,48,384]{3,2,1,0:T(8,128)}, f32[4,8,48,384]{3,2,1,0:T(8,128)}, u32[]{:S(2)}, u32[]{:S(2)}) collective-permute-start(f32[4,8,48,384]{3,2,1,0:T(8,128)} %pad_maximum_fusion.2.refs_2_), channel_id=1, source_target_pairs={{0,1},{1,0},{2,3},{3,2},{4,5},{5,4},{6,7},{7,6},{8,9},{9,8},{10,11... | collective-permute-start | bytes 7077896 | tf_op jit(solution)/shard_map/ppermute | solution.py:33
  72.5 2.3 %collective-permute-done.5.refs_2_ = f32[4,8,48,384]{3,2,1,0:T(8,128)S(1)} collective-permute-done((f32[4,8,48,384]{3,2,1,0:T(8,128)S(1)}, f32[4,8,48,384]{3,2,1,0:T(8,128)S(1)}, u32[]{:S(2)}, u32[]{:S(2)}) %collective-permute-start.5) | collective-permute-done | bytes 2359328 | tf_op jit(solution)/shard_map/ppermute | solution.py:33
  77.4 2.7 %collective-permute-start.6 = (f32[2,8,48,384]{3,2,1,0:T(8,128)}, f32[2,8,48,384]{3,2,1,0:T(8,128)}, u32[]{:S(2)}, u32[]{:S(2)}) collective-permute-start(f32[2,8,48,384]{3,2,1,0:T(8,128)} %slice.48), channel_id=1, source_target_pairs={{0,18},{1,13},{2,16},{3,15},{4,22},{5,1},{6,20},{7,3},{8,26},{9,5}... | collective-permute-start | bytes 3538952 | tf_op jit(solution)/shard_map/ppermute | solution.py:33
  80.1 5.2 %shard_map.29 = (bf16[768,1536]{1,0:T(8,128)(2,1)S(1)}, bf16[768,1536]{1,0:T(8,128)(2,1)S(1)}, bf16[4,384,2304]{2,1,0:T(8,128)(2,1)S(1)}) custom-call(s32[4]{0:T(128)S(1)} %pad_add_fusion.place, f32[4,8,48,384]{3,2,1,0:T(8,128)S(1)} %pad_maximum_fusion.1.refs_0_, f32[4,8,48,384]{3,2,1,0:T(8,128)} %collective-permute-done.13.refs_1_, ...), custom_call_target="tpu_custom_call" | custom-call | flops 2717908992 | bytes 12582912 | tf_op jit(solution)/shard_map/pallas_call | solution.py:230
  85.4 2.8 %copy-done = bf16[4,384,2304]{2,1,0:T(8,128)(2,1)} copy-done((bf16[4,384,2304]{2,1,0:T(8,128)(2,1)}, bf16[4,384,2304]{2,1,0:T(8,128)(2,1)S(1)}, u32[]{:S(2)}) %copy-start) | copy-done | bytes 7077912
  91.1 1.7 collective-permute-done.7.refs_4_
  93.6 27.6 %shard_map.30 = (f32[2,8,48,384]{3,2,1,0:T(8,128)S(1)}, f32[2,8,48,384]{3,2,1,0:T(8,128)S(1)}, bf16[4,384,2304]{2,1,0:T(8,128)(2,1)}) custom-call(s32[4]{0:T(128)S(1)} %pad_add_fusion.place, f32[4,8,48,384]{3,2,1,0:T(8,128)} %copy-done.6, f32[4,8,48,384]{3,2,1,0:T(8,128)} %copy-done.11, f32[4,8,48,384]{3,2,1,0:T(8,128)} %copy-done.10, ...), custom_call_target="tpu_custom_call" | custom-call | flops 13589544960 | bytes 12582912 | tf_op jit(solution)/shard_map/pallas_call | solution.py:230
  124.4 3.0 %copy-done.2 = bf16[4,384,2304]{2,1,0:T(8,128)(2,1)S(1)} copy-done((bf16[4,384,2304]{2,1,0:T(8,128)(2,1)S(1)}, bf16[4,384,2304]{2,1,0:T(8,128)(2,1)}, u32[]{:S(2)}) %copy-start.2) | copy-done | bytes 7077912
  127.4 8.4 %shard_map.31 = (f32[2,8,48,384]{3,2,1,0:T(8,128)S(1)}, f32[2,8,48,384]{3,2,1,0:T(8,128)S(1)}, f32[2,8,48,384]{3,2,1,0:T(8,128)S(1)}, f32[2,8,48,384]{3,2,1,0:T(8,128)S(1)}) custom-call(s32[4]{0:T(128)S(1)} %pad_add_fusion.place, bf16[4,384,2304]{2,1,0:T(8,128)(2,1)S(1)} %copy-done.2, bf16[4,384,2304]{2,1,0:T(8,128)(2,1)S(1)} %copy-done.1), custom_call_target="tpu_custom_call" | custom-call | flops 5435817984 | bytes 12582912 | tf_op jit(solution)/shard_map/pallas_call | solution.py:230
  135.8 2.7 %collective-permute-start.20 = (f32[2,8,48,384]{3,2,1,0:T(8,128)S(1)}, f32[2,8,48,384]{3,2,1,0:T(8,128)S(1)}, u32[]{:S(2)}, u32[]{:S(2)}) collective-permute-start(f32[2,8,48,384]{3,2,1,0:T(8,128)S(1)} %get-tuple-element.20), channel_id=1, source_target_pairs={{0,18},{1,13},{2,16},{3,15},{4,22},{5,1},{6,20},{7,3},{8,26},{9,5}... | collective-permute-start | bytes 3538952 | tf_op jit(solution)/shard_map/ppermute | solution.py:33
  138.8 2.7 %collective-permute-start.25 = (f32[2,8,48,384]{3,2,1,0:T(8,128)S(1)}, f32[2,8,48,384]{3,2,1,0:T(8,128)S(1)}, u32[]{:S(2)}, u32[]{:S(2)}) collective-permute-start(f32[2,8,48,384]{3,2,1,0:T(8,128)S(1)} %add.36), channel_id=1, source_target_pairs={{0,18},{1,13},{2,16},{3,15},{4,22},{5,1},{6,20},{7,3},{8,26},{9,5}... | collective-permute-start | bytes 3538952 | tf_op jit(solution)/shard_map/ppermute | solution.py:33
  141.6 10.8 %collective-permute-done.19.b1 = f32[2,8,48,384]{3,2,1,0:T(8,128)S(1)} collective-permute-done((f32[2,8,48,384]{3,2,1,0:T(8,128)S(1)}, f32[2,8,48,384]{3,2,1,0:T(8,128)S(1)}, u32[]{:S(2)}, u32[]{:S(2)}) %collective-permute-start.19) | collective-permute-done | bytes 1179680 | tf_op jit(solution)/shard_map/ppermute | solution.py:33
  152.4 4.4 %shard_map.32 = f32[4,8,48,384]{3,2,1,0:T(8,128)S(1)} custom-call(s32[4]{0:T(128)S(1)} %pad_add_fusion.place, bf16[4,384,2304]{2,1,0:T(8,128)(2,1)S(1)} %copy-done.2, bf16[4,384,2304]{2,1,0:T(8,128)(2,1)S(1)} %copy-done.1, f32[2,8,48,384]{3,2,1,0:T(8,128)S(1)} %collective-permute-done.19.b1, f32[2,8,48,384]{3,2,1,0:T(8,128)S(1)} %collective-permute-done.20.d0), custom_call_target="tpu_custom_call" | custom-call | flops 2717908992 | bytes 12582912 | tf_op jit(solution)/shard_map/pallas_call | solution.py:230
  156.8 8.2 %collective-permute-done.22 = f32[2,8,48,384]{3,2,1,0:T(8,128)S(1)} collective-permute-done((f32[2,8,48,384]{3,2,1,0:T(8,128)S(1)}, f32[2,8,48,384]{3,2,1,0:T(8,128)S(1)}, u32[]{:S(2)}, u32[]{:S(2)}) %collective-permute-start.22) | collective-permute-done | bytes 1179680 | tf_op jit(solution)/shard_map/ppermute | solution.py:33
  165.6 2.7 %collective-permute-start.27 = (f32[8,48,384]{2,1,0:T(8,128)S(1)}, f32[8,48,384]{2,1,0:T(8,128)S(1)}, u32[]{:S(2)}, u32[]{:S(2)}) collective-permute-start(f32[8,48,384]{2,1,0:T(8,128)S(1)} %get-tuple-element.27), channel_id=1, source_target_pairs={{0,12},{1,19},{2,14},{3,17},{4,0},{5,23},{6,2},{7,21},{8,4},{9,27}... | collective-permute-start | bytes 1769480 | tf_op jit(solution)/shard_map/ppermute | solution.py:33
  168.3 2.0 collective-permute-start.26
  170.2 5.6 %collective-permute-done.23 = f32[8,48,384]{2,1,0:T(8,128)S(1)} collective-permute-done((f32[8,48,384]{2,1,0:T(8,128)S(1)}, f32[8,48,384]{2,1,0:T(8,128)S(1)}, u32[]{:S(2)}, u32[]{:S(2)}) %collective-permute-start.23) | collective-permute-done | bytes 589856 | tf_op jit(solution)/shard_map/ppermute | solution.py:33
  176.0 6.6 %collective-permute-done.26 = f32[8,48,384]{2,1,0:T(8,128)S(1)} collective-permute-done((f32[8,48,384]{2,1,0:T(8,128)S(1)}, f32[8,48,384]{2,1,0:T(8,128)S(1)}, u32[]{:S(2)}, u32[]{:S(2)}) %collective-permute-start.26) | collective-permute-done | bytes 589856 | tf_op jit(solution)/shard_map/ppermute | solution.py:33
  182.8 7.5 %collective-permute-start.28 = (f32[8,48,384]{2,1,0:T(8,128)S(1)}, f32[8,48,384]{2,1,0:T(8,128)S(1)}, u32[]{:S(2)}, u32[]{:S(2)}) collective-permute-start(f32[8,48,384]{2,1,0:T(8,128)S(1)} %fusion.3), channel_id=1, source_target_pairs={{0,0},{1,4},{2,2},{3,6},{4,1},{5,5},{6,3},{7,7},{8,8},{9,12},{10,1... | collective-permute-start | bytes 1769480 | tf_op jit(solution)/shard_map/ppermute | solution.py:33
  190.3 7.6 %collective-permute-done.28 = f32[8,48,384]{2,1,0:T(8,128)S(1)} collective-permute-done((f32[8,48,384]{2,1,0:T(8,128)S(1)}, f32[8,48,384]{2,1,0:T(8,128)S(1)}, u32[]{:S(2)}, u32[]{:S(2)}) %collective-permute-start.28) | collective-permute-done | bytes 589856 | tf_op jit(solution)/shard_map/ppermute | solution.py:33
  (76 shorter events, 30.9 us)
Async XLA Ops:
  0.0 12.7 %collective-permute-start = (f32[8,48,384]{2,1,0:T(8,128)}, f32[8,48,384]{2,1,0:T(8,128)S(1)}, u32[]{:S(2)}, u32[]{:S(2)}) collective-permute-start(f32[8,48,384]{2,1,0:T(8,128)} %l_ref.1), channel_id=1, source_target_pairs={{0,0},{1,4},{2,2},{3,6},{4,1},{5,5},{6,3},{7,7},{8,8},{9,12},{10,1... | collective-permute-start | bytes 1769480 | tf_op jit(solution)/shard_map/ppermute | solution.py:33
  4.9 21.0 %collective-permute-start.8 = (f32[8,48,384]{2,1,0:T(8,128)}, f32[8,48,384]{2,1,0:T(8,128)S(1)}, u32[]{:S(2)}, u32[]{:S(2)}) collective-permute-start(f32[8,48,384]{2,1,0:T(8,128)} %param.3), channel_id=1, source_target_pairs={{0,0},{1,1},{2,64},{3,65},{4,4},{5,5},{6,68},{7,69},{8,8},{9,9},{1... | collective-permute-start | bytes 1769480 | tf_op jit(solution)/shard_map/ppermute | solution.py:33
  12.7 18.9 %collective-permute-start.3 = (f32[8,48,384]{2,1,0:T(8,128)S(1)}, f32[8,48,384]{2,1,0:T(8,128)S(1)}, u32[]{:S(2)}, u32[]{:S(2)}) collective-permute-start(f32[8,48,384]{2,1,0:T(8,128)S(1)} %collective-permute-done.after), channel_id=1, source_target_pairs={{0,4},{1,17},{2,6},{3,19},{4,8},{5,21},{6,10},{7,23},{8,12},{9,25}... | collective-permute-start | bytes 1769480 | tf_op jit(solution)/shard_map/ppermute | solution.py:33
  16.3 14.2 %all-to-all-start = ((f32[8,48,384]{2,1,0:T(8,128)}), f32[8,48,384]{2,1,0:T(8,128)S(1)}, u32[]{:S(2)}, u32[]{:S(2)}) async-start(f32[8,48,384]{2,1,0:T(8,128)} %shard_map.28), calls=%async_computation | async-start | bytes 1179648 | tf_op jit(solution)/shard_map/all_to_all | solution.py:288
  22.1 22.0 %collective-permute-start.2 = (f32[8,48,384]{2,1,0:T(8,128)S(1)}, f32[8,48,384]{2,1,0:T(8,128)}, u32[]{:S(2)}, u32[]{:S(2)}) collective-permute-start(f32[8,48,384]{2,1,0:T(8,128)S(1)} %collective-permute-done.after), channel_id=1, source_target_pairs={{0,8},{1,3},{2,10},{3,1},{4,12},{5,7},{6,14},{7,5},{8,0},{9,11},{1... | collective-permute-start | bytes 1769480 | tf_op jit(solution)/shard_map/ppermute | solution.py:33
  23.6 20.5 %collective-permute-start.1 = (f32[8,48,384]{2,1,0:T(8,128)S(1)}, f32[8,48,384]{2,1,0:T(8,128)}, u32[]{:S(2)}, u32[]{:S(2)}) collective-permute-start(f32[8,48,384]{2,1,0:T(8,128)S(1)} %collective-permute-done.after), channel_id=1, source_target_pairs={{0,12},{1,19},{2,14},{3,17},{4,0},{5,23},{6,2},{7,21},{8,4},{9,27}... | collective-permute-start | bytes 1769480 | tf_op jit(solution)/shard_map/ppermute | solution.py:33
  26.0 19.6 %copy-start.8 = (f32[8,48,384]{2,1,0:T(8,128)}, f32[8,48,384]{2,1,0:T(8,128)S(1)}, u32[]{:S(2)}) copy-start(f32[8,48,384]{2,1,0:T(8,128)S(1)} %collective-permute-done.8) | copy-start | bytes 1769476
  26.0 20.9 %collective-permute-start.11 = (f32[8,48,384]{2,1,0:T(8,128)S(1)}, f32[8,48,384]{2,1,0:T(8,128)S(1)}, u32[]{:S(2)}, u32[]{:S(2)}) collective-permute-start(f32[8,48,384]{2,1,0:T(8,128)S(1)} %collective-permute-done.8), channel_id=1, source_target_pairs={{0,32},{1,33},{2,34},{3,35},{4,36},{5,37},{6,38},{7,39},{8,40},{9,... | collective-permute-start | bytes 1769480 | tf_op jit(solution)/shard_map/ppermute | solution.py:33
  27.3 21.1 %collective-permute-start.9 = (f32[8,48,384]{2,1,0:T(8,128)S(1)}, f32[8,48,384]{2,1,0:T(8,128)S(1)}, u32[]{:S(2)}, u32[]{:S(2)}) collective-permute-start(f32[8,48,384]{2,1,0:T(8,128)S(1)} %collective-permute-done.8), channel_id=1, source_target_pairs={{0,96},{1,97},{2,98},{3,99},{4,100},{5,101},{6,102},{7,103},{8,104... | collective-permute-start | bytes 1769480 | tf_op jit(solution)/shard_map/ppermute | solution.py:33
  31.6 21.3 %collective-permute-start.16 = (f32[8,48,384]{2,1,0:T(8,128)S(1)}, f32[8,48,384]{2,1,0:T(8,128)S(1)}, u32[]{:S(2)}, u32[]{:S(2)}) collective-permute-start(f32[8,48,384]{2,1,0:T(8,128)S(1)} %all-to-all-done), channel_id=1, source_target_pairs={{0,32},{1,33},{2,34},{3,35},{4,36},{5,37},{6,38},{7,39},{8,40},{9,... | collective-permute-start | bytes 1769480 | tf_op jit(solution)/shard_map/ppermute | solution.py:33
  44.1 11.7 %collective-permute-start.14 = (f32[8,48,384]{2,1,0:T(8,128)S(1)}, f32[8,48,384]{2,1,0:T(8,128)S(1)}, u32[]{:S(2)}, u32[]{:S(2)}) collective-permute-start(f32[8,48,384]{2,1,0:T(8,128)S(1)} %all-to-all-done), channel_id=1, source_target_pairs={{0,96},{1,97},{2,98},{3,99},{4,100},{5,101},{6,102},{7,103},{8,104... | collective-permute-start | bytes 1769480 | tf_op jit(solution)/shard_map/ppermute | solution.py:33
  45.6 29.3 %collective-permute-start.5 = (f32[4,8,48,384]{3,2,1,0:T(8,128)S(1)}, f32[4,8,48,384]{3,2,1,0:T(8,128)S(1)}, u32[]{:S(2)}, u32[]{:S(2)}) collective-permute-start(f32[4,8,48,384]{3,2,1,0:T(8,128)S(1)} %pad_maximum_fusion.refs_0_), channel_id=1, source_target_pairs={{0,16},{1,5},{2,18},{3,7},{4,20},{5,9},{6,22},{7,11},{8,24},{9,13}... | collective-permute-start | bytes 7077896 | tf_op jit(solution)/shard_map/ppermute | solution.py:33
  46.9 29.3 %collective-permute-start.4 = (f32[4,8,48,384]{3,2,1,0:T(8,128)S(1)}, f32[4,8,48,384]{3,2,1,0:T(8,128)S(1)}, u32[]{:S(2)}, u32[]{:S(2)}) collective-permute-start(f32[4,8,48,384]{3,2,1,0:T(8,128)S(1)} %pad_maximum_fusion.refs_0_), channel_id=1, source_target_pairs={{0,18},{1,13},{2,16},{3,15},{4,22},{5,1},{6,20},{7,3},{8,26},{9,5}... | collective-permute-start | bytes 7077896 | tf_op jit(solution)/shard_map/ppermute | solution.py:33
  48.4 10.8 %collective-permute-start.12 = (f32[4,48,384]{2,1,0:T(8,128)S(1)}, f32[4,48,384]{2,1,0:T(8,128)S(1)}, u32[]{:S(2)}, u32[]{:S(2)}) collective-permute-start(f32[4,48,384]{2,1,0:T(8,128)S(1)} %slice.51), channel_id=1, source_target_pairs={{0,32},{1,33},{2,34},{3,35},{4,36},{5,37},{6,38},{7,39},{8,40},{9,... | collective-permute-start | bytes 884744 | tf_op jit(solution)/shard_map/ppermute | solution.py:33
  52.9 7.3 %collective-permute-start.10 = (f32[4,48,384]{2,1,0:T(8,128)S(1)}, f32[4,48,384]{2,1,0:T(8,128)S(1)}, u32[]{:S(2)}, u32[]{:S(2)}) collective-permute-start(f32[4,48,384]{2,1,0:T(8,128)S(1)} %slice.50), channel_id=1, source_target_pairs={{0,96},{1,97},{2,98},{3,99},{4,100},{5,101},{6,102},{7,103},{8,104... | collective-permute-start | bytes 884744 | tf_op jit(solution)/shard_map/ppermute | solution.py:33
  55.8 12.4 %collective-permute-start.17 = (f32[4,48,384]{2,1,0:T(8,128)S(1)}, f32[4,48,384]{2,1,0:T(8,128)S(1)}, u32[]{:S(2)}, u32[]{:S(2)}) collective-permute-start(f32[4,48,384]{2,1,0:T(8,128)S(1)} %slice.53), channel_id=1, source_target_pairs={{0,32},{1,33},{2,34},{3,35},{4,36},{5,37},{6,38},{7,39},{8,40},{9,... | collective-permute-start | bytes 884744 | tf_op jit(solution)/shard_map/ppermute | solution.py:33
  59.2 9.0 %collective-permute-start.15 = (f32[4,48,384]{2,1,0:T(8,128)S(1)}, f32[4,48,384]{2,1,0:T(8,128)S(1)}, u32[]{:S(2)}, u32[]{:S(2)}) collective-permute-start(f32[4,48,384]{2,1,0:T(8,128)S(1)} %slice.52), channel_id=1, source_target_pairs={{0,96},{1,97},{2,98},{3,99},{4,100},{5,101},{6,102},{7,103},{8,104... | collective-permute-start | bytes 884744 | tf_op jit(solution)/shard_map/ppermute | solution.py:33
  61.5 18.6 %collective-permute-start.13 = (f32[4,8,48,384]{3,2,1,0:T(8,128)S(1)}, f32[4,8,48,384]{3,2,1,0:T(8,128)}, u32[]{:S(2)}, u32[]{:S(2)}) collective-permute-start(f32[4,8,48,384]{3,2,1,0:T(8,128)S(1)} %pad_maximum_fusion.1.refs_0_), channel_id=1, source_target_pairs={{0,1},{1,0},{2,3},{3,2},{4,5},{5,4},{6,7},{7,6},{8,9},{9,8},{10,11... | collective-permute-start | bytes 7077896 | tf_op jit(solution)/shard_map/ppermute | solution.py:33
  69.9 10.3 %collective-permute-start.18 = (f32[4,8,48,384]{3,2,1,0:T(8,128)}, f32[4,8,48,384]{3,2,1,0:T(8,128)}, u32[]{:S(2)}, u32[]{:S(2)}) collective-permute-start(f32[4,8,48,384]{3,2,1,0:T(8,128)} %pad_maximum_fusion.2.refs_2_), channel_id=1, source_target_pairs={{0,1},{1,0},{2,3},{3,2},{4,5},{5,4},{6,7},{7,6},{8,9},{9,8},{10,11... | collective-permute-start | bytes 7077896 | tf_op jit(solution)/shard_map/ppermute | solution.py:33
  76.1 16.8 %collective-permute-start.7 = (f32[2,8,48,384]{3,2,1,0:T(8,128)}, f32[2,8,48,384]{3,2,1,0:T(8,128)S(1)}, u32[]{:S(2)}, u32[]{:S(2)}) collective-permute-start(f32[2,8,48,384]{3,2,1,0:T(8,128)} %slice.49), channel_id=1, source_target_pairs={{0,16},{1,5},{2,18},{3,7},{4,20},{5,9},{6,22},{7,11},{8,24},{9,13}... | collective-permute-start | bytes 3538952 | tf_op jit(solution)/shard_map/ppermute | solution.py:33
  77.4 16.2 %collective-permute-start.6 = (f32[2,8,48,384]{3,2,1,0:T(8,128)}, f32[2,8,48,384]{3,2,1,0:T(8,128)}, u32[]{:S(2)}, u32[]{:S(2)}) collective-permute-start(f32[2,8,48,384]{3,2,1,0:T(8,128)} %slice.48), channel_id=1, source_target_pairs={{0,18},{1,13},{2,16},{3,15},{4,22},{5,1},{6,20},{7,3},{8,26},{9,5}... | collective-permute-start | bytes 3538952 | tf_op jit(solution)/shard_map/ppermute | solution.py:33
  93.6 30.7 %copy-start.1 = (bf16[4,384,2304]{2,1,0:T(8,128)(2,1)S(1)}, bf16[4,384,2304]{2,1,0:T(8,128)(2,1)}, u32[]{:S(2)}) copy-start(bf16[4,384,2304]{2,1,0:T(8,128)(2,1)} %copy-done) | copy-start | bytes 21233668
  121.2 17.3 %collective-permute-start.21 = (f32[2,8,48,384]{3,2,1,0:T(8,128)S(1)}, f32[2,8,48,384]{3,2,1,0:T(8,128)S(1)}, u32[]{:S(2)}, u32[]{:S(2)}) collective-permute-start(f32[2,8,48,384]{3,2,1,0:T(8,128)S(1)} %get-tuple-element.22), channel_id=1, source_target_pairs={{0,16},{1,5},{2,18},{3,7},{4,20},{5,9},{6,22},{7,11},{8,24},{9,13}... | collective-permute-start | bytes 3538952 | tf_op jit(solution)/shard_map/ppermute | solution.py:33
  122.7 16.0 %collective-permute-start.24 = (f32[2,8,48,384]{3,2,1,0:T(8,128)S(1)}, f32[2,8,48,384]{3,2,1,0:T(8,128)S(1)}, u32[]{:S(2)}, u32[]{:S(2)}) collective-permute-start(f32[2,8,48,384]{3,2,1,0:T(8,128)S(1)} %get-tuple-element.24), channel_id=1, source_target_pairs={{0,18},{1,13},{2,16},{3,15},{4,22},{5,1},{6,20},{7,3},{8,26},{9,5}... | collective-permute-start | bytes 3538952 | tf_op jit(solution)/shard_map/ppermute | solution.py:33
  135.7 16.6 %collective-permute-start.19 = (f32[2,8,48,384]{3,2,1,0:T(8,128)S(1)}, f32[2,8,48,384]{3,2,1,0:T(8,128)S(1)}, u32[]{:S(2)}, u32[]{:S(2)}) collective-permute-start(f32[2,8,48,384]{3,2,1,0:T(8,128)S(1)} %get-tuple-element.19), channel_id=1, source_target_pairs={{0,16},{1,5},{2,18},{3,7},{4,20},{5,9},{6,22},{7,11},{8,24},{9,13}... | collective-permute-start | bytes 3538952 | tf_op jit(solution)/shard_map/ppermute | solution.py:33
  135.8 16.5 %collective-permute-start.20 = (f32[2,8,48,384]{3,2,1,0:T(8,128)S(1)}, f32[2,8,48,384]{3,2,1,0:T(8,128)S(1)}, u32[]{:S(2)}, u32[]{:S(2)}) collective-permute-start(f32[2,8,48,384]{3,2,1,0:T(8,128)S(1)} %get-tuple-element.20), channel_id=1, source_target_pairs={{0,18},{1,13},{2,16},{3,15},{4,22},{5,1},{6,20},{7,3},{8,26},{9,5}... | collective-permute-start | bytes 3538952 | tf_op jit(solution)/shard_map/ppermute | solution.py:33
  138.6 26.4 %collective-permute-start.22 = (f32[2,8,48,384]{3,2,1,0:T(8,128)S(1)}, f32[2,8,48,384]{3,2,1,0:T(8,128)S(1)}, u32[]{:S(2)}, u32[]{:S(2)}) collective-permute-start(f32[2,8,48,384]{3,2,1,0:T(8,128)S(1)} %add.31), channel_id=1, source_target_pairs={{0,16},{1,5},{2,18},{3,7},{4,20},{5,9},{6,22},{7,11},{8,24},{9,13}... | collective-permute-start | bytes 3538952 | tf_op jit(solution)/shard_map/ppermute | solution.py:33
  138.8 26.2 %collective-permute-start.25 = (f32[2,8,48,384]{3,2,1,0:T(8,128)S(1)}, f32[2,8,48,384]{3,2,1,0:T(8,128)S(1)}, u32[]{:S(2)}, u32[]{:S(2)}) collective-permute-start(f32[2,8,48,384]{3,2,1,0:T(8,128)S(1)} %add.36), channel_id=1, source_target_pairs={{0,18},{1,13},{2,16},{3,15},{4,22},{5,1},{6,20},{7,3},{8,26},{9,5}... | collective-permute-start | bytes 3538952 | tf_op jit(solution)/shard_map/ppermute | solution.py:33
  165.5 10.3 %collective-permute-start.23 = (f32[8,48,384]{2,1,0:T(8,128)S(1)}, f32[8,48,384]{2,1,0:T(8,128)S(1)}, u32[]{:S(2)}, u32[]{:S(2)}) collective-permute-start(f32[8,48,384]{2,1,0:T(8,128)S(1)} %slice_bitcast_fusion.2), channel_id=1, source_target_pairs={{0,4},{1,17},{2,6},{3,19},{4,8},{5,21},{6,10},{7,23},{8,12},{9,25}... | collective-permute-start | bytes 1769480 | tf_op jit(solution)/shard_map/ppermute | solution.py:33
  165.6 10.4 %collective-permute-start.27 = (f32[8,48,384]{2,1,0:T(8,128)S(1)}, f32[8,48,384]{2,1,0:T(8,128)S(1)}, u32[]{:S(2)}, u32[]{:S(2)}) collective-permute-start(f32[8,48,384]{2,1,0:T(8,128)S(1)} %get-tuple-element.27), channel_id=1, source_target_pairs={{0,12},{1,19},{2,14},{3,17},{4,0},{5,23},{6,2},{7,21},{8,4},{9,27}... | collective-permute-start | bytes 1769480 | tf_op jit(solution)/shard_map/ppermute | solution.py:33
  168.3 14.4 %collective-permute-start.26 = (f32[8,48,384]{2,1,0:T(8,128)S(1)}, f32[8,48,384]{2,1,0:T(8,128)S(1)}, u32[]{:S(2)}, u32[]{:S(2)}) collective-permute-start(f32[8,48,384]{2,1,0:T(8,128)S(1)} %get-tuple-element.28), channel_id=1, source_target_pairs={{0,8},{1,3},{2,10},{3,1},{4,12},{5,7},{6,14},{7,5},{8,0},{9,11},{1... | collective-permute-start | bytes 1769480 | tf_op jit(solution)/shard_map/ppermute | solution.py:33
  182.8 15.1 %collective-permute-start.28 = (f32[8,48,384]{2,1,0:T(8,128)S(1)}, f32[8,48,384]{2,1,0:T(8,128)S(1)}, u32[]{:S(2)}, u32[]{:S(2)}) collective-permute-start(f32[8,48,384]{2,1,0:T(8,128)S(1)} %fusion.3), channel_id=1, source_target_pairs={{0,0},{1,4},{2,2},{3,6},{4,1},{5,5},{6,3},{7,7},{8,8},{9,12},{10,1... | collective-permute-start | bytes 1769480 | tf_op jit(solution)/shard_map/ppermute | solution.py:33
  (10 other events, 57.4 us)

commit v5 on v4

--- a/solution.py
+++ b/solution.py
@@ -176,25 +176,32 @@
                     at = ((j % 2) * 8 + q * 4 + p) * 48
                     half[m * 4 + j // 2, at : at + 48, :] = h[j * 48 : j * 48 + 48, p * 192 : p * 192 + 192]
 
-    @pl.loop(0, 8)
-    def _(i):
+    for i in range(8):
         high, low = split(half[i].T)
         for k, part in enumerate((high, low, high)):
             for b in range(4):
-                a_wide[b, offset(i, 48), k * 768 : k * 768 + 768] = part[b * 48 : b * 48 + 48, :]
+                a_wide[b, i * 48 : i * 48 + 48, k * 768 : k * 768 + 768] = part[b * 48 : b * 48 + 48, :]
 
     wait(c_copies)
     copies = [pltpu.make_async_copy(blocks.at[pl.ds(2 * k, 2)], outs[k], out_sem) for k in range(2)]
-    copies.append(pltpu.make_async_copy(a_wide, outs[2], out_sem))
+    copies.append(pltpu.make_async_copy(a_wide.at[:, :, pl.ds(0, 1536)], outs[2], out_sem))
     start(copies[2:])
     ladder_of(place, 2, a_wide, c_wide, blocks)
     start(copies[:2])
     wait(copies)
 
 
+def held_copies(a_in, c_in, a_wide, c_wide, sem):
+    return [
+        pltpu.make_async_copy(a_in, a_wide.at[:, :, pl.ds(0, 1536)], sem),
+        pltpu.make_async_copy(a_in.at[:, :, pl.ds(0, 768)], a_wide.at[:, :, pl.ds(1536, 768)], sem),
+        pltpu.make_async_copy(c_in, c_wide, sem),
+    ]
+
+
 def third_kernel(place, a_in, c_in, *refs):
     outs, (a_wide, c_wide, blocks, sem, out_sem) = refs[:4], refs[4:]
-    held = [pltpu.make_async_copy(a_in, a_wide, sem), pltpu.make_async_copy(c_in, c_wide, sem)]
+    held = held_copies(a_in, c_in, a_wide, c_wide, sem)
     start(held)
     wait(held)
     copies = [pltpu.make_async_copy(blocks.at[k // 2, pl.ds(k % 2 * 2, 2)], out, out_sem) for k, out in enumerate(outs)]
@@ -206,7 +213,7 @@
 
 def fourth_kernel(place, a_in, c_in, b1, d0, out, a_wide, c_wide, sem):
     del b1, d0
-    held = [pltpu.make_async_copy(a_in, a_wide, sem), pltpu.make_async_copy(c_in, c_wide, sem)]
+    held = held_copies(a_in, c_in, a_wide, c_wide, sem)
     start(held)
     wait(held)
     ladder_of(place, 0, a_wide, c_wide, out)
@@ -220,17 +227,18 @@
 QUAD = jax.ShapeDtypeStruct((4, 8, 48, 384), F32)
 PAIR = jax.ShapeDtypeStruct((2, 8, 48, 384), F32)
 WIDE = jax.ShapeDtypeStruct((4, 384, 2304), BF16)
+BOTH = jax.ShapeDtypeStruct((4, 384, 1536), BF16)
 
 
 AMPS = (768, 1536)
 HALF_AMPS = jax.ShapeDtypeStruct(AMPS, BF16)
 
 
-def call(body, out_shape, out_spec, scratch, megabytes, units, place, *args):
+def call(body, out_shape, out_spec, scratch, megabytes, units, place, *args, in_hbm=0):
     return pl.pallas_call(
         body,
         out_shape=out_shape,
-        in_specs=[ON_SMEM] + [ANYWHERE] * len(args),
+        in_specs=[ON_SMEM] + [ON_HBM] * in_hbm + [ANYWHERE] * (len(args) - in_hbm),
         out_specs=[out_spec] * len(out_shape),
         scratch_shapes=scratch,
         compiler_params=pltpu.CompilerParams(vmem_limit_bytes=megabytes << 20),
@@ -248,17 +256,17 @@
     scratch = [pltpu.VMEM((8, 192, 1536), F32)] + [pltpu.VMEM(AMPS, BF16)] * 2 + [pltpu.VMEM((8, 768, 192), F32)]
     scratch += [pltpu.VMEM(WIDE.shape, BF16)] * 2 + [pltpu.VMEM(QUAD.shape, F32)]
     scratch += [DMA, DMA((2,)), DMA, DMA]
-    return call(second_kernel, [PAIR] * 2 + [WIDE], ON_HBM, scratch, 48, 5, place, *rows, *parts)
+    return call(second_kernel, [PAIR] * 2 + [BOTH], ON_HBM, scratch, 48, 5, place, *rows, *parts)
 
 
 def third(place, parts):
     scratch = [pltpu.VMEM(WIDE.shape, BF16)] * 2 + [pltpu.VMEM((2, *QUAD.shape), F32), DMA, DMA]
-    return call(third_kernel, [PAIR] * 4, ON_HBM, scratch, 32, 2, place, *parts)
+    return call(third_kernel, [PAIR] * 4, ON_HBM, scratch, 32, 2, place, *parts, in_hbm=2)
 
 
 def fourth(place, parts, after):
     scratch = [pltpu.VMEM(WIDE.shape, BF16)] * 2 + [DMA]
-    return call(fourth_kernel, [QUAD], ON_VMEM, scratch, 28, 1, place, *parts, *after)[0]
+    return call(fourth_kernel, [QUAD], ON_VMEM, scratch, 28, 1, place, *parts, *after, in_hbm=2)[0]
 
 
 def shuffle(cholesky, after):
@@ -303,8 +311,8 @@
     rows = (s, p, m, from_plus(p[:2]), from_minus(m[2:]))
 
     t_hi, t_lo, c_wide = halves(place, amps, cols)
-    r2a, r2b, a_wide = second(place, rows, (t_hi, t_lo, c_wide))
-    r1a, r1b, r3a, r3b = third(place, (a_wide, c_wide))
+    r2a, r2b, a_both = second(place, rows, (t_hi, t_lo, c_wide))
+    r1a, r1b, r3a, r3b = third(place, (a_both, c_wide))
 
     def to_plus(value):
         return permute(value, lambda *at: far(at, 1))
@@ -314,10 +322,10 @@
 
     a0, a1 = to_plus(r2a), to_minus(r2b)
     b1, d0 = to_plus(r1b), to_minus(r3a)
-    r0 = fourth(place, (a_wide, c_wide), (b1, d0))
+    r0 = fourth(place, (a_both, c_wide), (b1, d0))
     b0, d1 = to_plus(r1a + a0), to_minus(r3b + a1)
     q = (r0[:2] + b0 + d0, r0[2:] + b1 + d1)
-    got = [permute(q[u // 2][u % 2], lambda *at, u=u: near(at, u)) for u in (1, 2, 3)]
+    got = [permute(q[u // 2][u % 2], lambda *at, u=u: near(at, u)) for u in (3, 2, 1)]
     total = (q[0][0] + got[0]) + (got[1] + got[2])
     return permute(total, lambda *at: swapped(at)).transpose(0, 2, 1)
 

time: 199 us -> 197 us (0.990)
  starting transfers between devices: 60.7 us -> 58.2 us
  waiting for transfers between devices: 72.2 us -> 74.7 us
    all_to_all x1, waiting for transfers between devices: 1.91 us -> 4.49 us  [body(): lax.all_to_all(shuffle(cholesky, mine), ('xl', 'z'), 0, 0, tiled=True)]
  transfers between devices with their start and end apart: 30 -> 30, of which waited for: 16 -> 17; matrix products, arithmetic and copies ran while one was open for 4% -> 4% of each run, Pallas kernels for 10% -> 10%
where the time goes in v5:
time: 197 us
  waiting for transfers between devices  74.7 us (38%)
  starting transfers between devices  58.2 us (30%)
  Pallas kernels  45 us (23%)
  local copies, waits for them, and re-layouts  13.2 us (7%)
  other arithmetic  5.21 us (3%)
    ppermute x29, waiting for transfers between devices, permute(): return lax.ppermute(value, AXES, pairs)  70.3 us
    ppermute x29, starting transfers between devices, permute(): return lax.ppermute(value, AXES, pairs)  53.6 us
    pallas_call x4, Pallas kernels, call(): pl.pallas_call(body, out_shape=out_shape, in_specs=[ON_SMEM] + [ON_HBM] *...  43.6 us
    unnamed x25, local copies, waits for them, and re-layouts  10.6 us
    all_to_all x1, starting transfers between devices, body(): lax.all_to_all(shuffle(cholesky, mine), ('xl', 'z'), 0, 0, tiled=True)  4.58 us
    all_to_all x1, waiting for transfers between devices, body(): lax.all_to_all(shuffle(cholesky, mine), ('xl', 'z'), 0, 0, tiled=True)  4.49 us
  transfers between devices with their start and end apart: 30, of which 17 were waited for; matrix products, arithmetic and copies ran while one was open for 4% of the time, Pallas kernels for 10%

profile of v5, /device:TPU:1, one launch (start us, length us, event | category | flops | bytes accessed | tf_op | source)
XLA Modules:
  0.0 196.6 jit_solution(15149779683709379618)
XLA Ops:
  0.0 4.9 %collective-permute-start = (f32[8,48,384]{2,1,0:T(8,128)}, f32[8,48,384]{2,1,0:T(8,128)S(1)}, u32[]{:S(2)}, u32[]{:S(2)}) collective-permute-start(f32[8,48,384]{2,1,0:T(8,128)} %l_ref.1), channel_id=1, source_target_pairs={{0,0},{1,4},{2,2},{3,6},{4,1},{5,5},{6,3},{7,7},{8,8},{9,12},{10,1... | collective-permute-start | bytes 1769480 | tf_op jit(solution)/shard_map/ppermute | solution.py:33
  6.7 6.0 %collective-permute-done.after = f32[8,48,384]{2,1,0:T(8,128)S(1)} collective-permute-done((f32[8,48,384]{2,1,0:T(8,128)}, f32[8,48,384]{2,1,0:T(8,128)S(1)}, u32[]{:S(2)}, u32[]{:S(2)}) %collective-permute-start) | collective-permute-done | bytes 589856 | tf_op jit(solution)/shard_map/ppermute | solution.py:33
  12.7 2.8 %collective-permute-start.1 = (f32[8,48,384]{2,1,0:T(8,128)S(1)}, f32[8,48,384]{2,1,0:T(8,128)S(1)}, u32[]{:S(2)}, u32[]{:S(2)}) collective-permute-start(f32[8,48,384]{2,1,0:T(8,128)S(1)} %collective-permute-done.after), channel_id=1, source_target_pairs={{0,12},{1,19},{2,14},{3,17},{4,0},{5,23},{6,2},{7,21},{8,4},{9,27}... | collective-permute-start | bytes 1769480 | tf_op jit(solution)/shard_map/ppermute | solution.py:33
  17.9 4.6 %all-to-all-start = ((f32[8,48,384]{2,1,0:T(8,128)}), f32[8,48,384]{2,1,0:T(8,128)S(1)}, u32[]{:S(2)}, u32[]{:S(2)}) async-start(f32[8,48,384]{2,1,0:T(8,128)} %shard_map.28), calls=%async_computation | async-start | bytes 1179648 | tf_op jit(solution)/shard_map/all_to_all | solution.py:296
  24.7 2.7 %collective-permute-start.9 = (f32[8,48,384]{2,1,0:T(8,128)S(1)}, f32[8,48,384]{2,1,0:T(8,128)S(1)}, u32[]{:S(2)}, u32[]{:S(2)}) collective-permute-start(f32[8,48,384]{2,1,0:T(8,128)S(1)} %collective-permute-done.8), channel_id=1, source_target_pairs={{0,96},{1,97},{2,98},{3,99},{4,100},{5,101},{6,102},{7,103},{8,104... | collective-permute-start | bytes 1769480 | tf_op jit(solution)/shard_map/ppermute | solution.py:33
  27.5 4.5 %all-to-all-done = f32[8,48,384]{2,1,0:T(8,128)S(1)} async-done(((f32[8,48,384]{2,1,0:T(8,128)}), f32[8,48,384]{2,1,0:T(8,128)S(1)}, u32[]{:S(2)}, u32[]{:S(2)}) %all-to-all-start) | async-done | bytes 589856 | tf_op jit(solution)/shard_map/all_to_all | solution.py:296
  32.0 9.2 %collective-permute-start.14 = (f32[8,48,384]{2,1,0:T(8,128)S(1)}, f32[8,48,384]{2,1,0:T(8,128)S(1)}, u32[]{:S(2)}, u32[]{:S(2)}) collective-permute-start(f32[8,48,384]{2,1,0:T(8,128)S(1)} %all-to-all-done), channel_id=1, source_target_pairs={{0,96},{1,97},{2,98},{3,99},{4,100},{5,101},{6,102},{7,103},{8,104... | collective-permute-start | bytes 1769480 | tf_op jit(solution)/shard_map/ppermute | solution.py:33
  43.7 2.7 %collective-permute-start.4 = (f32[4,8,48,384]{3,2,1,0:T(8,128)S(1)}, f32[4,8,48,384]{3,2,1,0:T(8,128)S(1)}, u32[]{:S(2)}, u32[]{:S(2)}) collective-permute-start(f32[4,8,48,384]{3,2,1,0:T(8,128)S(1)} %pad_maximum_fusion.refs_0_), channel_id=1, source_target_pairs={{0,18},{1,13},{2,16},{3,15},{4,22},{5,1},{6,20},{7,3},{8,26},{9,5}... | collective-permute-start | bytes 7077896 | tf_op jit(solution)/shard_map/ppermute | solution.py:33
  46.5 2.5 %collective-permute-start.10 = (f32[4,48,384]{2,1,0:T(8,128)S(1)}, f32[4,48,384]{2,1,0:T(8,128)S(1)}, u32[]{:S(2)}, u32[]{:S(2)}) collective-permute-start(f32[4,48,384]{2,1,0:T(8,128)S(1)} %slice.50), channel_id=1, source_target_pairs={{0,96},{1,97},{2,98},{3,99},{4,100},{5,101},{6,102},{7,103},{8,104... | collective-permute-start | bytes 884744 | tf_op jit(solution)/shard_map/ppermute | solution.py:33
  49.0 4.3 %collective-permute-done.14 = f32[8,48,384]{2,1,0:T(8,128)S(1)} collective-permute-done((f32[8,48,384]{2,1,0:T(8,128)S(1)}, f32[8,48,384]{2,1,0:T(8,128)S(1)}, u32[]{:S(2)}, u32[]{:S(2)}) %collective-permute-start.14) | collective-permute-done | bytes 589856 | tf_op jit(solution)/shard_map/ppermute | solution.py:33
  54.1 3.0 %collective-permute-done.16 = f32[8,48,384]{2,1,0:T(8,128)S(1)} collective-permute-done((f32[8,48,384]{2,1,0:T(8,128)S(1)}, f32[8,48,384]{2,1,0:T(8,128)S(1)}, u32[]{:S(2)}, u32[]{:S(2)}) %collective-permute-start.16) | collective-permute-done | bytes 589856 | tf_op jit(solution)/shard_map/ppermute | solution.py:33
  57.1 2.3 %collective-permute-done.10 = f32[4,48,384]{2,1,0:T(8,128)S(1)} collective-permute-done((f32[4,48,384]{2,1,0:T(8,128)S(1)}, f32[4,48,384]{2,1,0:T(8,128)S(1)}, u32[]{:S(2)}, u32[]{:S(2)}) %collective-permute-start.10) | collective-permute-done | bytes 294944 | tf_op jit(solution)/shard_map/ppermute | solution.py:33
  60.2 1.7 collective-permute-done.12
  63.2 2.9 %collective-permute-start.13 = (f32[4,8,48,384]{3,2,1,0:T(8,128)S(1)}, f32[4,8,48,384]{3,2,1,0:T(8,128)}, u32[]{:S(2)}, u32[]{:S(2)}) collective-permute-start(f32[4,8,48,384]{3,2,1,0:T(8,128)S(1)} %pad_maximum_fusion.1.refs_0_), channel_id=1, source_target_pairs={{0,1},{1,0},{2,3},{3,2},{4,5},{5,4},{6,7},{7,6},{8,9},{9,8},{10,11... | collective-permute-start | bytes 7077896 | tf_op jit(solution)/shard_map/ppermute | solution.py:33
  66.2 3.6 %collective-permute-done.17 = f32[4,48,384]{2,1,0:T(8,128)S(1)} collective-permute-done((f32[4,48,384]{2,1,0:T(8,128)S(1)}, f32[4,48,384]{2,1,0:T(8,128)S(1)}, u32[]{:S(2)}, u32[]{:S(2)}) %collective-permute-start.17) | collective-permute-done | bytes 294944 | tf_op jit(solution)/shard_map/ppermute | solution.py:33
  73.9 3.0 %collective-permute-start.6 = (f32[2,8,48,384]{3,2,1,0:T(8,128)}, f32[2,8,48,384]{3,2,1,0:T(8,128)S(1)}, u32[]{:S(2)}, u32[]{:S(2)}) collective-permute-start(f32[2,8,48,384]{3,2,1,0:T(8,128)} %slice.48), channel_id=1, source_target_pairs={{0,18},{1,13},{2,16},{3,15},{4,22},{5,1},{6,20},{7,3},{8,26},{9,5}... | collective-permute-start | bytes 3538952 | tf_op jit(solution)/shard_map/ppermute | solution.py:33
  78.7 5.2 %shard_map.29 = (bf16[768,1536]{1,0:T(8,128)(2,1)S(1)}, bf16[768,1536]{1,0:T(8,128)(2,1)S(1)}, bf16[4,384,2304]{2,1,0:T(8,128)(2,1)S(1)}) custom-call(s32[4]{0:T(128)S(1)} %pad_add_fusion.place, f32[4,8,48,384]{3,2,1,0:T(8,128)S(1)} %pad_maximum_fusion.1.refs_0_, f32[4,8,48,384]{3,2,1,0:T(8,128)} %collective-permute-done.13.refs_1_, ...), custom_call_target="tpu_custom_call" | custom-call | flops 2717908992 | bytes 12582912 | tf_op jit(solution)/shard_map/pallas_call | solution.py:238
  84.0 2.8 %copy-done = bf16[4,384,2304]{2,1,0:T(8,128)(2,1)} copy-done((bf16[4,384,2304]{2,1,0:T(8,128)(2,1)}, bf16[4,384,2304]{2,1,0:T(8,128)(2,1)S(1)}, u32[]{:S(2)}) %copy-start) | copy-done | bytes 7077912
  90.3 4.6 %collective-permute-done.7.refs_4_ = f32[2,8,48,384]{3,2,1,0:T(8,128)} collective-permute-done((f32[2,8,48,384]{3,2,1,0:T(8,128)}, f32[2,8,48,384]{3,2,1,0:T(8,128)}, u32[]{:S(2)}, u32[]{:S(2)}) %collective-permute-start.7) | collective-permute-done | bytes 1179680 | tf_op jit(solution)/shard_map/ppermute | solution.py:33
  94.9 25.6 %shard_map.30 = (f32[2,8,48,384]{3,2,1,0:T(8,128)S(1)}, f32[2,8,48,384]{3,2,1,0:T(8,128)S(1)}, bf16[4,384,1536]{2,1,0:T(8,128)(2,1)}) custom-call(s32[4]{0:T(128)S(1)} %pad_add_fusion.place, f32[4,8,48,384]{3,2,1,0:T(8,128)} %copy-done.6, f32[4,8,48,384]{3,2,1,0:T(8,128)} %copy-done.10, f32[4,8,48,384]{3,2,1,0:T(8,128)} %copy-done.11, ...), custom_call_target="tpu_custom_call" | custom-call | flops 13589544960 | bytes 12582912 | tf_op jit(solution)/shard_map/pallas_call | solution.py:238
  122.1 2.3 %copy-done.2 = bf16[4,384,1536]{2,1,0:T(8,128)(2,1)S(1)} copy-done((bf16[4,384,1536]{2,1,0:T(8,128)(2,1)S(1)}, bf16[4,384,1536]{2,1,0:T(8,128)(2,1)}, u32[]{:S(2)}) %copy-start.2) | copy-done | bytes 4718616
  124.4 8.4 %shard_map.31 = (f32[2,8,48,384]{3,2,1,0:T(8,128)S(1)}, f32[2,8,48,384]{3,2,1,0:T(8,128)S(1)}, f32[2,8,48,384]{3,2,1,0:T(8,128)S(1)}, f32[2,8,48,384]{3,2,1,0:T(8,128)S(1)}) custom-call(s32[4]{0:T(128)S(1)} %pad_add_fusion.place, bf16[4,384,1536]{2,1,0:T(8,128)(2,1)S(1)} %copy-done.2, bf16[4,384,2304]{2,1,0:T(8,128)(2,1)S(1)} %copy-done.1), custom_call_target="tpu_custom_call" | custom-call | flops 5435817984 | bytes 12582912 | tf_op jit(solution)/shard_map/pallas_call | solution.py:238
  132.9 2.7 %collective-permute-start.20 = (f32[2,8,48,384]{3,2,1,0:T(8,128)S(1)}, f32[2,8,48,384]{3,2,1,0:T(8,128)S(1)}, u32[]{:S(2)}, u32[]{:S(2)}) collective-permute-start(f32[2,8,48,384]{3,2,1,0:T(8,128)S(1)} %get-tuple-element.20), channel_id=1, source_target_pairs={{0,18},{1,13},{2,16},{3,15},{4,22},{5,1},{6,20},{7,3},{8,26},{9,5}... | collective-permute-start | bytes 3538952 | tf_op jit(solution)/shard_map/ppermute | solution.py:33
  137.8 12.1 %collective-permute-done.19.b1 = f32[2,8,48,384]{3,2,1,0:T(8,128)S(1)} collective-permute-done((f32[2,8,48,384]{3,2,1,0:T(8,128)S(1)}, f32[2,8,48,384]{3,2,1,0:T(8,128)S(1)}, u32[]{:S(2)}, u32[]{:S(2)}) %collective-permute-start.19) | collective-permute-done | bytes 1179680 | tf_op jit(solution)/shard_map/ppermute | solution.py:33
  149.9 4.4 %shard_map.32 = f32[4,8,48,384]{3,2,1,0:T(8,128)S(1)} custom-call(s32[4]{0:T(128)S(1)} %pad_add_fusion.place, bf16[4,384,1536]{2,1,0:T(8,128)(2,1)S(1)} %copy-done.2, bf16[4,384,2304]{2,1,0:T(8,128)(2,1)S(1)} %copy-done.1, f32[2,8,48,384]{3,2,1,0:T(8,128)S(1)} %collective-permute-done.19.b1, f32[2,8,48,384]{3,2,1,0:T(8,128)S(1)} %collective-permute-done.20.d0), custom_call_target="tpu_custom_call" | custom-call | flops 2717908992 | bytes 12582912 | tf_op jit(solution)/shard_map/pallas_call | solution.py:238
  154.4 7.0 %collective-permute-done.24 = f32[2,8,48,384]{3,2,1,0:T(8,128)S(1)} collective-permute-done((f32[2,8,48,384]{3,2,1,0:T(8,128)S(1)}, f32[2,8,48,384]{3,2,1,0:T(8,128)S(1)}, u32[]{:S(2)}, u32[]{:S(2)}) %collective-permute-start.24) | collective-permute-done | bytes 1179680 | tf_op jit(solution)/shard_map/ppermute | solution.py:33
  163.0 2.5 %collective-permute-start.25 = (f32[8,48,384]{2,1,0:T(8,128)S(1)}, f32[8,48,384]{2,1,0:T(8,128)S(1)}, u32[]{:S(2)}, u32[]{:S(2)}) collective-permute-start(f32[8,48,384]{2,1,0:T(8,128)S(1)} %get-tuple-element.28), channel_id=1, source_target_pairs={{0,12},{1,19},{2,14},{3,17},{4,0},{5,23},{6,2},{7,21},{8,4},{9,27}... | collective-permute-start | bytes 1769480 | tf_op jit(solution)/shard_map/ppermute | solution.py:33
  165.5 1.9 collective-permute-start.26
  167.6 12.3 %collective-permute-done.25 = f32[8,48,384]{2,1,0:T(8,128)S(1)} collective-permute-done((f32[8,48,384]{2,1,0:T(8,128)S(1)}, f32[8,48,384]{2,1,0:T(8,128)S(1)}, u32[]{:S(2)}, u32[]{:S(2)}) %collective-permute-start.25) | collective-permute-done | bytes 589856 | tf_op jit(solution)/shard_map/ppermute | solution.py:33
  179.9 2.5 %collective-permute-done.27 = f32[8,48,384]{2,1,0:T(8,128)S(1)} collective-permute-done((f32[8,48,384]{2,1,0:T(8,128)S(1)}, f32[8,48,384]{2,1,0:T(8,128)S(1)}, u32[]{:S(2)}, u32[]{:S(2)}) %collective-permute-start.27) | collective-permute-done | bytes 589856 | tf_op jit(solution)/shard_map/ppermute | solution.py:33
  182.5 5.7 %collective-permute-start.28 = (f32[8,48,384]{2,1,0:T(8,128)S(1)}, f32[8,48,384]{2,1,0:T(8,128)S(1)}, u32[]{:S(2)}, u32[]{:S(2)}) collective-permute-start(f32[8,48,384]{2,1,0:T(8,128)S(1)} %fusion.3), channel_id=1, source_target_pairs={{0,0},{1,4},{2,2},{3,6},{4,1},{5,5},{6,3},{7,7},{8,8},{9,12},{10,1... | collective-permute-start | bytes 1769480 | tf_op jit(solution)/shard_map/ppermute | solution.py:33
  188.2 7.6 %collective-permute-done.28 = f32[8,48,384]{2,1,0:T(8,128)S(1)} collective-permute-done((f32[8,48,384]{2,1,0:T(8,128)S(1)}, f32[8,48,384]{2,1,0:T(8,128)S(1)}, u32[]{:S(2)}, u32[]{:S(2)}) %collective-permute-start.28) | collective-permute-done | bytes 589856 | tf_op jit(solution)/shard_map/ppermute | solution.py:33
  (76 shorter events, 28.0 us)
Async XLA Ops:
  0.0 12.7 %collective-permute-start = (f32[8,48,384]{2,1,0:T(8,128)}, f32[8,48,384]{2,1,0:T(8,128)S(1)}, u32[]{:S(2)}, u32[]{:S(2)}) collective-permute-start(f32[8,48,384]{2,1,0:T(8,128)} %l_ref.1), channel_id=1, source_target_pairs={{0,0},{1,4},{2,2},{3,6},{4,1},{5,5},{6,3},{7,7},{8,8},{9,12},{10,1... | collective-permute-start | bytes 1769480 | tf_op jit(solution)/shard_map/ppermute | solution.py:33
  4.9 19.8 %collective-permute-start.8 = (f32[8,48,384]{2,1,0:T(8,128)}, f32[8,48,384]{2,1,0:T(8,128)S(1)}, u32[]{:S(2)}, u32[]{:S(2)}) collective-permute-start(f32[8,48,384]{2,1,0:T(8,128)} %param.3), channel_id=1, source_target_pairs={{0,0},{1,1},{2,64},{3,65},{4,4},{5,5},{6,68},{7,69},{8,8},{9,9},{1... | collective-permute-start | bytes 1769480 | tf_op jit(solution)/shard_map/ppermute | solution.py:33
  12.7 19.3 %collective-permute-start.1 = (f32[8,48,384]{2,1,0:T(8,128)S(1)}, f32[8,48,384]{2,1,0:T(8,128)S(1)}, u32[]{:S(2)}, u32[]{:S(2)}) collective-permute-start(f32[8,48,384]{2,1,0:T(8,128)S(1)} %collective-permute-done.after), channel_id=1, source_target_pairs={{0,12},{1,19},{2,14},{3,17},{4,0},{5,23},{6,2},{7,21},{8,4},{9,27}... | collective-permute-start | bytes 1769480 | tf_op jit(solution)/shard_map/ppermute | solution.py:33
  17.9 14.1 %all-to-all-start = ((f32[8,48,384]{2,1,0:T(8,128)}), f32[8,48,384]{2,1,0:T(8,128)S(1)}, u32[]{:S(2)}, u32[]{:S(2)}) async-start(f32[8,48,384]{2,1,0:T(8,128)} %shard_map.28), calls=%async_computation | async-start | bytes 1179648 | tf_op jit(solution)/shard_map/all_to_all | solution.py:296
  22.4 18.8 %collective-permute-start.2 = (f32[8,48,384]{2,1,0:T(8,128)S(1)}, f32[8,48,384]{2,1,0:T(8,128)}, u32[]{:S(2)}, u32[]{:S(2)}) collective-permute-start(f32[8,48,384]{2,1,0:T(8,128)S(1)} %collective-permute-done.after), channel_id=1, source_target_pairs={{0,8},{1,3},{2,10},{3,1},{4,12},{5,7},{6,14},{7,5},{8,0},{9,11},{1... | collective-permute-start | bytes 1769480 | tf_op jit(solution)/shard_map/ppermute | solution.py:33
  23.9 18.4 %collective-permute-start.3 = (f32[8,48,384]{2,1,0:T(8,128)S(1)}, f32[8,48,384]{2,1,0:T(8,128)}, u32[]{:S(2)}, u32[]{:S(2)}) collective-permute-start(f32[8,48,384]{2,1,0:T(8,128)S(1)} %collective-permute-done.after), channel_id=1, source_target_pairs={{0,4},{1,17},{2,6},{3,19},{4,8},{5,21},{6,10},{7,23},{8,12},{9,25}... | collective-permute-start | bytes 1769480 | tf_op jit(solution)/shard_map/ppermute | solution.py:33
  24.7 21.6 %collective-permute-start.9 = (f32[8,48,384]{2,1,0:T(8,128)S(1)}, f32[8,48,384]{2,1,0:T(8,128)S(1)}, u32[]{:S(2)}, u32[]{:S(2)}) collective-permute-start(f32[8,48,384]{2,1,0:T(8,128)S(1)} %collective-permute-done.8), channel_id=1, source_target_pairs={{0,96},{1,97},{2,98},{3,99},{4,100},{5,101},{6,102},{7,103},{8,104... | collective-permute-start | bytes 1769480 | tf_op jit(solution)/shard_map/ppermute | solution.py:33
  27.5 19.0 %collective-permute-start.11 = (f32[8,48,384]{2,1,0:T(8,128)S(1)}, f32[8,48,384]{2,1,0:T(8,128)S(1)}, u32[]{:S(2)}, u32[]{:S(2)}) collective-permute-start(f32[8,48,384]{2,1,0:T(8,128)S(1)} %collective-permute-done.8), channel_id=1, source_target_pairs={{0,32},{1,33},{2,34},{3,35},{4,36},{5,37},{6,38},{7,39},{8,40},{9,... | collective-permute-start | bytes 1769480 | tf_op jit(solution)/shard_map/ppermute | solution.py:33
  32.0 21.3 %collective-permute-start.14 = (f32[8,48,384]{2,1,0:T(8,128)S(1)}, f32[8,48,384]{2,1,0:T(8,128)S(1)}, u32[]{:S(2)}, u32[]{:S(2)}) collective-permute-start(f32[8,48,384]{2,1,0:T(8,128)S(1)} %all-to-all-done), channel_id=1, source_target_pairs={{0,96},{1,97},{2,98},{3,99},{4,100},{5,101},{6,102},{7,103},{8,104... | collective-permute-start | bytes 1769480 | tf_op jit(solution)/shard_map/ppermute | solution.py:33
  41.2 15.9 %collective-permute-start.16 = (f32[8,48,384]{2,1,0:T(8,128)S(1)}, f32[8,48,384]{2,1,0:T(8,128)S(1)}, u32[]{:S(2)}, u32[]{:S(2)}) collective-permute-start(f32[8,48,384]{2,1,0:T(8,128)S(1)} %all-to-all-done), channel_id=1, source_target_pairs={{0,32},{1,33},{2,34},{3,35},{4,36},{5,37},{6,38},{7,39},{8,40},{9,... | collective-permute-start | bytes 1769480 | tf_op jit(solution)/shard_map/ppermute | solution.py:33
  43.7 19.5 %copy-start.6 = (f32[4,8,48,384]{3,2,1,0:T(8,128)}, f32[4,8,48,384]{3,2,1,0:T(8,128)S(1)}, u32[]{:S(2)}) copy-start(f32[4,8,48,384]{3,2,1,0:T(8,128)S(1)} %pad_maximum_fusion.refs_0_) | copy-start | bytes 7077892
  43.7 28.9 %collective-permute-start.4 = (f32[4,8,48,384]{3,2,1,0:T(8,128)S(1)}, f32[4,8,48,384]{3,2,1,0:T(8,128)S(1)}, u32[]{:S(2)}, u32[]{:S(2)}) collective-permute-start(f32[4,8,48,384]{3,2,1,0:T(8,128)S(1)} %pad_maximum_fusion.refs_0_), channel_id=1, source_target_pairs={{0,18},{1,13},{2,16},{3,15},{4,22},{5,1},{6,20},{7,3},{8,26},{9,5}... | collective-permute-start | bytes 7077896 | tf_op jit(solution)/shard_map/ppermute | solution.py:33
  46.4 30.5 %collective-permute-start.5 = (f32[4,8,48,384]{3,2,1,0:T(8,128)S(1)}, f32[4,8,48,384]{3,2,1,0:T(8,128)S(1)}, u32[]{:S(2)}, u32[]{:S(2)}) collective-permute-start(f32[4,8,48,384]{3,2,1,0:T(8,128)S(1)} %pad_maximum_fusion.refs_0_), channel_id=1, source_target_pairs={{0,16},{1,5},{2,18},{3,7},{4,20},{5,9},{6,22},{7,11},{8,24},{9,13}... | collective-permute-start | bytes 7077896 | tf_op jit(solution)/shard_map/ppermute | solution.py:33
  46.5 12.9 %collective-permute-start.10 = (f32[4,48,384]{2,1,0:T(8,128)S(1)}, f32[4,48,384]{2,1,0:T(8,128)S(1)}, u32[]{:S(2)}, u32[]{:S(2)}) collective-permute-start(f32[4,48,384]{2,1,0:T(8,128)S(1)} %slice.50), channel_id=1, source_target_pairs={{0,96},{1,97},{2,98},{3,99},{4,100},{5,101},{6,102},{7,103},{8,104... | collective-permute-start | bytes 884744 | tf_op jit(solution)/shard_map/ppermute | solution.py:33
  53.3 8.6 %collective-permute-start.12 = (f32[4,48,384]{2,1,0:T(8,128)S(1)}, f32[4,48,384]{2,1,0:T(8,128)S(1)}, u32[]{:S(2)}, u32[]{:S(2)}) collective-permute-start(f32[4,48,384]{2,1,0:T(8,128)S(1)} %slice.51), channel_id=1, source_target_pairs={{0,32},{1,33},{2,34},{3,35},{4,36},{5,37},{6,38},{7,39},{8,40},{9,... | collective-permute-start | bytes 884744 | tf_op jit(solution)/shard_map/ppermute | solution.py:33
  57.1 9.1 %collective-permute-start.15 = (f32[4,48,384]{2,1,0:T(8,128)S(1)}, f32[4,48,384]{2,1,0:T(8,128)S(1)}, u32[]{:S(2)}, u32[]{:S(2)}) collective-permute-start(f32[4,48,384]{2,1,0:T(8,128)S(1)} %slice.52), channel_id=1, source_target_pairs={{0,96},{1,97},{2,98},{3,99},{4,100},{5,101},{6,102},{7,103},{8,104... | collective-permute-start | bytes 884744 | tf_op jit(solution)/shard_map/ppermute | solution.py:33
  59.4 10.4 %collective-permute-start.17 = (f32[4,48,384]{2,1,0:T(8,128)S(1)}, f32[4,48,384]{2,1,0:T(8,128)S(1)}, u32[]{:S(2)}, u32[]{:S(2)}) collective-permute-start(f32[4,48,384]{2,1,0:T(8,128)S(1)} %slice.53), channel_id=1, source_target_pairs={{0,32},{1,33},{2,34},{3,35},{4,36},{5,37},{6,38},{7,39},{8,40},{9,... | collective-permute-start | bytes 884744 | tf_op jit(solution)/shard_map/ppermute | solution.py:33
  63.2 15.5 %collective-permute-start.13 = (f32[4,8,48,384]{3,2,1,0:T(8,128)S(1)}, f32[4,8,48,384]{3,2,1,0:T(8,128)}, u32[]{:S(2)}, u32[]{:S(2)}) collective-permute-start(f32[4,8,48,384]{3,2,1,0:T(8,128)S(1)} %pad_maximum_fusion.1.refs_0_), channel_id=1, source_target_pairs={{0,1},{1,0},{2,3},{3,2},{4,5},{5,4},{6,7},{7,6},{8,9},{9,8},{10,11... | collective-permute-start | bytes 7077896 | tf_op jit(solution)/shard_map/ppermute | solution.py:33
  71.4 7.3 %collective-permute-start.18 = (f32[4,8,48,384]{3,2,1,0:T(8,128)}, f32[4,8,48,384]{3,2,1,0:T(8,128)}, u32[]{:S(2)}, u32[]{:S(2)}) collective-permute-start(f32[4,8,48,384]{3,2,1,0:T(8,128)} %pad_maximum_fusion.2.refs_2_), channel_id=1, source_target_pairs={{0,1},{1,0},{2,3},{3,2},{4,5},{5,4},{6,7},{7,6},{8,9},{9,8},{10,11... | collective-permute-start | bytes 7077896 | tf_op jit(solution)/shard_map/ppermute | solution.py:33
  73.9 16.4 %collective-permute-start.6 = (f32[2,8,48,384]{3,2,1,0:T(8,128)}, f32[2,8,48,384]{3,2,1,0:T(8,128)S(1)}, u32[]{:S(2)}, u32[]{:S(2)}) collective-permute-start(f32[2,8,48,384]{3,2,1,0:T(8,128)} %slice.48), channel_id=1, source_target_pairs={{0,18},{1,13},{2,16},{3,15},{4,22},{5,1},{6,20},{7,3},{8,26},{9,5}... | collective-permute-start | bytes 3538952 | tf_op jit(solution)/shard_map/ppermute | solution.py:33
  78.1 16.9 %collective-permute-start.7 = (f32[2,8,48,384]{3,2,1,0:T(8,128)}, f32[2,8,48,384]{3,2,1,0:T(8,128)}, u32[]{:S(2)}, u32[]{:S(2)}) collective-permute-start(f32[2,8,48,384]{3,2,1,0:T(8,128)} %slice.49), channel_id=1, source_target_pairs={{0,16},{1,5},{2,18},{3,7},{4,20},{5,9},{6,22},{7,11},{8,24},{9,13}... | collective-permute-start | bytes 3538952 | tf_op jit(solution)/shard_map/ppermute | solution.py:33
  94.9 27.2 %copy-start.1 = (bf16[4,384,2304]{2,1,0:T(8,128)(2,1)S(1)}, bf16[4,384,2304]{2,1,0:T(8,128)(2,1)}, u32[]{:S(2)}) copy-start(bf16[4,384,2304]{2,1,0:T(8,128)(2,1)} %copy-done) | copy-start | bytes 21233668
  120.6 15.4 %collective-permute-start.23 = (f32[2,8,48,384]{3,2,1,0:T(8,128)S(1)}, f32[2,8,48,384]{3,2,1,0:T(8,128)S(1)}, u32[]{:S(2)}, u32[]{:S(2)}) collective-permute-start(f32[2,8,48,384]{3,2,1,0:T(8,128)S(1)} %get-tuple-element.24), channel_id=1, source_target_pairs={{0,18},{1,13},{2,16},{3,15},{4,22},{5,1},{6,20},{7,3},{8,26},{9,5}... | collective-permute-start | bytes 3538952 | tf_op jit(solution)/shard_map/ppermute | solution.py:33
  120.6 16.7 %collective-permute-start.21 = (f32[2,8,48,384]{3,2,1,0:T(8,128)S(1)}, f32[2,8,48,384]{3,2,1,0:T(8,128)S(1)}, u32[]{:S(2)}, u32[]{:S(2)}) collective-permute-start(f32[2,8,48,384]{3,2,1,0:T(8,128)S(1)} %get-tuple-element.22), channel_id=1, source_target_pairs={{0,16},{1,5},{2,18},{3,7},{4,20},{5,9},{6,22},{7,11},{8,24},{9,13}... | collective-permute-start | bytes 3538952 | tf_op jit(solution)/shard_map/ppermute | solution.py:33
  132.8 17.1 %collective-permute-start.19 = (f32[2,8,48,384]{3,2,1,0:T(8,128)S(1)}, f32[2,8,48,384]{3,2,1,0:T(8,128)S(1)}, u32[]{:S(2)}, u32[]{:S(2)}) collective-permute-start(f32[2,8,48,384]{3,2,1,0:T(8,128)S(1)} %get-tuple-element.19), channel_id=1, source_target_pairs={{0,16},{1,5},{2,18},{3,7},{4,20},{5,9},{6,22},{7,11},{8,24},{9,13}... | collective-permute-start | bytes 3538952 | tf_op jit(solution)/shard_map/ppermute | solution.py:33
  132.9 17.0 %collective-permute-start.20 = (f32[2,8,48,384]{3,2,1,0:T(8,128)S(1)}, f32[2,8,48,384]{3,2,1,0:T(8,128)S(1)}, u32[]{:S(2)}, u32[]{:S(2)}) collective-permute-start(f32[2,8,48,384]{3,2,1,0:T(8,128)S(1)} %get-tuple-element.20), channel_id=1, source_target_pairs={{0,18},{1,13},{2,16},{3,15},{4,22},{5,1},{6,20},{7,3},{8,26},{9,5}... | collective-permute-start | bytes 3538952 | tf_op jit(solution)/shard_map/ppermute | solution.py:33
  136.1 25.2 %collective-permute-start.24 = (f32[2,8,48,384]{3,2,1,0:T(8,128)S(1)}, f32[2,8,48,384]{3,2,1,0:T(8,128)S(1)}, u32[]{:S(2)}, u32[]{:S(2)}) collective-permute-start(f32[2,8,48,384]{3,2,1,0:T(8,128)S(1)} %add.35), channel_id=1, source_target_pairs={{0,18},{1,13},{2,16},{3,15},{4,22},{5,1},{6,20},{7,3},{8,26},{9,5}... | collective-permute-start | bytes 3538952 | tf_op jit(solution)/shard_map/ppermute | solution.py:33
  137.5 25.0 %collective-permute-start.22 = (f32[2,8,48,384]{3,2,1,0:T(8,128)S(1)}, f32[2,8,48,384]{3,2,1,0:T(8,128)S(1)}, u32[]{:S(2)}, u32[]{:S(2)}) collective-permute-start(f32[2,8,48,384]{3,2,1,0:T(8,128)S(1)} %add.31), channel_id=1, source_target_pairs={{0,16},{1,5},{2,18},{3,7},{4,20},{5,9},{6,22},{7,11},{8,24},{9,13}... | collective-permute-start | bytes 3538952 | tf_op jit(solution)/shard_map/ppermute | solution.py:33
  163.0 16.9 %collective-permute-start.25 = (f32[8,48,384]{2,1,0:T(8,128)S(1)}, f32[8,48,384]{2,1,0:T(8,128)S(1)}, u32[]{:S(2)}, u32[]{:S(2)}) collective-permute-start(f32[8,48,384]{2,1,0:T(8,128)S(1)} %get-tuple-element.28), channel_id=1, source_target_pairs={{0,12},{1,19},{2,14},{3,17},{4,0},{5,23},{6,2},{7,21},{8,4},{9,27}... | collective-permute-start | bytes 1769480 | tf_op jit(solution)/shard_map/ppermute | solution.py:33
  165.5 14.4 %collective-permute-start.26 = (f32[8,48,384]{2,1,0:T(8,128)S(1)}, f32[8,48,384]{2,1,0:T(8,128)S(1)}, u32[]{:S(2)}, u32[]{:S(2)}) collective-permute-start(f32[8,48,384]{2,1,0:T(8,128)S(1)} %get-tuple-element.27), channel_id=1, source_target_pairs={{0,8},{1,3},{2,10},{3,1},{4,12},{5,7},{6,14},{7,5},{8,0},{9,11},{1... | collective-permute-start | bytes 1769480 | tf_op jit(solution)/shard_map/ppermute | solution.py:33
  167.5 14.9 %collective-permute-start.27 = (f32[8,48,384]{2,1,0:T(8,128)S(1)}, f32[8,48,384]{2,1,0:T(8,128)S(1)}, u32[]{:S(2)}, u32[]{:S(2)}) collective-permute-start(f32[8,48,384]{2,1,0:T(8,128)S(1)} %slice_bitcast_fusion), channel_id=1, source_target_pairs={{0,4},{1,17},{2,6},{3,19},{4,8},{5,21},{6,10},{7,23},{8,12},{9,25}... | collective-permute-start | bytes 1769480 | tf_op jit(solution)/shard_map/ppermute | solution.py:33
  182.5 13.3 %collective-permute-start.28 = (f32[8,48,384]{2,1,0:T(8,128)S(1)}, f32[8,48,384]{2,1,0:T(8,128)S(1)}, u32[]{:S(2)}, u32[]{:S(2)}) collective-permute-start(f32[8,48,384]{2,1,0:T(8,128)S(1)} %fusion.3), channel_id=1, source_target_pairs={{0,0},{1,4},{2,2},{3,6},{4,1},{5,5},{6,3},{7,7},{8,8},{9,12},{10,1... | collective-permute-start | bytes 1769480 | tf_op jit(solution)/shard_map/ppermute | solution.py:33
  (10 other events, 66.4 us)

commit v6 on v5

--- a/solution.py
+++ b/solution.py
@@ -156,14 +156,12 @@
 
 
 def second_kernel(place, *refs):
-    rows, (t_hi_in, t_lo_in, c_in), outs = refs[:5], refs[5:8], refs[8:11]
-    l_rows, t_hi, t_lo, half, a_wide, c_wide, blocks, t_sem, row_sem, c_sem, out_sem = refs[11:]
-    t_copies = [pltpu.make_async_copy(t_hi_in, t_hi, t_sem), pltpu.make_async_copy(t_lo_in, t_lo, t_sem)]
+    (t_hi, t_lo, c_wide), rows, outs = refs[:3], refs[3:8], refs[8:11]
+    l_rows, half, a_wide, blocks, row_sem, out_sem = refs[11:]
     r_copies = [row_copies(place, rows, l_rows, pl.ds(4 * q, 4), row_sem.at[q]) for q in range(2)]
-    c_copies = [pltpu.make_async_copy(c_in, c_wide, c_sem)]
-    start(t_copies + r_copies[0])
-    wait(t_copies + r_copies[0])
-    start(r_copies[1] + c_copies)
+    start(r_copies[0])
+    wait(r_copies[0])
+    start(r_copies[1])
     for q in range(2):
         if q == 1:
             wait(r_copies[1])
@@ -182,7 +180,6 @@
             for b in range(4):
                 a_wide[b, i * 48 : i * 48 + 48, k * 768 : k * 768 + 768] = part[b * 48 : b * 48 + 48, :]
 
-    wait(c_copies)
     copies = [pltpu.make_async_copy(blocks.at[pl.ds(2 * k, 2)], outs[k], out_sem) for k in range(2)]
     copies.append(pltpu.make_async_copy(a_wide.at[:, :, pl.ds(0, 1536)], outs[2], out_sem))
     start(copies[2:])
@@ -234,11 +231,11 @@
 HALF_AMPS = jax.ShapeDtypeStruct(AMPS, BF16)
 
 
-def call(body, out_shape, out_spec, scratch, megabytes, units, place, *args, in_hbm=0):
+def call(body, out_shape, out_spec, scratch, megabytes, units, place, *args, in_hbm=0, in_vmem=0):
     return pl.pallas_call(
         body,
         out_shape=out_shape,
-        in_specs=[ON_SMEM] + [ON_HBM] * in_hbm + [ANYWHERE] * (len(args) - in_hbm),
+        in_specs=[ON_SMEM] + [ON_VMEM] * in_vmem + [ON_HBM] * in_hbm + [ANYWHERE] * (len(args) - in_hbm - in_vmem),
         out_specs=[out_spec] * len(out_shape),
         scratch_shapes=scratch,
         compiler_params=pltpu.CompilerParams(vmem_limit_bytes=megabytes << 20),
@@ -253,10 +250,9 @@
 
 
 def second(place, rows, parts):
-    scratch = [pltpu.VMEM((8, 192, 1536), F32)] + [pltpu.VMEM(AMPS, BF16)] * 2 + [pltpu.VMEM((8, 768, 192), F32)]
-    scratch += [pltpu.VMEM(WIDE.shape, BF16)] * 2 + [pltpu.VMEM(QUAD.shape, F32)]
-    scratch += [DMA, DMA((2,)), DMA, DMA]
-    return call(second_kernel, [PAIR] * 2 + [BOTH], ON_HBM, scratch, 48, 5, place, *rows, *parts)
+    scratch = [pltpu.VMEM((8, 192, 1536), F32), pltpu.VMEM((8, 768, 192), F32)]
+    scratch += [pltpu.VMEM(WIDE.shape, BF16), pltpu.VMEM(QUAD.shape, F32), DMA((2,)), DMA]
+    return call(second_kernel, [PAIR] * 2 + [BOTH], ON_HBM, scratch, 40, 5, place, *parts, *rows, in_vmem=3)
 
 
 def third(place, parts):

time: 197 us -> 206 us (1.046)
  local copies, waits for them, and re-layouts: 13.2 us -> 20.7 us
  waiting for transfers between devices: 74.7 us -> 68.3 us
  Pallas kernels: 45 us -> 47.8 us
  starting transfers between devices: 58.2 us -> 60.7 us
    ppermute x29, waiting for transfers between devices: 70.3 us -> 63.7 us  [permute(): return lax.ppermute(value, AXES, pairs)]
    unnamed x25 -> x29, local copies, waits for them, and re-layouts: 10.6 us -> 16.2 us
    pallas_call x4, Pallas kernels: 43.6 us -> 46.5 us  [call(): pl.pallas_call(body, out_shape=out_shape, in_specs=[ON_SMEM] + [ON_VMEM]...]
    ppermute x29, starting transfers between devices: 53.6 us -> 56.1 us  [permute(): return lax.ppermute(value, AXES, pairs)]
  transfers between devices with their start and end apart: 30 -> 30, of which waited for: 17 -> 16; matrix products, arithmetic and copies ran while one was open for 4% -> 5% of each run, Pallas kernels for 10% -> 10%
where the time goes in v6:
time: 206 us; the launch traced here: 205 us
  waiting for transfers between devices  68.3 us (33%)
  starting transfers between devices  60.7 us (29%)
  Pallas kernels  47.8 us (23%)
  local copies, waits for them, and re-layouts  20.7 us (10%)
  other arithmetic  7.23 us (4%)
    ppermute x29, waiting for transfers between devices, permute(): return lax.ppermute(value, AXES, pairs)  63.7 us
    ppermute x29, starting transfers between devices, permute(): return lax.ppermute(value, AXES, pairs)  56.1 us
    pallas_call x4, Pallas kernels, call(): pl.pallas_call(body, out_shape=out_shape, in_specs=[ON_SMEM] + [ON_VMEM]...  46.5 us
    unnamed x29, local copies, waits for them, and re-layouts  16.2 us
    another operation x4, other arithmetic, round_y(): ring = jnp.stack([own, p, far_one, m])  4.69 us
    all_to_all x1, waiting for transfers between devices, body(): lax.all_to_all(shuffle(cholesky, mine), ('xl', 'z'), 0, 0, tiled=True)  4.59 us
    all_to_all x1, starting transfers between devices, body(): lax.all_to_all(shuffle(cholesky, mine), ('xl', 'z'), 0, 0, tiled=True)  4.58 us
  transfers between devices with their start and end apart: 30, of which 16 were waited for; matrix products, arithmetic and copies ran while one was open for 5% of the time, Pallas kernels for 10%

profile of v6, /device:TPU:1, one launch (start us, length us, event | category | flops | bytes accessed | tf_op | source)
XLA Modules:
  0.0 204.9 jit_solution(2194850053088497186)
XLA Ops:
  0.0 4.9 %collective-permute-start.6 = (f32[8,48,384]{2,1,0:T(8,128)}, f32[8,48,384]{2,1,0:T(8,128)S(1)}, u32[]{:S(2)}, u32[]{:S(2)}) collective-permute-start(f32[8,48,384]{2,1,0:T(8,128)} %l_ref.1), channel_id=1, source_target_pairs={{0,0},{1,4},{2,2},{3,6},{4,1},{5,5},{6,3},{7,7},{8,8},{9,12},{10,1... | collective-permute-start | bytes 1769480 | tf_op jit(solution)/shard_map/ppermute | solution.py:33
  4.9 5.9 %collective-permute-start = (f32[8,48,384]{2,1,0:T(8,128)}, f32[8,48,384]{2,1,0:T(8,128)}, u32[]{:S(2)}, u32[]{:S(2)}) collective-permute-start(f32[8,48,384]{2,1,0:T(8,128)} %param.3), channel_id=1, source_target_pairs={{0,0},{1,1},{2,64},{3,65},{4,4},{5,5},{6,68},{7,69},{8,8},{9,9},{1... | collective-permute-start | bytes 1769480 | tf_op jit(solution)/shard_map/ppermute | solution.py:33
  12.7 2.9 %collective-permute-start.12 = (f32[8,48,384]{2,1,0:T(8,128)S(1)}, f32[8,48,384]{2,1,0:T(8,128)S(1)}, u32[]{:S(2)}, u32[]{:S(2)}) collective-permute-start(f32[8,48,384]{2,1,0:T(8,128)S(1)} %collective-permute-done.6.after), channel_id=1, source_target_pairs={{0,12},{1,19},{2,14},{3,17},{4,0},{5,23},{6,2},{7,21},{8,4},{9,27}... | collective-permute-start | bytes 1769480 | tf_op jit(solution)/shard_map/ppermute | solution.py:33
  18.0 4.6 %all-to-all-start = ((f32[8,48,384]{2,1,0:T(8,128)}), f32[8,48,384]{2,1,0:T(8,128)S(1)}, u32[]{:S(2)}, u32[]{:S(2)}) async-start(f32[8,48,384]{2,1,0:T(8,128)} %shard_map.28), calls=%async_computation | async-start | bytes 1179648 | tf_op jit(solution)/shard_map/all_to_all | solution.py:292
  24.9 2.7 %collective-permute-start.1 = (f32[8,48,384]{2,1,0:T(8,128)}, f32[8,48,384]{2,1,0:T(8,128)}, u32[]{:S(2)}, u32[]{:S(2)}) collective-permute-start(f32[8,48,384]{2,1,0:T(8,128)} %collective-permute-done), channel_id=1, source_target_pairs={{0,96},{1,97},{2,98},{3,99},{4,100},{5,101},{6,102},{7,103},{8,104... | collective-permute-start | bytes 1769480 | tf_op jit(solution)/shard_map/ppermute | solution.py:33
  27.6 4.6 %all-to-all-done = f32[8,48,384]{2,1,0:T(8,128)S(1)} async-done(((f32[8,48,384]{2,1,0:T(8,128)}), f32[8,48,384]{2,1,0:T(8,128)S(1)}, u32[]{:S(2)}, u32[]{:S(2)}) %all-to-all-start) | async-done | bytes 589856 | tf_op jit(solution)/shard_map/all_to_all | solution.py:292
  33.5 4.7 %collective-permute-done.13 = f32[8,48,384]{2,1,0:T(8,128)S(1)} collective-permute-done((f32[8,48,384]{2,1,0:T(8,128)S(1)}, f32[8,48,384]{2,1,0:T(8,128)S(1)}, u32[]{:S(2)}, u32[]{:S(2)}) %collective-permute-start.13) | collective-permute-done | bytes 589856 | tf_op jit(solution)/shard_map/ppermute | solution.py:33
  38.2 3.1 %collective-permute-start.7 = (f32[8,48,384]{2,1,0:T(8,128)S(1)}, f32[8,48,384]{2,1,0:T(8,128)S(1)}, u32[]{:S(2)}, u32[]{:S(2)}) collective-permute-start(f32[8,48,384]{2,1,0:T(8,128)S(1)} %all-to-all-done), channel_id=1, source_target_pairs={{0,96},{1,97},{2,98},{3,99},{4,100},{5,101},{6,102},{7,103},{8,104... | collective-permute-start | bytes 1769480 | tf_op jit(solution)/shard_map/ppermute | solution.py:33
  44.8 2.7 %collective-permute-start.15 = (f32[4,8,48,384]{3,2,1,0:T(8,128)S(1)}, f32[4,8,48,384]{3,2,1,0:T(8,128)S(1)}, u32[]{:S(2)}, u32[]{:S(2)}) collective-permute-start(f32[4,8,48,384]{3,2,1,0:T(8,128)S(1)} %pad_maximum_fusion.2.refs_3_), channel_id=1, source_target_pairs={{0,18},{1,13},{2,16},{3,15},{4,22},{5,1},{6,20},{7,3},{8,26},{9,5}... | collective-permute-start | bytes 7077896 | tf_op jit(solution)/shard_map/ppermute | solution.py:33
  48.5 2.4 %collective-permute-start.2 = (f32[4,48,384]{2,1,0:T(8,128)S(1)}, f32[4,48,384]{2,1,0:T(8,128)S(1)}, u32[]{:S(2)}, u32[]{:S(2)}) collective-permute-start(f32[4,48,384]{2,1,0:T(8,128)S(1)} %slice.48), channel_id=1, source_target_pairs={{0,96},{1,97},{2,98},{3,99},{4,100},{5,101},{6,102},{7,103},{8,104... | collective-permute-start | bytes 884744 | tf_op jit(solution)/shard_map/ppermute | solution.py:33
  51.9 3.3 %collective-permute-done.9 = f32[8,48,384]{2,1,0:T(8,128)S(1)} collective-permute-done((f32[8,48,384]{2,1,0:T(8,128)S(1)}, f32[8,48,384]{2,1,0:T(8,128)S(1)}, u32[]{:S(2)}, u32[]{:S(2)}) %collective-permute-start.9) | collective-permute-done | bytes 589856 | tf_op jit(solution)/shard_map/ppermute | solution.py:33
  55.7 3.4 %collective-permute-done.2 = f32[4,48,384]{2,1,0:T(8,128)S(1)} collective-permute-done((f32[4,48,384]{2,1,0:T(8,128)S(1)}, f32[4,48,384]{2,1,0:T(8,128)S(1)}, u32[]{:S(2)}, u32[]{:S(2)}) %collective-permute-start.2) | collective-permute-done | bytes 294944 | tf_op jit(solution)/shard_map/ppermute | solution.py:33
  59.1 3.4 %collective-permute-start.8 = (f32[4,48,384]{2,1,0:T(8,128)S(1)}, f32[4,48,384]{2,1,0:T(8,128)S(1)}, u32[]{:S(2)}, u32[]{:S(2)}) collective-permute-start(f32[4,48,384]{2,1,0:T(8,128)S(1)} %slice.50), channel_id=1, source_target_pairs={{0,96},{1,97},{2,98},{3,99},{4,100},{5,101},{6,102},{7,103},{8,104... | collective-permute-start | bytes 884744 | tf_op jit(solution)/shard_map/ppermute | solution.py:33
  62.7 3.0 %pad_maximum_fusion.refs_0_ = f32[4,8,48,384]{3,2,1,0:T(8,128)} fusion(f32[1,8,48,384]{3,2,1,0:T(8,128)} %bitcast.7, f32[1,8,48,384]{3,2,1,0:T(8,128)S(1)} %maximum_bitcast_fusion, f32[1,8,48,384]{3,2,1,0:T(8,128)} %bitcast.5, f32[1,8,48,384]{3,2,1,0:T(8,128)} %bitcast.4), kind=kLoop, calls=%fused_computation | loop fusion | flops 1769472 | bytes 4718592 | tf_op jit(solution)/shard_map/stack | solution.py:300
  65.7 5.9 %collective-permute-start.5 = (f32[4,8,48,384]{3,2,1,0:T(8,128)}, f32[4,8,48,384]{3,2,1,0:T(8,128)}, u32[]{:S(2)}, u32[]{:S(2)}) collective-permute-start(f32[4,8,48,384]{3,2,1,0:T(8,128)} %pad_maximum_fusion.refs_0_), channel_id=1, source_target_pairs={{0,1},{1,0},{2,3},{3,2},{4,5},{5,4},{6,7},{7,6},{8,9},{9,8},{10,11... | collective-permute-start | bytes 7077896 | tf_op jit(solution)/shard_map/ppermute | solution.py:33
  74.9 2.9 %collective-permute-start.17 = (f32[2,8,48,384]{3,2,1,0:T(8,128)}, f32[2,8,48,384]{3,2,1,0:T(8,128)}, u32[]{:S(2)}, u32[]{:S(2)}) collective-permute-start(f32[2,8,48,384]{3,2,1,0:T(8,128)} %slice.52), channel_id=1, source_target_pairs={{0,18},{1,13},{2,16},{3,15},{4,22},{5,1},{6,20},{7,3},{8,26},{9,5}... | collective-permute-start | bytes 3538952 | tf_op jit(solution)/shard_map/ppermute | solution.py:33
  79.7 5.8 %shard_map.29 = (bf16[768,1536]{1,0:T(8,128)(2,1)S(1)}, bf16[768,1536]{1,0:T(8,128)(2,1)S(1)}, bf16[4,384,2304]{2,1,0:T(8,128)(2,1)S(1)}) custom-call(s32[4]{0:T(128)S(1)} %pad_add_fusion.place, f32[4,8,48,384]{3,2,1,0:T(8,128)} %pad_maximum_fusion.refs_0_, f32[4,8,48,384]{3,2,1,0:T(8,128)} %collective-permute-done.5.refs_1_, ...), custom_call_target="tpu_custom_call" | custom-call | flops 2717908992 | bytes 12582912 | tf_op jit(solution)/shard_map/pallas_call | solution.py:235
  85.5 2.8 %copy-done = bf16[4,384,2304]{2,1,0:T(8,128)(2,1)} copy-done((bf16[4,384,2304]{2,1,0:T(8,128)(2,1)}, bf16[4,384,2304]{2,1,0:T(8,128)(2,1)S(1)}, u32[]{:S(2)}) %copy-start) | copy-done | bytes 7077912
  91.3 4.6 %collective-permute-done.18.refs_7_ = f32[2,8,48,384]{3,2,1,0:T(8,128)} collective-permute-done((f32[2,8,48,384]{3,2,1,0:T(8,128)}, f32[2,8,48,384]{3,2,1,0:T(8,128)}, u32[]{:S(2)}, u32[]{:S(2)}) %collective-permute-start.18) | collective-permute-done | bytes 1179680 | tf_op jit(solution)/shard_map/ppermute | solution.py:33
  100.9 27.9 %shard_map.30 = (f32[2,8,48,384]{3,2,1,0:T(8,128)}, f32[2,8,48,384]{3,2,1,0:T(8,128)}, bf16[4,384,1536]{2,1,0:T(8,128)(2,1)}) custom-call(s32[4]{0:T(128)S(1)} %pad_add_fusion.place, bf16[768,1536]{1,0:T(8,128)(2,1)S(1)} %copy-done.7, bf16[768,1536]{1,0:T(8,128)(2,1)S(1)} %copy-done.9, bf16[4,384,2304]{2,1,0:T(8,128)(2,1)} %copy-done, ...), custom_call_target="tpu_custom_call" | custom-call | flops 13589544960 | bytes 12582912 | tf_op jit(solution)/shard_map/pallas_call | solution.py:235
  130.4 2.3 %copy-done.2 = bf16[4,384,1536]{2,1,0:T(8,128)(2,1)S(1)} copy-done((bf16[4,384,1536]{2,1,0:T(8,128)(2,1)S(1)}, bf16[4,384,1536]{2,1,0:T(8,128)(2,1)}, u32[]{:S(2)}) %copy-start.2) | copy-done | bytes 4718616
  132.7 8.4 %shard_map.31 = (f32[2,8,48,384]{3,2,1,0:T(8,128)S(1)}, f32[2,8,48,384]{3,2,1,0:T(8,128)S(1)}, f32[2,8,48,384]{3,2,1,0:T(8,128)S(1)}, f32[2,8,48,384]{3,2,1,0:T(8,128)S(1)}) custom-call(s32[4]{0:T(128)S(1)} %pad_add_fusion.place, bf16[4,384,1536]{2,1,0:T(8,128)(2,1)S(1)} %copy-done.2, bf16[4,384,2304]{2,1,0:T(8,128)(2,1)S(1)} %copy-done.1), custom_call_target="tpu_custom_call" | custom-call | flops 5435817984 | bytes 12582912 | tf_op jit(solution)/shard_map/pallas_call | solution.py:235
  141.2 2.7 %collective-permute-start.20 = (f32[2,8,48,384]{3,2,1,0:T(8,128)S(1)}, f32[2,8,48,384]{3,2,1,0:T(8,128)S(1)}, u32[]{:S(2)}, u32[]{:S(2)}) collective-permute-start(f32[2,8,48,384]{3,2,1,0:T(8,128)S(1)} %get-tuple-element.20), channel_id=1, source_target_pairs={{0,18},{1,13},{2,16},{3,15},{4,22},{5,1},{6,20},{7,3},{8,26},{9,5}... | collective-permute-start | bytes 3538952 | tf_op jit(solution)/shard_map/ppermute | solution.py:33
  144.6 1.9 collective-permute-start.24
  146.7 12.2 %collective-permute-done.19.b1 = f32[2,8,48,384]{3,2,1,0:T(8,128)S(1)} collective-permute-done((f32[2,8,48,384]{3,2,1,0:T(8,128)S(1)}, f32[2,8,48,384]{3,2,1,0:T(8,128)S(1)}, u32[]{:S(2)}, u32[]{:S(2)}) %collective-permute-start.19) | collective-permute-done | bytes 1179680 | tf_op jit(solution)/shard_map/ppermute | solution.py:33
  158.9 4.4 %shard_map.32 = f32[4,8,48,384]{3,2,1,0:T(8,128)S(1)} custom-call(s32[4]{0:T(128)S(1)} %pad_add_fusion.place, bf16[4,384,1536]{2,1,0:T(8,128)(2,1)S(1)} %copy-done.2, bf16[4,384,2304]{2,1,0:T(8,128)(2,1)S(1)} %copy-done.1, f32[2,8,48,384]{3,2,1,0:T(8,128)S(1)} %collective-permute-done.19.b1, f32[2,8,48,384]{3,2,1,0:T(8,128)S(1)} %collective-permute-done.20.d0), custom_call_target="tpu_custom_call" | custom-call | flops 2717908992 | bytes 12582912 | tf_op jit(solution)/shard_map/pallas_call | solution.py:235
  163.4 6.4 %collective-permute-done.24 = f32[2,8,48,384]{3,2,1,0:T(8,128)S(1)} collective-permute-done((f32[2,8,48,384]{3,2,1,0:T(8,128)S(1)}, f32[2,8,48,384]{3,2,1,0:T(8,128)S(1)}, u32[]{:S(2)}, u32[]{:S(2)}) %collective-permute-start.24) | collective-permute-done | bytes 1179680 | tf_op jit(solution)/shard_map/ppermute | solution.py:33
  172.1 3.9 %collective-permute-start.25 = (f32[8,48,384]{2,1,0:T(8,128)S(1)}, f32[8,48,384]{2,1,0:T(8,128)S(1)}, u32[]{:S(2)}, u32[]{:S(2)}) collective-permute-start(f32[8,48,384]{2,1,0:T(8,128)S(1)} %get-tuple-element.28), channel_id=1, source_target_pairs={{0,12},{1,19},{2,14},{3,17},{4,0},{5,23},{6,2},{7,21},{8,4},{9,27}... | collective-permute-start | bytes 1769480 | tf_op jit(solution)/shard_map/ppermute | solution.py:33
  176.8 12.4 %collective-permute-done.25 = f32[8,48,384]{2,1,0:T(8,128)S(1)} collective-permute-done((f32[8,48,384]{2,1,0:T(8,128)S(1)}, f32[8,48,384]{2,1,0:T(8,128)S(1)}, u32[]{:S(2)}, u32[]{:S(2)}) %collective-permute-start.25) | collective-permute-done | bytes 589856 | tf_op jit(solution)/shard_map/ppermute | solution.py:33
  189.1 3.6 %collective-permute-done.27 = f32[8,48,384]{2,1,0:T(8,128)S(1)} collective-permute-done((f32[8,48,384]{2,1,0:T(8,128)S(1)}, f32[8,48,384]{2,1,0:T(8,128)S(1)}, u32[]{:S(2)}, u32[]{:S(2)}) %collective-permute-start.27) | collective-permute-done | bytes 589856 | tf_op jit(solution)/shard_map/ppermute | solution.py:33
  192.8 3.8 %collective-permute-start.28 = (f32[8,48,384]{2,1,0:T(8,128)S(1)}, f32[8,48,384]{2,1,0:T(8,128)S(1)}, u32[]{:S(2)}, u32[]{:S(2)}) collective-permute-start(f32[8,48,384]{2,1,0:T(8,128)S(1)} %fusion.3), channel_id=1, source_target_pairs={{0,0},{1,4},{2,2},{3,6},{4,1},{5,5},{6,3},{7,7},{8,8},{9,12},{10,1... | collective-permute-start | bytes 1769480 | tf_op jit(solution)/shard_map/ppermute | solution.py:33
  196.6 7.6 %collective-permute-done.28 = f32[8,48,384]{2,1,0:T(8,128)S(1)} collective-permute-done((f32[8,48,384]{2,1,0:T(8,128)S(1)}, f32[8,48,384]{2,1,0:T(8,128)S(1)}, u32[]{:S(2)}, u32[]{:S(2)}) %collective-permute-start.28) | collective-permute-done | bytes 589856 | tf_op jit(solution)/shard_map/ppermute | solution.py:33
  (80 shorter events, 33.8 us)
Async XLA Ops:
  0.0 12.7 %collective-permute-start.6 = (f32[8,48,384]{2,1,0:T(8,128)}, f32[8,48,384]{2,1,0:T(8,128)S(1)}, u32[]{:S(2)}, u32[]{:S(2)}) collective-permute-start(f32[8,48,384]{2,1,0:T(8,128)} %l_ref.1), channel_id=1, source_target_pairs={{0,0},{1,4},{2,2},{3,6},{4,1},{5,5},{6,3},{7,7},{8,8},{9,12},{10,1... | collective-permute-start | bytes 1769480 | tf_op jit(solution)/shard_map/ppermute | solution.py:33
  4.9 19.9 %collective-permute-start = (f32[8,48,384]{2,1,0:T(8,128)}, f32[8,48,384]{2,1,0:T(8,128)}, u32[]{:S(2)}, u32[]{:S(2)}) collective-permute-start(f32[8,48,384]{2,1,0:T(8,128)} %param.3), channel_id=1, source_target_pairs={{0,0},{1,1},{2,64},{3,65},{4,4},{5,5},{6,68},{7,69},{8,8},{9,9},{1... | collective-permute-start | bytes 1769480 | tf_op jit(solution)/shard_map/ppermute | solution.py:33
  12.7 19.5 %collective-permute-start.12 = (f32[8,48,384]{2,1,0:T(8,128)S(1)}, f32[8,48,384]{2,1,0:T(8,128)S(1)}, u32[]{:S(2)}, u32[]{:S(2)}) collective-permute-start(f32[8,48,384]{2,1,0:T(8,128)S(1)} %collective-permute-done.6.after), channel_id=1, source_target_pairs={{0,12},{1,19},{2,14},{3,17},{4,0},{5,23},{6,2},{7,21},{8,4},{9,27}... | collective-permute-start | bytes 1769480 | tf_op jit(solution)/shard_map/ppermute | solution.py:33
  18.0 14.2 %all-to-all-start = ((f32[8,48,384]{2,1,0:T(8,128)}), f32[8,48,384]{2,1,0:T(8,128)S(1)}, u32[]{:S(2)}, u32[]{:S(2)}) async-start(f32[8,48,384]{2,1,0:T(8,128)} %shard_map.28), calls=%async_computation | async-start | bytes 1179648 | tf_op jit(solution)/shard_map/all_to_all | solution.py:292
  22.5 15.6 %collective-permute-start.13 = (f32[8,48,384]{2,1,0:T(8,128)S(1)}, f32[8,48,384]{2,1,0:T(8,128)S(1)}, u32[]{:S(2)}, u32[]{:S(2)}) collective-permute-start(f32[8,48,384]{2,1,0:T(8,128)S(1)} %collective-permute-done.6.after), channel_id=1, source_target_pairs={{0,8},{1,3},{2,10},{3,1},{4,12},{5,7},{6,14},{7,5},{8,0},{9,11},{1... | collective-permute-start | bytes 1769480 | tf_op jit(solution)/shard_map/ppermute | solution.py:33
  24.0 18.4 %collective-permute-start.14 = (f32[8,48,384]{2,1,0:T(8,128)S(1)}, f32[8,48,384]{2,1,0:T(8,128)S(1)}, u32[]{:S(2)}, u32[]{:S(2)}) collective-permute-start(f32[8,48,384]{2,1,0:T(8,128)S(1)} %collective-permute-done.6.after), channel_id=1, source_target_pairs={{0,4},{1,17},{2,6},{3,19},{4,8},{5,21},{6,10},{7,23},{8,12},{9,25}... | collective-permute-start | bytes 1769480 | tf_op jit(solution)/shard_map/ppermute | solution.py:33
  24.9 22.6 %collective-permute-start.1 = (f32[8,48,384]{2,1,0:T(8,128)}, f32[8,48,384]{2,1,0:T(8,128)}, u32[]{:S(2)}, u32[]{:S(2)}) collective-permute-start(f32[8,48,384]{2,1,0:T(8,128)} %collective-permute-done), channel_id=1, source_target_pairs={{0,96},{1,97},{2,98},{3,99},{4,100},{5,101},{6,102},{7,103},{8,104... | collective-permute-start | bytes 1769480 | tf_op jit(solution)/shard_map/ppermute | solution.py:33
  27.6 20.9 %collective-permute-start.3 = (f32[8,48,384]{2,1,0:T(8,128)}, f32[8,48,384]{2,1,0:T(8,128)}, u32[]{:S(2)}, u32[]{:S(2)}) collective-permute-start(f32[8,48,384]{2,1,0:T(8,128)} %collective-permute-done), channel_id=1, source_target_pairs={{0,32},{1,33},{2,34},{3,35},{4,36},{5,37},{6,38},{7,39},{8,40},{9,... | collective-permute-start | bytes 1769480 | tf_op jit(solution)/shard_map/ppermute | solution.py:33
  32.2 10.2 %copy-start.10 = (f32[8,48,384]{2,1,0:T(8,128)}, f32[8,48,384]{2,1,0:T(8,128)S(1)}, u32[]{:S(2)}) copy-start(f32[8,48,384]{2,1,0:T(8,128)S(1)} %collective-permute-done.12) | copy-start | bytes 1769476
  32.2 23.0 %collective-permute-start.9 = (f32[8,48,384]{2,1,0:T(8,128)S(1)}, f32[8,48,384]{2,1,0:T(8,128)S(1)}, u32[]{:S(2)}, u32[]{:S(2)}) collective-permute-start(f32[8,48,384]{2,1,0:T(8,128)S(1)} %all-to-all-done), channel_id=1, source_target_pairs={{0,32},{1,33},{2,34},{3,35},{4,36},{5,37},{6,38},{7,39},{8,40},{9,... | collective-permute-start | bytes 1769480 | tf_op jit(solution)/shard_map/ppermute | solution.py:33
  38.2 17.0 %collective-permute-start.7 = (f32[8,48,384]{2,1,0:T(8,128)S(1)}, f32[8,48,384]{2,1,0:T(8,128)S(1)}, u32[]{:S(2)}, u32[]{:S(2)}) collective-permute-start(f32[8,48,384]{2,1,0:T(8,128)S(1)} %all-to-all-done), channel_id=1, source_target_pairs={{0,96},{1,97},{2,98},{3,99},{4,100},{5,101},{6,102},{7,103},{8,104... | collective-permute-start | bytes 1769480 | tf_op jit(solution)/shard_map/ppermute | solution.py:33
  44.8 29.0 %collective-permute-start.15 = (f32[4,8,48,384]{3,2,1,0:T(8,128)S(1)}, f32[4,8,48,384]{3,2,1,0:T(8,128)S(1)}, u32[]{:S(2)}, u32[]{:S(2)}) collective-permute-start(f32[4,8,48,384]{3,2,1,0:T(8,128)S(1)} %pad_maximum_fusion.2.refs_3_), channel_id=1, source_target_pairs={{0,18},{1,13},{2,16},{3,15},{4,22},{5,1},{6,20},{7,3},{8,26},{9,5}... | collective-permute-start | bytes 7077896 | tf_op jit(solution)/shard_map/ppermute | solution.py:33
  47.5 30.4 %collective-permute-start.16 = (f32[4,8,48,384]{3,2,1,0:T(8,128)S(1)}, f32[4,8,48,384]{3,2,1,0:T(8,128)S(1)}, u32[]{:S(2)}, u32[]{:S(2)}) collective-permute-start(f32[4,8,48,384]{3,2,1,0:T(8,128)S(1)} %pad_maximum_fusion.2.refs_3_), channel_id=1, source_target_pairs={{0,16},{1,5},{2,18},{3,7},{4,20},{5,9},{6,22},{7,11},{8,24},{9,13}... | collective-permute-start | bytes 7077896 | tf_op jit(solution)/shard_map/ppermute | solution.py:33
  48.5 10.6 %collective-permute-start.2 = (f32[4,48,384]{2,1,0:T(8,128)S(1)}, f32[4,48,384]{2,1,0:T(8,128)S(1)}, u32[]{:S(2)}, u32[]{:S(2)}) collective-permute-start(f32[4,48,384]{2,1,0:T(8,128)S(1)} %slice.48), channel_id=1, source_target_pairs={{0,96},{1,97},{2,98},{3,99},{4,100},{5,101},{6,102},{7,103},{8,104... | collective-permute-start | bytes 884744 | tf_op jit(solution)/shard_map/ppermute | solution.py:33
  55.1 7.5 %collective-permute-start.4 = (f32[4,48,384]{2,1,0:T(8,128)S(1)}, f32[4,48,384]{2,1,0:T(8,128)S(1)}, u32[]{:S(2)}, u32[]{:S(2)}) collective-permute-start(f32[4,48,384]{2,1,0:T(8,128)S(1)} %slice.49), channel_id=1, source_target_pairs={{0,32},{1,33},{2,34},{3,35},{4,36},{5,37},{6,38},{7,39},{8,40},{9,... | collective-permute-start | bytes 884744 | tf_op jit(solution)/shard_map/ppermute | solution.py:33
  55.2 16.4 %collective-permute-start.10 = (f32[4,48,384]{2,1,0:T(8,128)S(1)}, f32[4,48,384]{2,1,0:T(8,128)S(1)}, u32[]{:S(2)}, u32[]{:S(2)}) collective-permute-start(f32[4,48,384]{2,1,0:T(8,128)S(1)} %slice.51), channel_id=1, source_target_pairs={{0,32},{1,33},{2,34},{3,35},{4,36},{5,37},{6,38},{7,39},{8,40},{9,... | collective-permute-start | bytes 884744 | tf_op jit(solution)/shard_map/ppermute | solution.py:33
  59.1 12.5 %collective-permute-start.8 = (f32[4,48,384]{2,1,0:T(8,128)S(1)}, f32[4,48,384]{2,1,0:T(8,128)S(1)}, u32[]{:S(2)}, u32[]{:S(2)}) collective-permute-start(f32[4,48,384]{2,1,0:T(8,128)S(1)} %slice.50), channel_id=1, source_target_pairs={{0,96},{1,97},{2,98},{3,99},{4,100},{5,101},{6,102},{7,103},{8,104... | collective-permute-start | bytes 884744 | tf_op jit(solution)/shard_map/ppermute | solution.py:33
  65.7 14.0 %collective-permute-start.5 = (f32[4,8,48,384]{3,2,1,0:T(8,128)}, f32[4,8,48,384]{3,2,1,0:T(8,128)}, u32[]{:S(2)}, u32[]{:S(2)}) collective-permute-start(f32[4,8,48,384]{3,2,1,0:T(8,128)} %pad_maximum_fusion.refs_0_), channel_id=1, source_target_pairs={{0,1},{1,0},{2,3},{3,2},{4,5},{5,4},{6,7},{7,6},{8,9},{9,8},{10,11... | collective-permute-start | bytes 7077896 | tf_op jit(solution)/shard_map/ppermute | solution.py:33
  73.2 6.5 %collective-permute-start.11 = (f32[4,8,48,384]{3,2,1,0:T(8,128)}, f32[4,8,48,384]{3,2,1,0:T(8,128)}, u32[]{:S(2)}, u32[]{:S(2)}) collective-permute-start(f32[4,8,48,384]{3,2,1,0:T(8,128)} %pad_maximum_fusion.1.refs_2_), channel_id=1, source_target_pairs={{0,1},{1,0},{2,3},{3,2},{4,5},{5,4},{6,7},{7,6},{8,9},{9,8},{10,11... | collective-permute-start | bytes 7077896 | tf_op jit(solution)/shard_map/ppermute | solution.py:33
  74.9 16.4 %collective-permute-start.17 = (f32[2,8,48,384]{3,2,1,0:T(8,128)}, f32[2,8,48,384]{3,2,1,0:T(8,128)}, u32[]{:S(2)}, u32[]{:S(2)}) collective-permute-start(f32[2,8,48,384]{3,2,1,0:T(8,128)} %slice.52), channel_id=1, source_target_pairs={{0,18},{1,13},{2,16},{3,15},{4,22},{5,1},{6,20},{7,3},{8,26},{9,5}... | collective-permute-start | bytes 3538952 | tf_op jit(solution)/shard_map/ppermute | solution.py:33
  79.0 16.9 %collective-permute-start.18 = (f32[2,8,48,384]{3,2,1,0:T(8,128)}, f32[2,8,48,384]{3,2,1,0:T(8,128)}, u32[]{:S(2)}, u32[]{:S(2)}) collective-permute-start(f32[2,8,48,384]{3,2,1,0:T(8,128)} %slice.53), channel_id=1, source_target_pairs={{0,16},{1,5},{2,18},{3,7},{4,20},{5,9},{6,22},{7,11},{8,24},{9,13}... | collective-permute-start | bytes 3538952 | tf_op jit(solution)/shard_map/ppermute | solution.py:33
  100.9 29.5 %copy-start.1 = (bf16[4,384,2304]{2,1,0:T(8,128)(2,1)S(1)}, bf16[4,384,2304]{2,1,0:T(8,128)(2,1)}, u32[]{:S(2)}) copy-start(bf16[4,384,2304]{2,1,0:T(8,128)(2,1)} %copy-done) | copy-start | bytes 21233668
  128.8 15.6 %collective-permute-start.23 = (f32[2,8,48,384]{3,2,1,0:T(8,128)}, f32[2,8,48,384]{3,2,1,0:T(8,128)S(1)}, u32[]{:S(2)}, u32[]{:S(2)}) collective-permute-start(f32[2,8,48,384]{3,2,1,0:T(8,128)} %get-tuple-element.24), channel_id=1, source_target_pairs={{0,18},{1,13},{2,16},{3,15},{4,22},{5,1},{6,20},{7,3},{8,26},{9,5}... | collective-permute-start | bytes 3538952 | tf_op jit(solution)/shard_map/ppermute | solution.py:33
  129.5 17.0 %collective-permute-start.21 = (f32[2,8,48,384]{3,2,1,0:T(8,128)}, f32[2,8,48,384]{3,2,1,0:T(8,128)S(1)}, u32[]{:S(2)}, u32[]{:S(2)}) collective-permute-start(f32[2,8,48,384]{3,2,1,0:T(8,128)} %get-tuple-element.22), channel_id=1, source_target_pairs={{0,16},{1,5},{2,18},{3,7},{4,20},{5,9},{6,22},{7,11},{8,24},{9,13}... | collective-permute-start | bytes 3538952 | tf_op jit(solution)/shard_map/ppermute | solution.py:33
  141.1 17.8 %collective-permute-start.19 = (f32[2,8,48,384]{3,2,1,0:T(8,128)S(1)}, f32[2,8,48,384]{3,2,1,0:T(8,128)S(1)}, u32[]{:S(2)}, u32[]{:S(2)}) collective-permute-start(f32[2,8,48,384]{3,2,1,0:T(8,128)S(1)} %get-tuple-element.19), channel_id=1, source_target_pairs={{0,16},{1,5},{2,18},{3,7},{4,20},{5,9},{6,22},{7,11},{8,24},{9,13}... | collective-permute-start | bytes 3538952 | tf_op jit(solution)/shard_map/ppermute | solution.py:33
  141.2 17.8 %collective-permute-start.20 = (f32[2,8,48,384]{3,2,1,0:T(8,128)S(1)}, f32[2,8,48,384]{3,2,1,0:T(8,128)S(1)}, u32[]{:S(2)}, u32[]{:S(2)}) collective-permute-start(f32[2,8,48,384]{3,2,1,0:T(8,128)S(1)} %get-tuple-element.20), channel_id=1, source_target_pairs={{0,18},{1,13},{2,16},{3,15},{4,22},{5,1},{6,20},{7,3},{8,26},{9,5}... | collective-permute-start | bytes 3538952 | tf_op jit(solution)/shard_map/ppermute | solution.py:33
  144.6 25.2 %collective-permute-start.24 = (f32[2,8,48,384]{3,2,1,0:T(8,128)S(1)}, f32[2,8,48,384]{3,2,1,0:T(8,128)S(1)}, u32[]{:S(2)}, u32[]{:S(2)}) collective-permute-start(f32[2,8,48,384]{3,2,1,0:T(8,128)S(1)} %add.35), channel_id=1, source_target_pairs={{0,18},{1,13},{2,16},{3,15},{4,22},{5,1},{6,20},{7,3},{8,26},{9,5}... | collective-permute-start | bytes 3538952 | tf_op jit(solution)/shard_map/ppermute | solution.py:33
  146.6 24.9 %collective-permute-start.22 = (f32[2,8,48,384]{3,2,1,0:T(8,128)S(1)}, f32[2,8,48,384]{3,2,1,0:T(8,128)S(1)}, u32[]{:S(2)}, u32[]{:S(2)}) collective-permute-start(f32[2,8,48,384]{3,2,1,0:T(8,128)S(1)} %add.31), channel_id=1, source_target_pairs={{0,16},{1,5},{2,18},{3,7},{4,20},{5,9},{6,22},{7,11},{8,24},{9,13}... | collective-permute-start | bytes 3538952 | tf_op jit(solution)/shard_map/ppermute | solution.py:33
  172.1 17.0 %collective-permute-start.25 = (f32[8,48,384]{2,1,0:T(8,128)S(1)}, f32[8,48,384]{2,1,0:T(8,128)S(1)}, u32[]{:S(2)}, u32[]{:S(2)}) collective-permute-start(f32[8,48,384]{2,1,0:T(8,128)S(1)} %get-tuple-element.28), channel_id=1, source_target_pairs={{0,12},{1,19},{2,14},{3,17},{4,0},{5,23},{6,2},{7,21},{8,4},{9,27}... | collective-permute-start | bytes 1769480 | tf_op jit(solution)/shard_map/ppermute | solution.py:33
  176.0 13.2 %collective-permute-start.26 = (f32[8,48,384]{2,1,0:T(8,128)S(1)}, f32[8,48,384]{2,1,0:T(8,128)S(1)}, u32[]{:S(2)}, u32[]{:S(2)}) collective-permute-start(f32[8,48,384]{2,1,0:T(8,128)S(1)} %get-tuple-element.27), channel_id=1, source_target_pairs={{0,8},{1,3},{2,10},{3,1},{4,12},{5,7},{6,14},{7,5},{8,0},{9,11},{1... | collective-permute-start | bytes 1769480 | tf_op jit(solution)/shard_map/ppermute | solution.py:33
  176.1 16.6 %collective-permute-start.27 = (f32[8,48,384]{2,1,0:T(8,128)S(1)}, f32[8,48,384]{2,1,0:T(8,128)S(1)}, u32[]{:S(2)}, u32[]{:S(2)}) collective-permute-start(f32[8,48,384]{2,1,0:T(8,128)S(1)} %slice_bitcast_fusion), channel_id=1, source_target_pairs={{0,4},{1,17},{2,6},{3,19},{4,8},{5,21},{6,10},{7,23},{8,12},{9,25}... | collective-permute-start | bytes 1769480 | tf_op jit(solution)/shard_map/ppermute | solution.py:33
  192.8 11.3 %collective-permute-start.28 = (f32[8,48,384]{2,1,0:T(8,128)S(1)}, f32[8,48,384]{2,1,0:T(8,128)S(1)}, u32[]{:S(2)}, u32[]{:S(2)}) collective-permute-start(f32[8,48,384]{2,1,0:T(8,128)S(1)} %fusion.3), channel_id=1, source_target_pairs={{0,0},{1,4},{2,2},{3,6},{4,1},{5,5},{6,3},{7,7},{8,8},{9,12},{10,1... | collective-permute-start | bytes 1769480 | tf_op jit(solution)/shard_map/ppermute | solution.py:33
  (12 other events, 26.1 us)
